TPU v7x, 32 devices: a whole 2x2x4 slice. The times are simulated.
32 devices in a mesh: dp: 4 (over z), group: 8 (over y, x, core).
Axes of the slice: x: 2, y: 2, z: 4, core: 2. Of those that a mesh axis runs over, the one named last changes fastest.
Arguments:
- queries: float32 [8, 512, 4096], P('group', 'dp'), may hold values from -0.6 to 0.6
- passages: float32 [8, 512, 4096], P('group', 'dp'), may hold values from -0.09375 to 0.09375
- hard_ids: int32 [8, 512, 3], P('group', 'dp'), may hold values from 0 to 4095, as said below
Outputs:
- query_grad: float32 [8, 512, 4096], P('group', 'dp')
- passage_grad: float32 [8, 512, 4096], P('group', 'dp')
- losses: float32 [8, 512], P('group', 'dp')
Inputs may be any that keep to these rules, and one draw needn't show every extreme that they name: `hard_ids`: passage g * 512 + i is held by the device that holds row i of sub-batch g. Of the 384 hard negatives of one device's queries, at most 12 are held by any one device, and some device holds exactly 12 of them; one device holds 12 of every device's hard negatives.
All inputs are finite; a program needn't handle non-finite values.
Results may differ from a plain program's by a relative error of at most 0.005.
Values may be sent and summed in bfloat16 or wider, within the bound.
No kernel may reach another device: no remote copies, remote signals or barrier semaphores. Data moves between devices by JAX's collectives and lax.ppermute only.
A program may use at most 128 MiB of HBM per device.

v0:
```python
import jax
import jax.numpy as jnp
from jax import lax
from jax.sharding import PartitionSpec as P

HARD = 3


inverse_temp = 50.0


def per_device(queries, passages, hard_ids):
    query_wide = queries[0]
    row_count, features = query_wide.shape
    query_low = query_wide.astype(jnp.bfloat16)
    passage_low = passages[0].astype(jnp.bfloat16)
    wanted_ids = hard_ids[0]
    dp_count = lax.axis_size("dp")
    group_count = lax.axis_size("group")
    devices = dp_count * group_count
    batch_rows = row_count * dp_count
    offset = lax.axis_index("dp") * row_count
    entries = row_count * HARD
    capacity = (entries + devices - 1) // devices
    flat_ids = wanted_ids.reshape(entries)
    sub_index = flat_ids // batch_rows
    within = flat_ids % batch_rows
    owner = within // row_count * group_count + sub_index
    local_row = within % row_count
    member = (owner[:, None] == jnp.arange(devices)[None, :]).astype(jnp.int32)
    rank = jnp.sum(jnp.cumsum(member, axis=0) * member, axis=1) - 1
    slot = owner * capacity + rank
    request = (
        jnp.full((devices * capacity,), -1, jnp.int32)
        .at[slot]
        .set(local_row)
        .reshape(devices, capacity)
    )
    asked = lax.all_to_all(request, ("dp", "group"), split_axis=0, concat_axis=0, tiled=True)
    safe = jnp.clip(asked, 0)
    fetched = jnp.take(passage_low, safe.reshape(-1), axis=0).reshape(asked.shape + (features,))
    fetched = jnp.where((asked >= 0)[..., None], fetched, jnp.zeros((), jnp.bfloat16))
    served, asked = (fetched, asked)
    answered = lax.all_to_all(served, ("dp", "group"), split_axis=0, concat_axis=0, tiled=True)
    hard_rows = answered.reshape(devices * capacity, features)[slot].reshape(
        row_count, HARD, features
    )
    hard_scores = (
        jnp.einsum("rd,rkd->rk", query_low, hard_rows, preferred_element_type=jnp.float32)
        * inverse_temp
    )
    own_rows = offset + jnp.arange(row_count)
    passage_all = lax.all_gather(passage_low, "dp", axis=0, tiled=True)
    scores = (
        lax.dot_general(
            query_low, passage_all, (((1,), (1,)), ((), ())), preferred_element_type=jnp.float32
        )
        * inverse_temp
    )
    highest = jnp.maximum(jnp.max(scores, axis=1), jnp.max(hard_scores, axis=1))
    totals = jnp.sum(jnp.exp(scores - highest[:, None]), axis=1) + jnp.sum(
        jnp.exp(hard_scores - highest[:, None]), axis=1
    )
    normal = highest + jnp.log(totals)
    positive_mask = jnp.arange(batch_rows)[None, :] == own_rows[:, None]
    positive = jnp.sum(jnp.where(positive_mask, scores, 0.0), axis=1)
    coeff_all = (jnp.exp(scores - normal[:, None]) - positive_mask.astype(jnp.float32)).astype(
        jnp.bfloat16
    )
    cycle_query = jnp.dot(coeff_all, passage_all, preferred_element_type=jnp.float32)
    losses = normal - positive
    hard_coeff = jnp.exp(hard_scores - normal[:, None])
    hard_wide = hard_rows.astype(jnp.float32)
    query_grad = inverse_temp * (cycle_query + jnp.sum(hard_coeff[:, :, None] * hard_wide, axis=1))
    hard_grad = (
        inverse_temp * hard_coeff[:, :, None] * query_low.astype(jnp.float32)[:, None, :]
    ).astype(jnp.bfloat16)
    outgoing = (
        jnp.zeros((devices * capacity, features), jnp.bfloat16)
        .at[slot]
        .set(hard_grad.reshape(entries, features))
    )
    incoming = lax.all_to_all(
        outgoing.reshape(devices, capacity, features),
        ("dp", "group"),
        split_axis=0,
        concat_axis=0,
        tiled=True,
    )
    selector = (asked.reshape(-1)[:, None] == jnp.arange(row_count)[None, :]).astype(jnp.bfloat16)
    hard_sum = lax.dot_general(
        selector,
        incoming.reshape(devices * capacity, features),
        (((0,), (0,)), ((), ())),
        preferred_element_type=jnp.float32,
    )
    cycle_passage = lax.psum_scatter(
        inverse_temp
        * lax.dot_general(
            coeff_all, query_low, (((0,), (0,)), ((), ())), preferred_element_type=jnp.float32
        ),
        "dp",
        scatter_dimension=0,
        tiled=True,
    )
    passage_grad = cycle_passage + hard_sum
    return (query_grad[None], passage_grad[None], losses[None])


def solution(mesh):
    return jax.shard_map(
        per_device,
        mesh=mesh,
        in_specs=(P("group", "dp", None), P("group", "dp", None), P("group", "dp", None)),
        out_specs=(P("group", "dp", None), P("group", "dp", None), P("group", "dp")),
        check_vma=False,
    )
```

profile of v0, /device:TPU:0, one launch (start us, length us, event | category | flops | bytes accessed | tf_op | source)
XLA Modules:
  0.0 478.0 jit_solution(14876856073033895971)
XLA Ops:
  7.2 0.8 copy.15
  8.0 0.2 reshape_squeeze.7
  8.2 0.2 reshape_squeeze.9
  8.4 0.2 reshape_squeeze.8
  8.6 0.9 reduce-window.6
  9.5 0.2 slice_reduce_fusion
  9.8 0.1 fusion.18
  9.9 2.9 scatter_custom_fusion
  12.9 0.7 all_to_all.14
  13.6 7.3 %all-to-all-start = ((s32[32,1,12]{2,1,0:T(1,128)}), s32[32,1,12]{2,1,0:T(1,128)S(1)}, u32[]{:S(2)}, u32[]{:S(2)}) async-start(s32[32,1,12]{2,1,0:T(1,128)} %bitcast.3), calls=%async_computation | async-start | bytes 32768 | tf_op jit(solution)/shard_map/all_to_all | solution.py:39
  20.9 1.7 convert_bitcast_fusion
  22.6 5.4 %all-to-all-done = s32[32,1,12]{2,1,0:T(1,128)S(1)} async-done(((s32[32,1,12]{2,1,0:T(1,128)}), s32[32,1,12]{2,1,0:T(1,128)S(1)}, u32[]{:S(2)}, u32[]{:S(2)}) %all-to-all-start) | async-done | bytes 1568 | tf_op jit(solution)/shard_map/all_to_all | solution.py:39
  28.0 0.1 copy.21
  28.1 0.1 copy.23
  28.3 0.1 reshape.352
  28.5 4.0 gather_fusion
  32.5 5.5 %gather.10 = bf16[32,12,4096]{2,1,0:T(8,128)(2,1)} reshape(bf16[384,4096]{1,0:T(8,128)(2,1)} %gather_fusion) | data formatting | bytes 6291456 | tf_op jit(solution)/shard_map/jit(_take)/gather | solution.py:41
  38.0 3.9 select_select_fusion
  41.9 3.7 all-to-all-start.1
  45.7 1.1 convert_element_type.44
  46.8 0.2 reduce-scatter.2.cloned.1.call-start
  47.1 3.7 bitcast_convert_fusion
  50.7 155.9 %all-to-all-done.1 = bf16[32,12,4096]{2,1,0:T(8,128)(2,1)} async-done(((bf16[32,12,4096]{2,1,0:T(8,128)(2,1)}), bf16[32,12,4096]{2,1,0:T(8,128)(2,1)}, u32[]{:S(2)}, u32[]{:S(2)}) %all-to-all-start.1) | async-done | bytes 3145760 | tf_op jit(solution)/shard_map/all_to_all | solution.py:44
  206.6 4.0 reshape.346
  210.6 4.0 gather_fusion.1
  214.7 7.2 %reshape.347 = bf16[128,3,4096]{2,1,0:T(4,128)(2,1)} reshape(bf16[384,4096]{1,0:T(8,128)(2,1)} %gather_fusion.1) | data formatting | bytes 6291456 | tf_op jit(solution)/shard_map/reshape | solution.py:45
  221.8 7.7 %fusion.8 = f32[128,1,3]{2,1,0:T(1,128)S(1)} fusion(bf16[128,3,4096]{2,1,0:T(4,128)(2,1)} %reshape.347, bf16[128,4096,1]{1,0,2:T(8,128)(2,1)S(1)} %bitcast.55), kind=kOutput, calls=%fused_computation.18 | convolution fusion | flops 3145728 | bytes 4195840 | tf_op jit(solution)/shard_map/rd,rkd->rk/dot_general | solution.py:49
  229.5 0.1 multiply_reduce_fusion.1
  229.7 3.8 fusion.32
  233.5 0.2 exponential_reduce_fusion.1
  233.7 0.2 select_reduce_fusion
  233.9 0.5 subtract_bitcast_fusion
  234.4 4.6 convolution_multiply_fusion
  239.1 1.6 copy-done.2
  240.6 6.0 %mul.122 = f32[128,3,4096]{2,1,0:T(4,128)} broadcast(f32[128,4096]{1,0:T(8,128)S(1)} %copy-done.2), dimensions={0,2} | broadcast | bytes 8388608 | tf_op jit(solution)/shard_map/mul | solution.py:76
  246.6 9.6 %mul.123 = f32[384,4096]{1,0:T(8,128)} reshape(f32[128,3,4096]{2,1,0:T(4,128)} %mul.122) | data formatting | bytes 12582912 | tf_op jit(solution)/shard_map/mul | solution.py:76
  256.2 0.2 mul.120
  256.4 8.3 %scatter_custom_fusion.1 = bf16[384,4096]{1,0:T(8,128)(2,1)S(1)} fusion(s32[384]{0:T(512)S(1)} %fusion.29, f32[384,4096]{1,0:T(8,128)} %mul.123, f32[384]{0:T(512)S(1)} %mul.120, bf16[]{:T(256)} %constant.97.clone.1), kind=kCustom, calls=%fused_computation.16 | custom fusion | flops 3145728 | bytes 9439234 | tf_op jit(solution)/shard_map/scatter | solution.py:81
  264.7 2.8 reshape.348
  267.5 3.6 all-to-all-start.2
  271.1 0.5 broadcast.355
  271.6 0.7 reduce.7
  272.3 0.1 all_to_all.17
  272.4 9.1 %multiply_reduce_fusion = f32[128,4096]{1,0:T(8,128)S(1)} fusion(bf16[128,3,4096]{2,1,0:T(4,128)(2,1)} %reshape.347, f32[128,3]{1,0:T(8,128)S(1)} %get-tuple-element.8), kind=kLoop, calls=%fused_computation.4 | loop fusion | flops 4194304 | bytes 5244416 | tf_op jit(solution)/shard_map/reduce_sum | solution.py:74
  281.6 2.1 fusion.2
  283.7 179.7 %all-to-all-done.2 = bf16[32,12,4096]{2,1,0:T(8,128)(2,1)} async-done(((bf16[32,12,4096]{2,1,0:T(8,128)(2,1)}), bf16[32,12,4096]{2,1,0:T(8,128)(2,1)}, u32[]{:S(2)}, u32[]{:S(2)}) %all-to-all-start.2) | async-done | bytes 3145760 | tf_op jit(solution)/shard_map/all_to_all | solution.py:83
  463.4 4.0 reshape.349
  467.5 3.7 fusion
  (27 shorter events, 0.5 us)
Async XLA Ops:
  13.6 14.4 %all-to-all-start = ((s32[32,1,12]{2,1,0:T(1,128)}), s32[32,1,12]{2,1,0:T(1,128)S(1)}, u32[]{:S(2)}, u32[]{:S(2)}) async-start(s32[32,1,12]{2,1,0:T(1,128)} %bitcast.3), calls=%async_computation | async-start | bytes 32768 | tf_op jit(solution)/shard_map/all_to_all | solution.py:39
  41.9 3.8 copy-start.3
  41.9 164.7 %all-to-all-start.1 = ((bf16[32,12,4096]{2,1,0:T(8,128)(2,1)}), bf16[32,12,4096]{2,1,0:T(8,128)(2,1)}, u32[]{:S(2)}, u32[]{:S(2)}) async-start(bf16[32,12,4096]{2,1,0:T(8,128)(2,1)} %select_select_fusion), calls=%async_computation.1 | async-start | bytes 8388608 | tf_op jit(solution)/shard_map/all_to_all | solution.py:44
  45.6 184.1 %all-gather.3.cloned.1.call-start = ((), (), s32[]{:S(2)}) async-start(), calls=%async_computation.5 | async-start | bytes 5242880 | tf_op jit(solution)/shard_map/all_gather | solution.py:53
  46.8 420.7 %reduce-scatter.2.cloned.1.call-start = ((), (), s32[]{:S(2)}) async-start(), calls=%async_computation.4 | async-start | bytes 10485760 | tf_op jit(solution)/shard_map/reduce_scatter | solution.py:97
  214.6 7.2 %copy-start.1 = (bf16[1,128,4096]{2,1,0:T(8,128)(2,1)S(1)}, bf16[1,128,4096]{2,1,0:T(8,128)(2,1)}, u32[]{:S(2)}) copy-start(bf16[1,128,4096]{2,1,0:T(8,128)(2,1)} %get-tuple-element.10) | copy-start | bytes 3145732
  239.0 1.6 copy-start.2
  267.5 195.9 %all-to-all-start.2 = ((bf16[32,12,4096]{2,1,0:T(8,128)(2,1)}), bf16[32,12,4096]{2,1,0:T(8,128)(2,1)}, u32[]{:S(2)}, u32[]{:S(2)}) async-start(bf16[32,12,4096]{2,1,0:T(8,128)(2,1)} %reshape.348), calls=%async_computation.3 | async-start | bytes 8388608 | tf_op jit(solution)/shard_map/all_to_all | solution.py:83
  272.4 9.1 %copy-start = (bf16[1,512,4096]{2,1,0:T(8,128)(2,1)S(1)}, bf16[1,512,4096]{2,1,0:T(8,128)(2,1)}, u32[]{:S(2)}) copy-start(bf16[1,512,4096]{2,1,0:T(8,128)(2,1)} %all-gather.3.cloned.1.call-done) | copy-start | bytes 12582916
Sparse Core Ops, SparseCore 0:
  48.6 153.8 all-gather.2
  239.2 226.2 reduce-scatter.1
where the time goes:
time: 482 us; the launch traced here: 478 us
  waiting for transfers between devices  341 us (71%)
  local copies, waits for them, and re-layouts  55.1 us (11%)
  other arithmetic  30.8 us (6%)
  matrix products  22 us (5%)
  starting transfers between devices  14.8 us (3%)
  between operations  14.3 us (3%)
    all_to_all x1, waiting for transfers between devices, per_device(): lax.all_to_all(outgoing.reshape(devices, capacity, features), ('dp', 'gro...  180 us
    all_to_all x1, waiting for transfers between devices, per_device(): lax.all_to_all(served, ('dp', 'group'), split_axis=0, concat_axis=0, tile...  156 us
    mul x3, local copies, waits for them, and re-layouts, per_device(): inverse_temp * hard_coeff[:, :, None]  15.7 us
    reshape x2, local copies, waits for them, and re-layouts, per_device(): answered.reshape(devices * capacity, features)[slot]  11.1 us
  transfers between devices with their start and end apart: 5, of which 3 were waited for; matrix products, arithmetic and copies ran while one was open for 15% of the time, Pallas kernels for 0%

commit v1 on v0

v1 whole, which is shorter than its diff:
```python
import jax
import jax.numpy as jnp
from jax import lax
from jax.sharding import PartitionSpec as P

inverse_temp = 50.0
parts = 2


def first_hop(block, count):
    upward = [(i, i + 1) for i in range(count - 1)]
    downward = [(i + 1, i) for i in range(count - 1)]
    up = {1: lax.ppermute(block, "dp", upward)}
    down = {1: lax.ppermute(block, "dp", downward)}
    if count > 2:
        far = lax.ppermute(block, "dp", [(0, count - 1), (count - 1, 0)])
        up[count - 1] = down[count - 1] = far
    return up, down


def other_hops(block, up, down, count):
    upward = [(i, i + 1) for i in range(count - 1)]
    downward = [(i + 1, i) for i in range(count - 1)]
    for hop in range(2, count - 1):
        up[hop] = lax.ppermute(up[hop - 1], "dp", upward)
        down[hop] = lax.ppermute(down[hop - 1], "dp", downward)
    me = lax.axis_index("dp")
    blocks = [block]
    for k in range(1, count):
        blocks.append(jnp.where(me >= k, up[k], down[count - k]))
    return jnp.concatenate(blocks, axis=0)


def per_device(queries, passages, hard_ids):
    row_count, features = queries.shape[1:]
    hard = hard_ids.shape[2]
    dp_count = lax.axis_size("dp")
    group_count = lax.axis_size("group")
    devices = dp_count * group_count
    me = lax.axis_index("dp")
    my_group = lax.axis_index("group")
    batch_rows = row_count * dp_count
    entries = row_count * hard
    capacity = (entries + devices - 1) // devices
    slots = devices * capacity
    width = features // parts

    passage_low = passages[0].astype(jnp.bfloat16)
    query_low = queries[0].astype(jnp.bfloat16)

    stream = [x[:, i * width : (i + 1) * width] for x in (passage_low, query_low) for i in range(parts)]
    gathered = []
    before = None
    for block in stream:
        sent = block if before is None else lax.optimization_barrier((block,) + before)[0]
        up, down = first_hop(sent, dp_count)
        before = (up[1], down[1])
        gathered.append(other_hops(block, up, down, dp_count))
    passage_parts, query_parts = gathered[:parts], gathered[parts:]

    ids = hard_ids[0].T.reshape(entries)
    owner_group = ids // batch_rows
    owner_dp = ids % batch_rows // row_count
    owner = owner_group * dp_count + owner_dp
    order = jnp.arange(entries)
    earlier = (order[None, :] < order[:, None]) & (owner[None, :] == owner[:, None])
    rank = jnp.sum(earlier.astype(jnp.int32), axis=1)
    slot = owner * capacity + rank
    place = jnp.arange(slots)[:, None] == slot[None, :]
    query_row = jnp.sum(jnp.where(place, order[None, :] % row_count + 1, 0), axis=1) - 1
    passage_row = jnp.sum(jnp.where(place, ids[None, :] % row_count + 1, 0), axis=1) - 1

    def place_of(rows, dp_index):
        return jnp.where(rows >= 0, (me - dp_index) % dp_count * row_count + rows, -1)

    def one_hot(positions, count):
        return (positions[:, None] == jnp.arange(count)[None, :]).astype(jnp.bfloat16)

    asked = lax.all_to_all(
        passage_row.reshape(group_count, dp_count * capacity), "group", split_axis=0, concat_axis=0, tiled=True
    ).reshape(group_count, dp_count, capacity)
    dp_indices = jnp.arange(dp_count)
    fetch_place = place_of(asked, dp_indices[None, :, None]).reshape(slots)
    told = lax.all_to_all(
        query_row.reshape(group_count, dp_count, capacity).transpose(1, 0, 2).reshape(dp_count, group_count * capacity),
        "dp",
        split_axis=0,
        concat_axis=0,
        tiled=True,
    ).reshape(dp_count, group_count, capacity)
    push_place = place_of(told, dp_indices[:, None, None]).transpose(1, 0, 2).reshape(slots)

    def send_rows(positions, table):
        chosen = jnp.dot(one_hot(positions, batch_rows), table, preferred_element_type=jnp.float32).astype(
            jnp.bfloat16
        )
        moved = lax.all_to_all(
            chosen.reshape(group_count, dp_count * capacity, -1), "group", split_axis=0, concat_axis=0, tiled=True
        )
        return moved.reshape(slots, -1)

    hard_parts = [send_rows(fetch_place, table) for table in passage_parts]
    pushed_parts = [send_rows(push_place, table) for table in query_parts]

    def inner(left, rights):
        total = 0.0
        for i, right in enumerate(rights):
            total = total + lax.dot_general(
                left[:, i * width : (i + 1) * width],
                right,
                (((1,), (1,)), ((), ())),
                preferred_element_type=jnp.float32,
            )
        return total * inverse_temp

    diagonal = jnp.arange(row_count)[:, None] == jnp.arange(batch_rows)[None, :]
    scores = inner(query_low, passage_parts)
    owned = query_row[None, :] == jnp.arange(row_count)[:, None]
    hard_scores = jnp.where(owned, inner(query_low, hard_parts), -jnp.inf)
    highest = jnp.maximum(jnp.max(scores, axis=1), jnp.max(hard_scores, axis=1))
    totals = jnp.sum(jnp.exp(scores - highest[:, None]), axis=1) + jnp.sum(
        jnp.exp(hard_scores - highest[:, None]), axis=1
    )
    normal = highest + jnp.log(totals)
    losses = normal - jnp.sum(jnp.where(diagonal, scores, 0.0), axis=1)
    coeff = (jnp.exp(scores - normal[:, None]) - diagonal.astype(jnp.float32)).astype(jnp.bfloat16)
    hard_coeff = jnp.exp(hard_scores - normal[:, None])

    note = jnp.concatenate(
        [
            x.reshape(group_count, dp_count, capacity).transpose(1, 0, 2).reshape(devices, capacity)
            for x in (passage_row.astype(jnp.float32), jnp.sum(hard_coeff, axis=0))
        ]
        + [jnp.broadcast_to(normal[None, :], (devices, row_count))],
        axis=1,
    )
    notes = lax.all_to_all(note, ("dp", "group"), split_axis=0, concat_axis=0, tiled=True)
    notes = notes.reshape(dp_count, group_count, 2 * capacity + row_count)
    owned_row = notes[:, :, :capacity].transpose(1, 0, 2).reshape(slots)
    owned_coeff = notes[:, :, capacity : 2 * capacity].transpose(1, 0, 2).reshape(slots)
    normals = lax.dynamic_index_in_dim(notes[:, :, 2 * capacity :], my_group, axis=1, keepdims=False)
    normals = normals[(me - dp_indices) % dp_count].reshape(batch_rows)

    hard_low = hard_coeff.astype(jnp.bfloat16)
    query_grad = jnp.concatenate(
        [
            inverse_temp
            * (
                jnp.dot(coeff, table, preferred_element_type=jnp.float32)
                + jnp.dot(hard_low, rows, preferred_element_type=jnp.float32)
            )
            for table, rows in zip(passage_parts, hard_parts)
        ],
        axis=1,
    )

    back_scores = inner(passage_low, query_parts)
    back_coeff = (jnp.exp(back_scores - normals[None, :]) - diagonal.astype(jnp.float32)).astype(jnp.bfloat16)
    spread = jnp.where(
        jnp.arange(row_count).astype(jnp.float32)[:, None] == owned_row[None, :], owned_coeff[None, :], 0.0
    ).astype(jnp.bfloat16)
    passage_grad = jnp.concatenate(
        [
            inverse_temp
            * (
                jnp.dot(back_coeff, table, preferred_element_type=jnp.float32)
                + jnp.dot(spread, rows, preferred_element_type=jnp.float32)
            )
            for table, rows in zip(query_parts, pushed_parts)
        ],
        axis=1,
    )
    return (query_grad[None], passage_grad[None], losses[None])


def solution(mesh):
    return jax.shard_map(
        per_device,
        mesh=mesh,
        in_specs=(P("group", "dp", None), P("group", "dp", None), P("group", "dp", None)),
        out_specs=(P("group", "dp", None), P("group", "dp", None), P("group", "dp")),
        check_vma=False,
    )
```

time: 482 us -> 244 us (0.51)
  waiting for transfers between devices: 341 us -> 95.8 us
  starting transfers between devices: 14.8 us -> 90.3 us
  local copies, waits for them, and re-layouts: 55.1 us -> 10.3 us
  other arithmetic: 30.8 us -> 17.5 us
  between operations: 14.3 us -> 1.5 us
  matrix products: 22 us -> 27.2 us
    all_to_all x3 -> x7, waiting for transfers between devices: 341 us -> 56.7 us  [the longest x4 43.8 us: send_rows(): lax.all_to_all(chosen.reshape(group_count, dp_count * capacity, -1), 'gro...]
    ppermute x0 -> x20, starting transfers between devices: none -> 66 us  [the longest x4 25.2 us: other_hops(): up[hop] = lax.ppermute(up[hop - 1], 'dp', upward)]
    ppermute x0 -> x20, waiting for transfers between devices: none -> 39.2 us  [the longest x4 29 us: other_hops(): down[hop] = lax.ppermute(down[hop - 1], 'dp', downward)]
    reshape x4 -> x3, local copies, waits for them, and re-layouts: 17.9 us -> 0.28 us  [the longest x1 0.12 us: per_device(): x.reshape(group_count, dp_count, capacity).transpose(1, 0, 2)]
    mul x3 -> x0, local copies, waits for them, and re-layouts: 15.7 us -> none  [per_device(): inverse_temp * hard_coeff[:, :, None]]
    gather x3 -> x1, local copies, waits for them, and re-layouts: 13.6 us -> 0.56 us  [per_device(): normals = normals[(me - dp_indices) % dp_count].reshape(batch_rows)]
    all_to_all x3 -> x7, starting transfers between devices: 14.6 us -> 24.3 us  [the longest x4 14.6 us: send_rows(): lax.all_to_all(chosen.reshape(group_count, dp_count * capacity, -1), 'gro...]
    reduce_sum x3 -> x4, other arithmetic: 9.45 us -> 0.72 us  [the longest x1 0.25 us: per_device(): jnp.sum(jnp.where(place, order[None, :] % row_count + 1, 0), axis=1) - 1]
  transfers between devices with their start and end apart: 5 -> 27, of which waited for: 3 -> 12; matrix products, arithmetic and copies ran while one was open for 15% -> 17% of each run, Pallas kernels for 0% -> 0%
where the time goes in v1:
time: 244 us; the launch traced here: 243 us
  waiting for transfers between devices  95.8 us (39%)
  starting transfers between devices  90.3 us (37%)
  matrix products  27.2 us (11%)
  other arithmetic  17.5 us (7%)
  local copies, waits for them, and re-layouts  10.3 us (4%)
    all_to_all x4, waiting for transfers between devices, send_rows(): lax.all_to_all(chosen.reshape(group_count, dp_count * capacity, -1), 'gro...  43.8 us
    ppermute x4, waiting for transfers between devices, other_hops(): down[hop] = lax.ppermute(down[hop - 1], 'dp', downward)  29 us
    ppermute x4, starting transfers between devices, other_hops(): up[hop] = lax.ppermute(up[hop - 1], 'dp', upward)  25.2 us
    ppermute x4, starting transfers between devices, first_hop(): far = lax.ppermute(block, 'dp', [(0, count - 1), (count - 1, 0)])  16.8 us
    all_to_all x4, starting transfers between devices, send_rows(): lax.all_to_all(chosen.reshape(group_count, dp_count * capacity, -1), 'gro...  14.6 us
    ppermute x4, starting transfers between devices, first_hop(): up = {1: lax.ppermute(block, 'dp', upward)}  13.5 us
    dot_general x6, matrix products, inner(): lax.dot_general(left[:, i * width:(i + 1) * width], right, (((1,), (1,)),...  10.2 us
    dot_general x4, matrix products, send_rows(): jnp.dot(one_hot(positions, batch_rows), table, preferred_element_type=jnp...  9.83 us
  transfers between devices with their start and end apart: 27, of which 12 were waited for; matrix products, arithmetic and copies ran while one was open for 17% of the time, Pallas kernels for 0%

profile of v1, /device:TPU:0, one launch (start us, length us, event | category | flops | bytes accessed | tf_op | source)
XLA Modules:
  0.0 242.6 jit_solution(4557509215756291369)
XLA Ops:
  0.6 1.7 convert_bitcast_fusion.1
  4.2 4.9 %collective-permute-start = (bf16[128,2048]{1,0:T(8,128)(2,1)S(1)}, bf16[128,2048]{1,0:T(8,128)(2,1)S(1)}, u32[]{:S(2)}, u32[]{:S(2)}) collective-permute-start(bf16[128,2048]{1,0:T(8,128)(2,1)S(1)} %get-tuple-element.17), channel_id=1, source_target_pairs={{0,8},{8,16},{16,24},{1,9},{9,17},{17,25},{2,10},{10,18},{18,26},{... | collective-permute-start | bytes 1572872 | tf_op jit(solution)/shard_map/ppermute | solution.py:13
  10.5 6.6 %collective-permute-start.1 = (bf16[128,2048]{1,0:T(8,128)(2,1)S(1)}, bf16[128,2048]{1,0:T(8,128)(2,1)S(1)}, u32[]{:S(2)}, u32[]{:S(2)}) collective-permute-start(bf16[128,2048]{1,0:T(8,128)(2,1)S(1)} %get-tuple-element.17), channel_id=1, source_target_pairs={{0,24},{24,0},{1,25},{25,1},{2,26},{26,2},{3,27},{27,3},{4,28},{28... | collective-permute-start | bytes 1572872 | tf_op jit(solution)/shard_map/ppermute | solution.py:16
  18.3 3.7 %all-to-all-start = ((s32[8,1,48]{2,1,0:T(1,128)}), s32[8,1,48]{2,1,0:T(1,128)S(1)}, u32[]{:S(2)}, u32[]{:S(2)}) async-start(s32[8,1,48]{2,1,0:T(1,128)} %sub.117), calls=%async_computation | async-start | bytes 8192 | tf_op jit(solution)/shard_map/all_to_all | solution.py:79
  22.0 1.7 convert_bitcast_fusion
  26.6 3.2 %all-to-all-start.4 = ((s32[4,1,96]{2,1,0:T(1,128)}), s32[4,1,96]{2,1,0:T(1,128)S(1)}, u32[]{:S(2)}, u32[]{:S(2)}) async-start(s32[4,1,96]{2,1,0:T(1,128)} %bitcast.23), calls=%async_computation.4 | async-start | bytes 4096 | tf_op jit(solution)/shard_map/all_to_all | solution.py:84
  31.1 6.7 %all-to-all-done.4 = s32[4,1,96]{2,1,0:T(1,128)S(1)} async-done(((s32[4,1,96]{2,1,0:T(1,128)}), s32[4,1,96]{2,1,0:T(1,128)S(1)}, u32[]{:S(2)}, u32[]{:S(2)}) %all-to-all-start.4) | async-done | bytes 1568 | tf_op jit(solution)/shard_map/all_to_all | solution.py:84
  38.5 3.2 %collective-permute-start.5 = (bf16[128,2048]{1,0:T(8,128)(2,1)}, bf16[128,2048]{1,0:T(8,128)(2,1)}, u32[]{:S(2)}, u32[]{:S(2)}) collective-permute-start(bf16[128,2048]{1,0:T(8,128)(2,1)} %get-tuple-element.6), channel_id=1, source_target_pairs={{0,8},{8,16},{16,24},{1,9},{9,17},{17,25},{2,10},{10,18},{18,26},{... | collective-permute-start | bytes 1572872 | tf_op jit(solution)/shard_map/ppermute | solution.py:13
  43.1 5.4 %collective-permute-start.2 = (bf16[128,2048]{1,0:T(8,128)(2,1)S(1)}, bf16[128,2048]{1,0:T(8,128)(2,1)}, u32[]{:S(2)}, u32[]{:S(2)}) collective-permute-start(bf16[128,2048]{1,0:T(8,128)(2,1)S(1)} %collective-permute-done), channel_id=1, source_target_pairs={{0,8},{8,16},{16,24},{1,9},{9,17},{17,25},{2,10},{10,18},{18,26},{... | collective-permute-start | bytes 1572872 | tf_op jit(solution)/shard_map/ppermute | solution.py:25
  49.9 4.1 %collective-permute-start.6 = (bf16[128,2048]{1,0:T(8,128)(2,1)}, bf16[128,2048]{1,0:T(8,128)(2,1)}, u32[]{:S(2)}, u32[]{:S(2)}) collective-permute-start(bf16[128,2048]{1,0:T(8,128)(2,1)} %get-tuple-element.6), channel_id=1, source_target_pairs={{0,24},{24,0},{1,25},{25,1},{2,26},{26,2},{3,27},{27,3},{4,28},{28... | collective-permute-start | bytes 1572872 | tf_op jit(solution)/shard_map/ppermute | solution.py:16
  54.1 4.7 %collective-permute-done.8 = bf16[128,2048]{1,0:T(8,128)(2,1)} collective-permute-done((bf16[128,2048]{1,0:T(8,128)(2,1)}, bf16[128,2048]{1,0:T(8,128)(2,1)}, u32[]{:S(2)}, u32[]{:S(2)}) %collective-permute-start.8) | collective-permute-done | bytes 524320 | tf_op jit(solution)/shard_map/ppermute | solution.py:14
  58.8 2.4 collective-permute-start.10
  62.5 2.2 collective-permute-done.2
  64.8 13.1 %collective-permute-start.7 = (bf16[128,2048]{1,0:T(8,128)(2,1)}, bf16[128,2048]{1,0:T(8,128)(2,1)}, u32[]{:S(2)}, u32[]{:S(2)}) collective-permute-start(bf16[128,2048]{1,0:T(8,128)(2,1)} %collective-permute-done.5), channel_id=1, source_target_pairs={{0,8},{8,16},{16,24},{1,9},{9,17},{17,25},{2,10},{10,18},{18,26},{... | collective-permute-start | bytes 1572872 | tf_op jit(solution)/shard_map/ppermute | solution.py:25
  77.8 3.5 %collective-permute-done.4 = bf16[128,2048]{1,0:T(8,128)(2,1)} collective-permute-done((bf16[128,2048]{1,0:T(8,128)(2,1)S(1)}, bf16[128,2048]{1,0:T(8,128)(2,1)}, u32[]{:S(2)}, u32[]{:S(2)}) %collective-permute-start.4) | collective-permute-done | bytes 524320 | tf_op jit(solution)/shard_map/ppermute | solution.py:26
  83.7 2.2 convolution_convert_fusion.3
  85.9 3.7 %all-to-all-start.1 = ((bf16[8,48,2048]{2,1,0:T(8,128)(2,1)}), bf16[8,48,2048]{2,1,0:T(8,128)(2,1)S(1)}, u32[]{:S(2)}, u32[]{:S(2)}) async-start(bf16[8,48,2048]{2,1,0:T(8,128)(2,1)} %bitcast.105), calls=%async_computation.1 | async-start | bytes 3145728 | tf_op jit(solution)/shard_map/all_to_all | solution.py:97
  89.7 3.4 %collective-permute-start.11 = (bf16[128,2048]{1,0:T(8,128)(2,1)}, bf16[128,2048]{1,0:T(8,128)(2,1)S(1)}, u32[]{:S(2)}, u32[]{:S(2)}) collective-permute-start(bf16[128,2048]{1,0:T(8,128)(2,1)} %get-tuple-element.7), channel_id=1, source_target_pairs={{0,24},{24,0},{1,25},{25,1},{2,26},{26,2},{3,27},{27,3},{4,28},{28... | collective-permute-start | bytes 1572872 | tf_op jit(solution)/shard_map/ppermute | solution.py:16
  94.4 3.0 %collective-permute-start.15 = (bf16[128,2048]{1,0:T(8,128)(2,1)S(1)}, bf16[128,2048]{1,0:T(8,128)(2,1)}, u32[]{:S(2)}, u32[]{:S(2)}) collective-permute-start(bf16[128,2048]{1,0:T(8,128)(2,1)S(1)} %copy-done.30), channel_id=1, source_target_pairs={{0,8},{8,16},{16,24},{1,9},{9,17},{17,25},{2,10},{10,18},{18,26},{... | collective-permute-start | bytes 1572872 | tf_op jit(solution)/shard_map/ppermute | solution.py:13
  97.4 2.7 %collective-permute-start.16 = (bf16[128,2048]{1,0:T(8,128)(2,1)S(1)}, bf16[128,2048]{1,0:T(8,128)(2,1)S(1)}, u32[]{:S(2)}, u32[]{:S(2)}) collective-permute-start(bf16[128,2048]{1,0:T(8,128)(2,1)S(1)} %copy-done.30), channel_id=1, source_target_pairs={{0,24},{24,0},{1,25},{25,1},{2,26},{26,2},{3,27},{27,3},{4,28},{28... | collective-permute-start | bytes 1572872 | tf_op jit(solution)/shard_map/ppermute | solution.py:16
  101.4 21.9 %collective-permute-done.9 = bf16[128,2048]{1,0:T(8,128)(2,1)} collective-permute-done((bf16[128,2048]{1,0:T(8,128)(2,1)}, bf16[128,2048]{1,0:T(8,128)(2,1)}, u32[]{:S(2)}, u32[]{:S(2)}) %collective-permute-start.9) | collective-permute-done | bytes 524320 | tf_op jit(solution)/shard_map/ppermute | solution.py:26
  123.3 1.3 collective-permute-start.12
  126.5 1.4 collective-permute-start.14
  129.2 1.4 fusion.71
  130.6 2.2 convolution_convert_fusion.2
  132.8 5.5 %collective-permute-start.17 = (bf16[128,2048]{1,0:T(8,128)(2,1)}, bf16[128,2048]{1,0:T(8,128)(2,1)}, u32[]{:S(2)}, u32[]{:S(2)}) collective-permute-start(bf16[128,2048]{1,0:T(8,128)(2,1)} %collective-permute-done.15), channel_id=1, source_target_pairs={{0,8},{8,16},{16,24},{1,9},{9,17},{17,25},{2,10},{10,18},{18,26},{... | collective-permute-start | bytes 1572872 | tf_op jit(solution)/shard_map/ppermute | solution.py:25
  139.6 3.2 %collective-permute-done.12 = bf16[128,2048]{1,0:T(8,128)(2,1)S(1)} collective-permute-done((bf16[128,2048]{1,0:T(8,128)(2,1)}, bf16[128,2048]{1,0:T(8,128)(2,1)S(1)}, u32[]{:S(2)}, u32[]{:S(2)}) %collective-permute-start.12) | collective-permute-done | bytes 524320 | tf_op jit(solution)/shard_map/ppermute | solution.py:25
  142.9 3.6 %collective-permute-done.14 = bf16[128,2048]{1,0:T(8,128)(2,1)S(1)} collective-permute-done((bf16[128,2048]{1,0:T(8,128)(2,1)}, bf16[128,2048]{1,0:T(8,128)(2,1)S(1)}, u32[]{:S(2)}, u32[]{:S(2)}) %collective-permute-start.14) | collective-permute-done | bytes 524320 | tf_op jit(solution)/shard_map/ppermute | solution.py:26
  146.6 2.3 broadcast_select_fusion.8
  148.9 3.2 %convolution_convert_fusion.1 = bf16[384,2048]{1,0:T(8,128)(2,1)} fusion(s32[384]{0:T(512)S(1)} %eq.154, bf16[128,2048]{1,0:T(8,128)(2,1)S(1)} %get-tuple-element.20, bf16[128,2048]{1,0:T(8,128)(2,1)S(1)} %broadcast_select_fusion.5, bf16[128,2048]{1,0:T(8,128)(2,1)S(1)} %get-tuple-element.19, bf16[128,2048]{1,0:T(8,128)(2,1)} %get-tuple-element.7), kind=kOutput, calls=%fused_computation.2 | convolution fusion | flops 814678016 | bytes 3671552 | tf_op jit(solution)/shard_map/dot_general | solution.py:94
  152.2 3.7 %all-to-all-start.2 = ((bf16[8,48,2048]{2,1,0:T(8,128)(2,1)}), bf16[8,48,2048]{2,1,0:T(8,128)(2,1)S(1)}, u32[]{:S(2)}, u32[]{:S(2)}) async-start(bf16[8,48,2048]{2,1,0:T(8,128)(2,1)} %bitcast.106), calls=%async_computation.2 | async-start | bytes 3145728 | tf_op jit(solution)/shard_map/all_to_all | solution.py:97
  155.9 2.4 %fusion.66 = f32[384,128]{1,0:T(8,128)} fusion(bf16[384,2048]{1,0:T(8,128)(2,1)S(1)} %bitcast.97, bf16[128,4096]{1,0:T(8,128)(2,1)} %copy-done.2), kind=kOutput, calls=%fused_computation.149 | convolution fusion | flops 201326592 | bytes 2293760 | tf_op jit(solution)/shard_map/dot_general | solution.py:108
  159.5 1.4 fusion.60
  161.0 2.2 convolution_convert_fusion
  163.2 13.7 %all-to-all-done.2 = bf16[8,48,2048]{2,1,0:T(8,128)(2,1)S(1)} async-done(((bf16[8,48,2048]{2,1,0:T(8,128)(2,1)}), bf16[8,48,2048]{2,1,0:T(8,128)(2,1)S(1)}, u32[]{:S(2)}, u32[]{:S(2)}) %all-to-all-start.2) | async-done | bytes 1572896 | tf_op jit(solution)/shard_map/all_to_all | solution.py:97
  176.9 1.7 fusion.72
  180.4 2.7 %all-to-all-start.3 = ((f32[32,1,152]{2,1,0:T(1,128)}), f32[32,1,152]{2,1,0:T(1,128)S(1)}, u32[]{:S(2)}, u32[]{:S(2)}) async-start(f32[32,1,152]{2,1,0:T(1,128)} %all_to_all.31), calls=%async_computation.3 | async-start | bytes 65536 | tf_op jit(solution)/shard_map/all_to_all | solution.py:137
  183.2 1.5 fusion.36
  184.6 5.6 %all-to-all-done.3 = f32[32,1,152]{2,1,0:T(1,128)S(1)} async-done(((f32[32,1,152]{2,1,0:T(1,128)}), f32[32,1,152]{2,1,0:T(1,128)S(1)}, u32[]{:S(2)}, u32[]{:S(2)}) %all-to-all-start.3) | async-done | bytes 19488 | tf_op jit(solution)/shard_map/all_to_all | solution.py:137
  190.2 3.6 %all-to-all-start.5 = ((bf16[8,48,2048]{2,1,0:T(8,128)(2,1)}), bf16[8,48,2048]{2,1,0:T(8,128)(2,1)S(1)}, u32[]{:S(2)}, u32[]{:S(2)}) async-start(bf16[8,48,2048]{2,1,0:T(8,128)(2,1)} %bitcast.104), calls=%async_computation.5 | async-start | bytes 3145728 | tf_op jit(solution)/shard_map/all_to_all | solution.py:97
  195.5 1.8 fusion.2
  197.8 1.5 maximum_bitcast_fusion
  199.3 15.5 %all-to-all-done.5 = bf16[8,48,2048]{2,1,0:T(8,128)(2,1)S(1)} async-done(((bf16[8,48,2048]{2,1,0:T(8,128)(2,1)}), bf16[8,48,2048]{2,1,0:T(8,128)(2,1)S(1)}, u32[]{:S(2)}, u32[]{:S(2)}) %all-to-all-start.5) | async-done | bytes 1572896 | tf_op jit(solution)/shard_map/all_to_all | solution.py:97
  214.8 3.6 %all-to-all-start.6 = ((bf16[8,48,2048]{2,1,0:T(8,128)(2,1)}), bf16[8,48,2048]{2,1,0:T(8,128)(2,1)S(1)}, u32[]{:S(2)}, u32[]{:S(2)}) async-start(bf16[8,48,2048]{2,1,0:T(8,128)(2,1)} %bitcast.103), calls=%async_computation.6 | async-start | bytes 3145728 | tf_op jit(solution)/shard_map/all_to_all | solution.py:97
  219.4 2.5 %fusion.10 = bf16[128,512]{0,1:T(8,128)(2,1)S(1)} fusion(f32[512,128]{1,0:T(8,128)} %fusion.60, f32[512]{0:T(512)S(1)} %bitcast.116, bf16[128,4096]{1,0:T(8,128)(2,1)} %copy-done, bf16[128,2048]{1,0:T(8,128)(2,1)} %copy-done.11, bf16[128,2048]{1,0:T(8,128)(2,1)} %copy-done.24, bf16[128,2048]{1,0:T(8,128)(2,1)} %copy-done.9, ...), kind=kOutput, calls=%fused_computation.27 | convolution fusion | flops 277282816 | bytes 3016704 | tf_op jit(solution)/shard_map/dot_general | solution.py:108
  223.2 1.5 fusion.1
  224.7 14.6 %all-to-all-done.6 = bf16[8,48,2048]{2,1,0:T(8,128)(2,1)S(1)} async-done(((bf16[8,48,2048]{2,1,0:T(8,128)(2,1)}), bf16[8,48,2048]{2,1,0:T(8,128)(2,1)S(1)}, u32[]{:S(2)}, u32[]{:S(2)}) %all-to-all-start.6) | async-done | bytes 1572896 | tf_op jit(solution)/shard_map/all_to_all | solution.py:97
  241.2 1.5 maximum_bitcast_fusion.1
  (166 shorter events, 31.9 us)
Async XLA Ops:
  0.6 16.4 %copy-start.40 = (s32[1,128,3]{1,0,2:T(1,128)S(1)}, s32[1,128,3]{1,0,2:T(1,128)}, u32[]{:S(2)}) copy-start(s32[1,128,3]{1,0,2:T(1,128)} %param.5) | copy-start | bytes 4612
  4.2 20.7 %copy-start.33 = (bf16[128,2048]{1,0:T(8,128)(2,1)}, bf16[128,2048]{1,0:T(8,128)(2,1)S(1)}, u32[]{:S(2)}) copy-start(bf16[128,2048]{1,0:T(8,128)(2,1)S(1)} %get-tuple-element.17) | copy-start | bytes 1572868
  4.2 34.3 %collective-permute-start = (bf16[128,2048]{1,0:T(8,128)(2,1)S(1)}, bf16[128,2048]{1,0:T(8,128)(2,1)S(1)}, u32[]{:S(2)}, u32[]{:S(2)}) collective-permute-start(bf16[128,2048]{1,0:T(8,128)(2,1)S(1)} %get-tuple-element.17), channel_id=1, source_target_pairs={{0,8},{8,16},{16,24},{1,9},{9,17},{17,25},{2,10},{10,18},{18,26},{... | collective-permute-start | bytes 1572872 | tf_op jit(solution)/shard_map/ppermute | solution.py:13
  9.2 29.4 %collective-permute-start.3 = (bf16[128,2048]{1,0:T(8,128)(2,1)S(1)}, bf16[128,2048]{1,0:T(8,128)(2,1)S(1)}, u32[]{:S(2)}, u32[]{:S(2)}) collective-permute-start(bf16[128,2048]{1,0:T(8,128)(2,1)S(1)} %get-tuple-element.17), channel_id=1, source_target_pairs={{8,0},{16,8},{24,16},{9,1},{17,9},{25,17},{10,2},{18,10},{26,18},{... | collective-permute-start | bytes 1572872 | tf_op jit(solution)/shard_map/ppermute | solution.py:14
  10.5 39.4 %collective-permute-start.1 = (bf16[128,2048]{1,0:T(8,128)(2,1)S(1)}, bf16[128,2048]{1,0:T(8,128)(2,1)S(1)}, u32[]{:S(2)}, u32[]{:S(2)}) collective-permute-start(bf16[128,2048]{1,0:T(8,128)(2,1)S(1)} %get-tuple-element.17), channel_id=1, source_target_pairs={{0,24},{24,0},{1,25},{25,1},{2,26},{26,2},{3,27},{27,3},{4,28},{28... | collective-permute-start | bytes 1572872 | tf_op jit(solution)/shard_map/ppermute | solution.py:16
  18.3 8.3 %all-to-all-start = ((s32[8,1,48]{2,1,0:T(1,128)}), s32[8,1,48]{2,1,0:T(1,128)S(1)}, u32[]{:S(2)}, u32[]{:S(2)}) async-start(s32[8,1,48]{2,1,0:T(1,128)} %sub.117), calls=%async_computation | async-start | bytes 8192 | tf_op jit(solution)/shard_map/all_to_all | solution.py:79
  23.8 105.4 %copy-start.2 = (bf16[128,4096]{1,0:T(8,128)(2,1)}, bf16[128,4096]{1,0:T(8,128)(2,1)S(1)}, u32[]{:S(2)}) copy-start(bf16[128,4096]{1,0:T(8,128)(2,1)S(1)} %convert_bitcast_fusion) | copy-start | bytes 3145732
  26.6 11.2 %all-to-all-start.4 = ((s32[4,1,96]{2,1,0:T(1,128)}), s32[4,1,96]{2,1,0:T(1,128)S(1)}, u32[]{:S(2)}, u32[]{:S(2)}) async-start(s32[4,1,96]{2,1,0:T(1,128)} %bitcast.23), calls=%async_computation.4 | async-start | bytes 4096 | tf_op jit(solution)/shard_map/all_to_all | solution.py:84
  38.5 15.6 %collective-permute-start.5 = (bf16[128,2048]{1,0:T(8,128)(2,1)}, bf16[128,2048]{1,0:T(8,128)(2,1)}, u32[]{:S(2)}, u32[]{:S(2)}) collective-permute-start(bf16[128,2048]{1,0:T(8,128)(2,1)} %get-tuple-element.6), channel_id=1, source_target_pairs={{0,8},{8,16},{16,24},{1,9},{9,17},{17,25},{2,10},{10,18},{18,26},{... | collective-permute-start | bytes 1572872 | tf_op jit(solution)/shard_map/ppermute | solution.py:13
  41.8 17.1 %collective-permute-start.8 = (bf16[128,2048]{1,0:T(8,128)(2,1)}, bf16[128,2048]{1,0:T(8,128)(2,1)}, u32[]{:S(2)}, u32[]{:S(2)}) collective-permute-start(bf16[128,2048]{1,0:T(8,128)(2,1)} %get-tuple-element.6), channel_id=1, source_target_pairs={{8,0},{16,8},{24,16},{9,1},{17,9},{25,17},{10,2},{18,10},{26,18},{... | collective-permute-start | bytes 1572872 | tf_op jit(solution)/shard_map/ppermute | solution.py:14
  43.1 21.7 %collective-permute-start.2 = (bf16[128,2048]{1,0:T(8,128)(2,1)S(1)}, bf16[128,2048]{1,0:T(8,128)(2,1)}, u32[]{:S(2)}, u32[]{:S(2)}) collective-permute-start(bf16[128,2048]{1,0:T(8,128)(2,1)S(1)} %collective-permute-done), channel_id=1, source_target_pairs={{0,8},{8,16},{16,24},{1,9},{9,17},{17,25},{2,10},{10,18},{18,26},{... | collective-permute-start | bytes 1572872 | tf_op jit(solution)/shard_map/ppermute | solution.py:25
  48.4 32.9 %collective-permute-start.4 = (bf16[128,2048]{1,0:T(8,128)(2,1)S(1)}, bf16[128,2048]{1,0:T(8,128)(2,1)}, u32[]{:S(2)}, u32[]{:S(2)}) collective-permute-start(bf16[128,2048]{1,0:T(8,128)(2,1)S(1)} %collective-permute-done.3), channel_id=1, source_target_pairs={{8,0},{16,8},{24,16},{9,1},{17,9},{25,17},{10,2},{18,10},{26,18},{... | collective-permute-start | bytes 1572872 | tf_op jit(solution)/shard_map/ppermute | solution.py:26
  49.9 33.8 %copy-start.34 = (bf16[128,2048]{1,0:T(8,128)(2,1)S(1)}, bf16[128,2048]{1,0:T(8,128)(2,1)}, u32[]{:S(2)}) copy-start(bf16[128,2048]{1,0:T(8,128)(2,1)} %copy-done.33) | copy-start | bytes 1572868
  49.9 39.8 %collective-permute-start.6 = (bf16[128,2048]{1,0:T(8,128)(2,1)}, bf16[128,2048]{1,0:T(8,128)(2,1)}, u32[]{:S(2)}, u32[]{:S(2)}) collective-permute-start(bf16[128,2048]{1,0:T(8,128)(2,1)} %get-tuple-element.6), channel_id=1, source_target_pairs={{0,24},{24,0},{1,25},{25,1},{2,26},{26,2},{3,27},{27,3},{4,28},{28... | collective-permute-start | bytes 1572872 | tf_op jit(solution)/shard_map/ppermute | solution.py:16
  54.1 31.8 %copy-start.6 = (bf16[128,2048]{1,0:T(8,128)(2,1)}, bf16[128,2048]{1,0:T(8,128)(2,1)S(1)}, u32[]{:S(2)}) copy-start(bf16[128,2048]{1,0:T(8,128)(2,1)S(1)} %get-tuple-element.24) | copy-start | bytes 1572868
  54.1 75.0 %copy-start.4 = (bf16[128,2048]{1,0:T(8,128)(2,1)}, bf16[128,2048]{1,0:T(8,128)(2,1)S(1)}, u32[]{:S(2)}) copy-start(bf16[128,2048]{1,0:T(8,128)(2,1)S(1)} %get-tuple-element.23) | copy-start | bytes 1572868
  58.8 35.5 %collective-permute-start.10 = (bf16[128,2048]{1,0:T(8,128)(2,1)}, bf16[128,2048]{1,0:T(8,128)(2,1)}, u32[]{:S(2)}, u32[]{:S(2)}) collective-permute-start(bf16[128,2048]{1,0:T(8,128)(2,1)} %get-tuple-element.7), channel_id=1, source_target_pairs={{0,8},{8,16},{16,24},{1,9},{9,17},{17,25},{2,10},{10,18},{18,26},{... | collective-permute-start | bytes 1572872 | tf_op jit(solution)/shard_map/ppermute | solution.py:13
  61.2 33.1 %collective-permute-start.13 = (bf16[128,2048]{1,0:T(8,128)(2,1)}, bf16[128,2048]{1,0:T(8,128)(2,1)}, u32[]{:S(2)}, u32[]{:S(2)}) collective-permute-start(bf16[128,2048]{1,0:T(8,128)(2,1)} %get-tuple-element.7), channel_id=1, source_target_pairs={{8,0},{16,8},{24,16},{9,1},{17,9},{25,17},{10,2},{18,10},{26,18},{... | collective-permute-start | bytes 1572872 | tf_op jit(solution)/shard_map/ppermute | solution.py:14
  64.8 35.4 %collective-permute-start.7 = (bf16[128,2048]{1,0:T(8,128)(2,1)}, bf16[128,2048]{1,0:T(8,128)(2,1)}, u32[]{:S(2)}, u32[]{:S(2)}) collective-permute-start(bf16[128,2048]{1,0:T(8,128)(2,1)} %collective-permute-done.5), channel_id=1, source_target_pairs={{0,8},{8,16},{16,24},{1,9},{9,17},{17,25},{2,10},{10,18},{18,26},{... | collective-permute-start | bytes 1572872 | tf_op jit(solution)/shard_map/ppermute | solution.py:25
  81.3 42.0 %collective-permute-start.9 = (bf16[128,2048]{1,0:T(8,128)(2,1)}, bf16[128,2048]{1,0:T(8,128)(2,1)}, u32[]{:S(2)}, u32[]{:S(2)}) collective-permute-start(bf16[128,2048]{1,0:T(8,128)(2,1)} %collective-permute-done.8), channel_id=1, source_target_pairs={{8,0},{16,8},{24,16},{9,1},{17,9},{25,17},{10,2},{18,10},{26,18},{... | collective-permute-start | bytes 1572872 | tf_op jit(solution)/shard_map/ppermute | solution.py:26
  85.9 66.2 %all-to-all-start.1 = ((bf16[8,48,2048]{2,1,0:T(8,128)(2,1)}), bf16[8,48,2048]{2,1,0:T(8,128)(2,1)S(1)}, u32[]{:S(2)}, u32[]{:S(2)}) async-start(bf16[8,48,2048]{2,1,0:T(8,128)(2,1)} %bitcast.105), calls=%async_computation.1 | async-start | bytes 3145728 | tf_op jit(solution)/shard_map/all_to_all | solution.py:97
  89.6 4.8 %copy-start.30 = (bf16[128,2048]{1,0:T(8,128)(2,1)S(1)}, bf16[128,2048]{1,0:T(8,128)(2,1)}, u32[]{:S(2)}) copy-start(bf16[128,2048]{1,0:T(8,128)(2,1)} %get-tuple-element.8) | copy-start | bytes 1572868
  89.6 36.1 %copy-start.37 = (bf16[128,2048]{1,0:T(8,128)(2,1)S(1)}, bf16[128,2048]{1,0:T(8,128)(2,1)}, u32[]{:S(2)}) copy-start(bf16[128,2048]{1,0:T(8,128)(2,1)} %get-tuple-element.6) | copy-start | bytes 1572868
  89.7 36.9 %collective-permute-start.11 = (bf16[128,2048]{1,0:T(8,128)(2,1)}, bf16[128,2048]{1,0:T(8,128)(2,1)S(1)}, u32[]{:S(2)}, u32[]{:S(2)}) collective-permute-start(bf16[128,2048]{1,0:T(8,128)(2,1)} %get-tuple-element.7), channel_id=1, source_target_pairs={{0,24},{24,0},{1,25},{25,1},{2,26},{26,2},{3,27},{27,3},{4,28},{28... | collective-permute-start | bytes 1572872 | tf_op jit(solution)/shard_map/ppermute | solution.py:16
  94.4 36.3 %copy-start.13 = (bf16[128,2048]{1,0:T(8,128)(2,1)}, bf16[128,2048]{1,0:T(8,128)(2,1)S(1)}, u32[]{:S(2)}) copy-start(bf16[128,2048]{1,0:T(8,128)(2,1)S(1)} %get-tuple-element.25) | copy-start | bytes 1572868
  94.4 36.3 %copy-start.15 = (bf16[128,2048]{1,0:T(8,128)(2,1)}, bf16[128,2048]{1,0:T(8,128)(2,1)S(1)}, u32[]{:S(2)}) copy-start(bf16[128,2048]{1,0:T(8,128)(2,1)S(1)} %get-tuple-element.26) | copy-start | bytes 1572868
  94.4 38.4 %collective-permute-start.15 = (bf16[128,2048]{1,0:T(8,128)(2,1)S(1)}, bf16[128,2048]{1,0:T(8,128)(2,1)}, u32[]{:S(2)}, u32[]{:S(2)}) collective-permute-start(bf16[128,2048]{1,0:T(8,128)(2,1)S(1)} %copy-done.30), channel_id=1, source_target_pairs={{0,8},{8,16},{16,24},{1,9},{9,17},{17,25},{2,10},{10,18},{18,26},{... | collective-permute-start | bytes 1572872 | tf_op jit(solution)/shard_map/ppermute | solution.py:13
  97.4 49.2 %collective-permute-start.16 = (bf16[128,2048]{1,0:T(8,128)(2,1)S(1)}, bf16[128,2048]{1,0:T(8,128)(2,1)S(1)}, u32[]{:S(2)}, u32[]{:S(2)}) collective-permute-start(bf16[128,2048]{1,0:T(8,128)(2,1)S(1)} %copy-done.30), channel_id=1, source_target_pairs={{0,24},{24,0},{1,25},{25,1},{2,26},{26,2},{3,27},{27,3},{4,28},{28... | collective-permute-start | bytes 1572872 | tf_op jit(solution)/shard_map/ppermute | solution.py:16
  100.1 38.2 %collective-permute-start.18 = (bf16[128,2048]{1,0:T(8,128)(2,1)S(1)}, bf16[128,2048]{1,0:T(8,128)(2,1)}, u32[]{:S(2)}, u32[]{:S(2)}) collective-permute-start(bf16[128,2048]{1,0:T(8,128)(2,1)S(1)} %copy-done.30), channel_id=1, source_target_pairs={{8,0},{16,8},{24,16},{9,1},{17,9},{25,17},{10,2},{18,10},{26,18},{... | collective-permute-start | bytes 1572872 | tf_op jit(solution)/shard_map/ppermute | solution.py:14
  123.3 19.6 %collective-permute-start.12 = (bf16[128,2048]{1,0:T(8,128)(2,1)}, bf16[128,2048]{1,0:T(8,128)(2,1)S(1)}, u32[]{:S(2)}, u32[]{:S(2)}) collective-permute-start(bf16[128,2048]{1,0:T(8,128)(2,1)} %collective-permute-done.10), channel_id=1, source_target_pairs={{0,8},{8,16},{16,24},{1,9},{9,17},{17,25},{2,10},{10,18},{18,26},{... | collective-permute-start | bytes 1572872 | tf_op jit(solution)/shard_map/ppermute | solution.py:25
  125.7 4.9 %copy-start.26 = (bf16[128,2048]{1,0:T(8,128)(2,1)}, bf16[128,2048]{1,0:T(8,128)(2,1)S(1)}, u32[]{:S(2)}) copy-start(bf16[128,2048]{1,0:T(8,128)(2,1)S(1)} %broadcast_select_fusion.6) | copy-start | bytes 1572868
  126.5 2.7 %copy-start.7 = (bf16[128,2048]{1,0:T(8,128)(2,1)S(1)}, bf16[128,2048]{1,0:T(8,128)(2,1)}, u32[]{:S(2)}) copy-start(bf16[128,2048]{1,0:T(8,128)(2,1)} %copy-done.6) | copy-start | bytes 1572868
  126.5 2.7 %copy-start.22 = (bf16[128,2048]{1,0:T(8,128)(2,1)S(1)}, bf16[128,2048]{1,0:T(8,128)(2,1)}, u32[]{:S(2)}) copy-start(bf16[128,2048]{1,0:T(8,128)(2,1)} %copy-done.21) | copy-start | bytes 1572868
  126.5 2.7 %copy-start.35 = (bf16[128,2048]{1,0:T(8,128)(2,1)S(1)}, bf16[128,2048]{1,0:T(8,128)(2,1)}, u32[]{:S(2)}) copy-start(bf16[128,2048]{1,0:T(8,128)(2,1)} %copy-done.33) | copy-start | bytes 1572868
  126.5 20.0 %collective-permute-start.14 = (bf16[128,2048]{1,0:T(8,128)(2,1)}, bf16[128,2048]{1,0:T(8,128)(2,1)S(1)}, u32[]{:S(2)}, u32[]{:S(2)}) collective-permute-start(bf16[128,2048]{1,0:T(8,128)(2,1)} %collective-permute-done.13), channel_id=1, source_target_pairs={{8,0},{16,8},{24,16},{9,1},{17,9},{25,17},{10,2},{18,10},{26,18},{... | collective-permute-start | bytes 1572872 | tf_op jit(solution)/shard_map/ppermute | solution.py:26
  129.2 19.7 %copy-start.9 = (bf16[128,2048]{1,0:T(8,128)(2,1)}, bf16[128,2048]{1,0:T(8,128)(2,1)S(1)}, u32[]{:S(2)}) copy-start(bf16[128,2048]{1,0:T(8,128)(2,1)S(1)} %get-tuple-element.19) | copy-start | bytes 1572868
  129.2 19.7 %copy-start.11 = (bf16[128,2048]{1,0:T(8,128)(2,1)}, bf16[128,2048]{1,0:T(8,128)(2,1)S(1)}, u32[]{:S(2)}) copy-start(bf16[128,2048]{1,0:T(8,128)(2,1)S(1)} %get-tuple-element.20) | copy-start | bytes 1572868
  132.8 25.5 %collective-permute-start.17 = (bf16[128,2048]{1,0:T(8,128)(2,1)}, bf16[128,2048]{1,0:T(8,128)(2,1)}, u32[]{:S(2)}, u32[]{:S(2)}) collective-permute-start(bf16[128,2048]{1,0:T(8,128)(2,1)} %collective-permute-done.15), channel_id=1, source_target_pairs={{0,8},{8,16},{16,24},{1,9},{9,17},{17,25},{2,10},{10,18},{18,26},{... | collective-permute-start | bytes 1572872 | tf_op jit(solution)/shard_map/ppermute | solution.py:25
  138.3 20.0 %collective-permute-start.19 = (bf16[128,2048]{1,0:T(8,128)(2,1)}, bf16[128,2048]{1,0:T(8,128)(2,1)}, u32[]{:S(2)}, u32[]{:S(2)}) collective-permute-start(bf16[128,2048]{1,0:T(8,128)(2,1)} %collective-permute-done.18), channel_id=1, source_target_pairs={{8,0},{16,8},{24,16},{9,1},{17,9},{25,17},{10,2},{18,10},{26,18},{... | collective-permute-start | bytes 1572872 | tf_op jit(solution)/shard_map/ppermute | solution.py:26
  152.2 24.8 %all-to-all-start.2 = ((bf16[8,48,2048]{2,1,0:T(8,128)(2,1)}), bf16[8,48,2048]{2,1,0:T(8,128)(2,1)S(1)}, u32[]{:S(2)}, u32[]{:S(2)}) async-start(bf16[8,48,2048]{2,1,0:T(8,128)(2,1)} %bitcast.106), calls=%async_computation.2 | async-start | bytes 3145728 | tf_op jit(solution)/shard_map/all_to_all | solution.py:97
  155.9 3.6 %copy-start.1 = (bf16[128,4096]{1,0:T(8,128)(2,1)S(1)}, bf16[128,4096]{1,0:T(8,128)(2,1)}, u32[]{:S(2)}) copy-start(bf16[128,4096]{1,0:T(8,128)(2,1)} %copy-done) | copy-start | bytes 3145732
  155.9 3.6 %copy-start.17 = (bf16[128,2048]{1,0:T(8,128)(2,1)S(1)}, bf16[128,2048]{1,0:T(8,128)(2,1)}, u32[]{:S(2)}) copy-start(bf16[128,2048]{1,0:T(8,128)(2,1)} %get-tuple-element.21) | copy-start | bytes 1572868
  155.9 3.6 %copy-start.19 = (bf16[128,2048]{1,0:T(8,128)(2,1)S(1)}, bf16[128,2048]{1,0:T(8,128)(2,1)}, u32[]{:S(2)}) copy-start(bf16[128,2048]{1,0:T(8,128)(2,1)} %get-tuple-element.22) | copy-start | bytes 1572868
  155.9 3.6 %copy-start.31 = (bf16[128,2048]{1,0:T(8,128)(2,1)S(1)}, bf16[128,2048]{1,0:T(8,128)(2,1)}, u32[]{:S(2)}) copy-start(bf16[128,2048]{1,0:T(8,128)(2,1)} %get-tuple-element.8) | copy-start | bytes 1572868
  180.4 9.8 %all-to-all-start.3 = ((f32[32,1,152]{2,1,0:T(1,128)}), f32[32,1,152]{2,1,0:T(1,128)S(1)}, u32[]{:S(2)}, u32[]{:S(2)}) async-start(f32[32,1,152]{2,1,0:T(1,128)} %all_to_all.31), calls=%async_computation.3 | async-start | bytes 65536 | tf_op jit(solution)/shard_map/all_to_all | solution.py:137
  190.2 24.5 %all-to-all-start.5 = ((bf16[8,48,2048]{2,1,0:T(8,128)(2,1)}), bf16[8,48,2048]{2,1,0:T(8,128)(2,1)S(1)}, u32[]{:S(2)}, u32[]{:S(2)}) async-start(bf16[8,48,2048]{2,1,0:T(8,128)(2,1)} %bitcast.104), calls=%async_computation.5 | async-start | bytes 3145728 | tf_op jit(solution)/shard_map/all_to_all | solution.py:97
  214.8 24.5 %all-to-all-start.6 = ((bf16[8,48,2048]{2,1,0:T(8,128)(2,1)}), bf16[8,48,2048]{2,1,0:T(8,128)(2,1)S(1)}, u32[]{:S(2)}, u32[]{:S(2)}) async-start(bf16[8,48,2048]{2,1,0:T(8,128)(2,1)} %bitcast.103), calls=%async_computation.6 | async-start | bytes 3145728 | tf_op jit(solution)/shard_map/all_to_all | solution.py:97
  224.7 15.1 %copy-start.18 = (bf16[128,2048]{1,0:T(8,128)(2,1)S(1)}, bf16[128,2048]{1,0:T(8,128)(2,1)}, u32[]{:S(2)}) copy-start(bf16[128,2048]{1,0:T(8,128)(2,1)} %get-tuple-element.21) | copy-start | bytes 1572868
  (20 other events, 30.7 us)

commit v2 on v0

v2 whole, which is shorter than its diff:
```python
import jax
import jax.numpy as jnp
from jax import lax
from jax.sharding import PartitionSpec as P

inverse_temp = 50.0
pieces = 2


def matmul(a, b, left, right):
    return lax.dot_general(a, b, (((left,), (right,)), ((), ())), preferred_element_type=jnp.float32)


def per_device(queries, passages, hard_ids):
    row_count, features = queries.shape[1:]
    hard = hard_ids.shape[2]
    dp_count = lax.axis_size("dp")
    group_count = lax.axis_size("group")
    devices = dp_count * group_count
    me = lax.axis_index("dp")
    my_group = lax.axis_index("group")
    batch_rows = row_count * dp_count
    entries = row_count * hard
    capacity = (entries + devices - 1) // devices
    slots = devices * capacity
    piece_rows = row_count // pieces

    query_low = queries[0].astype(jnp.bfloat16)
    passage_low = passages[0].astype(jnp.bfloat16)

    gathered = []
    for i in range(pieces):
        piece = query_low[i * piece_rows : (i + 1) * piece_rows]
        gathered.append(lax.all_gather(piece, "dp", axis=0, tiled=True))

    ids = hard_ids[0].T.reshape(entries)
    owner_group = ids // batch_rows
    owner_dp = ids % batch_rows // row_count
    owner = owner_dp * group_count + owner_group
    order = jnp.arange(entries)
    earlier = (order[None, :] < order[:, None]) & (owner[None, :] == owner[:, None])
    rank = jnp.sum(earlier.astype(jnp.int32), axis=1)
    slot = owner * capacity + rank
    placed = jnp.arange(slots)[:, None] == slot[None, :]
    query_row = jnp.sum(jnp.where(placed, order[None, :] % row_count + 1, 0), axis=1) - 1
    passage_row = jnp.sum(jnp.where(placed, ids[None, :] % row_count + 1, 0), axis=1) - 1

    plane = group_count * capacity
    request = jnp.concatenate(
        [
            passage_row.reshape(dp_count, group_count, capacity),
            jnp.broadcast_to(query_row.reshape(dp_count, 1, plane), (dp_count, group_count, plane)),
        ],
        axis=2,
    ).reshape(devices, capacity + plane)
    request = lax.all_to_all(request, ("dp", "group"), split_axis=0, concat_axis=0, tiled=True)
    request = request.reshape(dp_count, group_count, capacity + plane)
    sent_row = request[:, :, :capacity].transpose(1, 0, 2).reshape(slots)
    wanting = lax.dynamic_index_in_dim(request[:, :, capacity:], my_group, axis=1, keepdims=False)
    wanting = wanting.reshape(dp_count, group_count, capacity).transpose(1, 0, 2).reshape(slots)
    wanting_dp = jnp.arange(slots) // capacity % dp_count

    select = (jnp.arange(row_count)[:, None] == sent_row[None, :]).astype(jnp.bfloat16)

    def exchange(rows):
        rows = rows.astype(jnp.bfloat16).reshape(group_count, dp_count * capacity, features)
        return lax.all_to_all(rows, "group", split_axis=0, concat_axis=0, tiled=True).reshape(slots, features)

    table = jnp.concatenate([passage_low, exchange(matmul(select, passage_low, 0, 0))], axis=0)

    weights, losses, query_grad = [], [], []
    share = None
    for i, piece in enumerate(gathered):
        if share is not None:
            piece = lax.optimization_barrier((piece, share))[0]
        first = i * piece_rows
        count = dp_count * piece_rows
        row = jnp.arange(count)[:, None]
        local = wanting - first
        target = jnp.where((local >= 0) & (local < piece_rows), wanting_dp * piece_rows + local, -1)
        mine = jnp.arange(row_count) - first
        positive = jnp.where((mine >= 0) & (mine < piece_rows), me * piece_rows + mine, -1)
        positive = row == jnp.concatenate([positive, jnp.full((slots,), -1, jnp.int32)])[None, :]
        masked = row != jnp.concatenate([jnp.broadcast_to(row[0], (row_count,)) * 0 - 1, target])[None, :]
        masked = masked & (jnp.arange(row_count + slots)[None, :] >= row_count)
        scores = jnp.where(masked, -jnp.inf, matmul(piece, table, 1, 1) * inverse_temp)
        highest = jnp.max(scores, axis=1)
        total = jnp.sum(jnp.exp(scores - highest[:, None]), axis=1)
        stats = jnp.broadcast_to(jnp.stack([highest, total])[None], (dp_count, 2, count))
        stats = lax.all_to_all(stats, "dp", split_axis=0, concat_axis=0, tiled=True)
        highest = jnp.max(stats[:, 0], axis=0)
        normal = highest + jnp.log(jnp.sum(stats[:, 1] * jnp.exp(stats[:, 0] - highest[None, :]), axis=0))
        loss = normal - jnp.sum(jnp.where(positive, scores, 0.0), axis=1)
        losses.append(lax.dynamic_slice_in_dim(loss, me * piece_rows, piece_rows, axis=0))
        weight = jnp.exp(scores - normal[:, None]) - positive.astype(jnp.float32)
        weights.append(weight.astype(jnp.bfloat16))
        share = (matmul(weights[-1], table, 1, 0) * inverse_temp).astype(jnp.bfloat16)
        query_grad.append(lax.psum_scatter(share, "dp", scatter_dimension=0, tiled=True))

    weights = jnp.concatenate(weights, axis=0)
    everything = jnp.concatenate(gathered, axis=0)
    passage_grad = matmul(weights[:, :row_count], everything, 0, 0)
    hard_grad = matmul(weights[:, row_count:], everything, 0, 0) * inverse_temp
    passage_grad = passage_grad * inverse_temp + matmul(select, exchange(hard_grad), 1, 0)
    query_grad = jnp.concatenate(query_grad, axis=0).astype(jnp.float32)
    return (query_grad[None], passage_grad[None], jnp.concatenate(losses)[None])


def solution(mesh):
    return jax.shard_map(
        per_device,
        mesh=mesh,
        in_specs=(P("group", "dp", None), P("group", "dp", None), P("group", "dp", None)),
        out_specs=(P("group", "dp", None), P("group", "dp", None), P("group", "dp")),
        check_vma=False,
    )
```

time: 482 us -> 207 us (0.43)
  waiting for transfers between devices: 341 us -> 118 us
  local copies, waits for them, and re-layouts: 55.1 us -> 1.84 us
  other arithmetic: 30.8 us -> 7.26 us
  blocking collectives: 0 us -> 16.4 us
  matrix products: 22 us -> 33.2 us
    all_to_all x2, waiting for transfers between devices: 336 us -> 69.5 us  [exchange(): lax.all_to_all(rows, 'group', split_axis=0, concat_axis=0, tiled=True)]
    reduce_scatter x1 -> x2, waiting for transfers between devices: 0.02 us -> 23 us  [per_device(): lax.psum_scatter(share, 'dp', scatter_dimension=0, tiled=True)]
    reshape x4 -> x2, local copies, waits for them, and re-layouts: 17.9 us -> 0.2 us  [per_device(): wanting.reshape(dp_count, group_count, capacity).transpose(1, 0, 2)]
    all_gather x1 -> x2, waiting for transfers between devices: 0.02 us -> 17.7 us  [per_device(): gathered.append(lax.all_gather(piece, 'dp', axis=0, tiled=True))]
    all_to_all x0 -> x2, blocking collectives: none -> 16.4 us  [per_device(): stats = lax.all_to_all(stats, 'dp', split_axis=0, concat_axis=0, tiled=True)]
    mul x3 -> x0, local copies, waits for them, and re-layouts: 15.7 us -> none  [per_device(): inverse_temp * hard_coeff[:, :, None]]
    gather x3 -> x0, local copies, waits for them, and re-layouts: 13.6 us -> none  [the longest x2 9.54 us: per_device(): jnp.take(passage_low, safe.reshape(-1), axis=0)]
    dot_general x5 -> x8, matrix products: 22 us -> 33.2 us  [matmul(): lax.dot_general(a, b, (((left,), (right,)), ((), ())), preferred_element_...]
  transfers between devices with their start and end apart: 5 -> 7, of which waited for: 3 -> 5; matrix products, arithmetic and copies ran while one was open for 15% -> 18% of each run, Pallas kernels for 0% -> 0%
where the time goes in v2:
time: 207 us; the launch traced here: 206 us
  waiting for transfers between devices  118 us (57%)
  matrix products  33.2 us (16%)
  blocking collectives  16.4 us (8%)
  starting transfers between devices  15.6 us (8%)
  between operations  14 us (7%)
  other arithmetic  7.26 us (4%)
    all_to_all x2, waiting for transfers between devices, exchange(): lax.all_to_all(rows, 'group', split_axis=0, concat_axis=0, tiled=True)  69.5 us
    dot_general x8, matrix products, matmul(): lax.dot_general(a, b, (((left,), (right,)), ((), ())), preferred_element_...  33.2 us
    reduce_scatter x2, waiting for transfers between devices, per_device(): lax.psum_scatter(share, 'dp', scatter_dimension=0, tiled=True)  23 us
    all_gather x2, waiting for transfers between devices, per_device(): gathered.append(lax.all_gather(piece, 'dp', axis=0, tiled=True))  17.7 us
    all_to_all x2, blocking collectives, per_device(): stats = lax.all_to_all(stats, 'dp', split_axis=0, concat_axis=0, tiled=True)  16.4 us
    all_to_all x2, starting transfers between devices, exchange(): lax.all_to_all(rows, 'group', split_axis=0, concat_axis=0, tiled=True)  8.14 us
    all_to_all x1, starting transfers between devices, per_device(): lax.all_to_all(request, ('dp', 'group'), split_axis=0, concat_axis=0, til...  7.3 us
    all_to_all x1, waiting for transfers between devices, per_device(): lax.all_to_all(request, ('dp', 'group'), split_axis=0, concat_axis=0, til...  7.01 us
  transfers between devices with their start and end apart: 7, of which 5 were waited for; matrix products, arithmetic and copies ran while one was open for 18% of the time, Pallas kernels for 0%

profile of v2, /device:TPU:0, one launch (start us, length us, event | category | flops | bytes accessed | tf_op | source)
XLA Modules:
  0.0 206.2 jit_solution(17032840147580423641)
XLA Ops:
  7.2 0.0 copy-start.2
  7.2 0.0 copy-start
  7.2 0.0 all-gather.5.cloned.1.call-start
  7.2 1.9 convert_element_type.52
  9.1 1.0 fusion.44
  10.1 0.0 all-gather.5.cloned.1.call-update
  10.2 0.2 convert_reduce_fusion
  10.4 0.2 select_reduce_fusion.1
  10.7 0.1 sub.99
  10.8 0.1 sub.97
  10.9 0.7 pad_add_fusion
  11.6 7.3 %all-to-all-start = ((s32[32,1,108]{2,1,0:T(1,128)}), s32[32,1,108]{2,1,0:T(1,128)S(1)}, u32[]{:S(2)}, u32[]{:S(2)}) async-start(s32[32,1,108]{2,1,0:T(1,128)} %bitcast.4), calls=%async_computation | async-start | bytes 32768 | tf_op jit(solution)/shard_map/all_to_all | solution.py:56
  18.9 0.1 convert_bitcast_fusion
  19.0 7.0 %all-to-all-done = s32[32,1,108]{2,1,0:T(1,128)S(1)} async-done(((s32[32,1,108]{2,1,0:T(1,128)}), s32[32,1,108]{2,1,0:T(1,128)S(1)}, u32[]{:S(2)}, u32[]{:S(2)}) %all-to-all-start) | async-done | bytes 13856 | tf_op jit(solution)/shard_map/all_to_all | solution.py:56
  26.0 0.1 eq.79
  26.1 2.7 %convolution_convert_fusion = bf16[384,4096]{1,0:T(8,128)(2,1)} fusion(bf16[128,4096]{1,0:T(8,128)(2,1)S(1)} %convert_bitcast_fusion, s32[384]{0:T(512)S(1)} %eq.79), kind=kOutput, calls=%fused_computation.1 | convolution fusion | flops 404275200 | bytes 4195840 | tf_op jit(solution)/shard_map/dot_general | solution.py:11
  28.9 4.4 %all-to-all-start.1 = ((bf16[8,48,4096]{2,1,0:T(8,128)(2,1)}), bf16[8,48,4096]{2,1,0:T(8,128)(2,1)}, u32[]{:S(2)}, u32[]{:S(2)}) async-start(bf16[8,48,4096]{2,1,0:T(8,128)(2,1)} %bitcast.9), calls=%async_computation.1 | async-start | bytes 6291456 | tf_op jit(solution)/shard_map/all_to_all | solution.py:67
  33.3 0.0 all-gather.7.cloned.1.call-start
  33.4 0.7 all-gather.7.cloned.1.call-update
  34.1 0.0 reduce-scatter.3.cloned.1.call-start
  34.2 0.1 slice.50
  34.3 0.1 reshape.309
  34.4 0.1 reshape.310
  34.5 36.7 %all-to-all-done.1 = bf16[8,48,4096]{2,1,0:T(8,128)(2,1)} async-done(((bf16[8,48,4096]{2,1,0:T(8,128)(2,1)}), bf16[8,48,4096]{2,1,0:T(8,128)(2,1)}, u32[]{:S(2)}, u32[]{:S(2)}) %all-to-all-start.1) | async-done | bytes 3145760 | tf_op jit(solution)/shard_map/all_to_all | solution.py:67
  71.2 3.8 %fusion.47 = (f32[256]{0:T(256)S(1)}, f32[256,512]{0,1:T(8,128)S(1)}) fusion(bf16[1,256,4096]{2,1,0:T(8,128)(2,1)} %all-gather.5.cloned.1.call-done, bf16[384,4096]{1,0:T(8,128)(2,1)} %bitcast.10, bf16[128,4096]{1,0:T(8,128)(2,1)S(1)} %convert_bitcast_fusion, pred[512]{0:T(512)(128)(4,1)S(1)} %iota_compare_fusion.9, s32[512]{0:T(512)S(1)} %concatenate.46), kind=kOutput, calls=%fused_computation.120 | convolution fusion | flops 1082785536 | bytes 6819328 | tf_op jit(solution)/shard_map/dot_general | solution.py:11
  75.0 0.2 select_reduce_fusion.3
  75.2 8.1 %all_to_all.29 = f32[4,2,256]{2,1,0:T(2,128)S(1)} all-to-all(f32[4,2,256]{2,1,0:T(2,128)S(1)} %broadcast_in_dim.49), channel_id=1, replica_groups=mesh['dp'=4,'group'=8] {'dp'}, dimensions={0} | all-to-all | bytes 16384 | tf_op jit(solution)/shard_map/all_to_all | solution.py:90
  83.4 0.1 subtract_convert_fusion.1
  83.5 4.6 %fusion = bf16[256,4096]{1,0:T(8,128)(2,1)} fusion(bf16[256,512]{0,1:T(8,128)(2,1)S(1)} %subtract_convert_fusion.1, bf16[384,4096]{1,0:T(8,128)(2,1)} %bitcast.10, bf16[128,4096]{1,0:T(8,128)(2,1)S(1)} %convert_bitcast_fusion), kind=kOutput, calls=%fused_computation.4 | convolution fusion | flops 1084227584 | bytes 6553600 | tf_op jit(solution)/shard_map/dot_general | solution.py:11
  88.1 0.0 reduce-scatter.3.cloned.1.call-update
  88.2 0.0 reduce-scatter.5.cloned.1.call-start
  88.2 17.7 %all-gather.7.cloned.1.call-done = bf16[1,256,4096]{2,1,0:T(8,128)(2,1)} async-done(((bf16[1,64,4096]{2,1,0:T(8,128)(2,1)}), bf16[1,256,4096]{2,1,0:T(8,128)(2,1)}) %all-gather.7.cloned.1.call-update) | async-done | bytes 2097168 | tf_op jit(solution)/shard_map/all_gather | solution.py:34
  105.9 3.8 %fusion.48 = (f32[256]{0:T(256)S(1)}, f32[256,512]{0,1:T(8,128)S(1)}) fusion(bf16[256,4096]{1,0:T(8,128)(2,1)} %bitcast.97, bf16[384,4096]{1,0:T(8,128)(2,1)} %bitcast.10, bf16[128,4096]{1,0:T(8,128)(2,1)S(1)} %convert_bitcast_fusion, pred[512]{0:T(512)(128)(4,1)S(1)} %iota_compare_fusion.9, s32[512]{0:T(512)S(1)} %concatenate.50), kind=kOutput, calls=%fused_computation.121 | convolution fusion | flops 1082785536 | bytes 6819328 | tf_op jit(solution)/shard_map/dot_general | solution.py:11
  109.7 0.2 select_reduce_fusion.2
  109.9 8.3 %all_to_all.30 = f32[4,2,256]{2,1,0:T(2,128)S(1)} all-to-all(f32[4,2,256]{2,1,0:T(2,128)S(1)} %broadcast_in_dim.50), channel_id=1, replica_groups=mesh['dp'=4,'group'=8] {'dp'}, dimensions={0} | all-to-all | bytes 16384 | tf_op jit(solution)/shard_map/all_to_all | solution.py:90
  118.2 0.1 subtract_convert_fusion
  118.4 4.6 %fusion.1 = bf16[256,4096]{1,0:T(8,128)(2,1)} fusion(bf16[256,512]{0,1:T(8,128)(2,1)S(1)} %subtract_convert_fusion, bf16[384,4096]{1,0:T(8,128)(2,1)} %bitcast.10, bf16[128,4096]{1,0:T(8,128)(2,1)S(1)} %convert_bitcast_fusion), kind=kOutput, calls=%fused_computation.5 | convolution fusion | flops 1084227584 | bytes 6553600 | tf_op jit(solution)/shard_map/dot_general | solution.py:11
  123.0 0.0 reduce-scatter.5.cloned.1.call-update
  123.1 5.7 %multiply_convert_fusion = bf16[384,4096]{1,0:T(8,128)(2,1)} fusion(bf16[256,4096]{1,0:T(8,128)(2,1)} %bitcast.98, bf16[256,4096]{1,0:T(8,128)(2,1)} %bitcast.95, bf16[256,512]{0,1:T(8,128)(2,1)S(1)} %subtract_convert_fusion, bf16[256,512]{0,1:T(8,128)(2,1)S(1)} %subtract_convert_fusion.1), kind=kOutput, calls=%fused_computation | convolution fusion | flops 1622933504 | bytes 7864320 | tf_op jit(solution)/shard_map/dot_general | solution.py:11
  128.7 3.7 %all-to-all-start.4 = ((bf16[8,48,4096]{2,1,0:T(8,128)(2,1)}), bf16[8,48,4096]{2,1,0:T(8,128)(2,1)S(1)}, u32[]{:S(2)}, u32[]{:S(2)}) async-start(bf16[8,48,4096]{2,1,0:T(8,128)(2,1)} %bitcast.85), calls=%async_computation.6 | async-start | bytes 6291456 | tf_op jit(solution)/shard_map/all_to_all | solution.py:67
  132.4 0.1 dynamic_slice.11
  132.5 0.1 dynamic_slice.12
  132.6 0.6 maximum_bitcast_fusion
  133.2 4.4 %convolution_multiply_fusion.2 = f32[128,4096]{1,0:T(8,128)} fusion(bf16[256,4096]{1,0:T(8,128)(2,1)} %bitcast.99, bf16[256,4096]{1,0:T(8,128)(2,1)} %bitcast.96, bf16[256,512]{0,1:T(8,128)(2,1)} %copy-done.1, bf16[256,512]{0,1:T(8,128)(2,1)S(1)} %subtract_convert_fusion.1), kind=kOutput, calls=%fused_computation.8 | convolution fusion | flops 546045952 | bytes 6815744 | tf_op jit(solution)/shard_map/dot_general | solution.py:11
  137.5 32.8 %all-to-all-done.4 = bf16[8,48,4096]{2,1,0:T(8,128)(2,1)S(1)} async-done(((bf16[8,48,4096]{2,1,0:T(8,128)(2,1)}), bf16[8,48,4096]{2,1,0:T(8,128)(2,1)S(1)}, u32[]{:S(2)}, u32[]{:S(2)}) %all-to-all-start.4) | async-done | bytes 3145760 | tf_op jit(solution)/shard_map/all_to_all | solution.py:67
  170.3 3.6 %fusion.2 = f32[1,128,4096]{2,1,0:T(8,128)} fusion(f32[128,4096]{1,0:T(8,128)} %convolution_multiply_fusion.2, bf16[384,4096]{1,0:T(8,128)(2,1)S(1)} %bitcast.84, s32[384]{0:T(512)S(1)} %eq.79), kind=kOutput, calls=%fused_computation.7 | convolution fusion | flops 403226624 | bytes 7341568 | tf_op jit(solution)/shard_map/dot_general | solution.py:11
  174.0 22.9 %reduce-scatter.5.cloned.1.call-done = bf16[64,4096]{1,0:T(8,128)(2,1)} async-done(((bf16[256,4096]{1,0:T(8,128)(2,1)}), bf16[64,4096]{1,0:T(8,128)(2,1)}) %reduce-scatter.5.cloned.1.call-update) | async-done | bytes 524304 | tf_op jit(solution)/shard_map/reduce_scatter | solution.py:98
  196.9 2.7 %maximum_convert_fusion = f32[1,128,4096]{2,1,0:T(8,128)} fusion(bf16[1,64,4096]{2,1,0:T(8,128)(2,1)} %bitcast.87, bf16[1,64,4096]{2,1,0:T(8,128)(2,1)} %bitcast.86), kind=kLoop, calls=%fused_computation.16 | loop fusion | flops 2097152 | bytes 3145728 | tf_op jit(solution)/shard_map/convert_element_type | solution.py:105
  (33 shorter events, 0.3 us)
Async XLA Ops:
  7.2 3.0 %copy-start.2 = (s32[1,128,3]{1,0,2:T(1,128)S(1)}, s32[1,128,3]{1,0,2:T(1,128)}, u32[]{:S(2)}) copy-start(s32[1,128,3]{1,0,2:T(1,128)} %param.5) | copy-start | bytes 4612
  7.2 11.7 %copy-start = (f32[1,128,4096]{2,1,0:T(8,128)S(1)}, f32[1,128,4096]{2,1,0:T(8,128)}, u32[]{:S(2)}) copy-start(f32[1,128,4096]{2,1,0:T(8,128)} %param.4) | copy-start | bytes 6291460
  7.2 64.0 %all-gather.5.cloned.1.call-start = ((), (), s32[]{:S(2)}) async-start(), calls=%async_computation.9 | async-start | bytes 2621440 | tf_op jit(solution)/shard_map/all_gather | solution.py:34
  11.6 14.5 %all-to-all-start = ((s32[32,1,108]{2,1,0:T(1,128)}), s32[32,1,108]{2,1,0:T(1,128)S(1)}, u32[]{:S(2)}, u32[]{:S(2)}) async-start(s32[32,1,108]{2,1,0:T(1,128)} %bitcast.4), calls=%async_computation | async-start | bytes 32768 | tf_op jit(solution)/shard_map/all_to_all | solution.py:56
  28.9 42.3 %all-to-all-start.1 = ((bf16[8,48,4096]{2,1,0:T(8,128)(2,1)}), bf16[8,48,4096]{2,1,0:T(8,128)(2,1)}, u32[]{:S(2)}, u32[]{:S(2)}) async-start(bf16[8,48,4096]{2,1,0:T(8,128)(2,1)} %bitcast.9), calls=%async_computation.1 | async-start | bytes 6291456 | tf_op jit(solution)/shard_map/all_to_all | solution.py:67
  33.3 72.6 %all-gather.7.cloned.1.call-start = ((), (), s32[]{:S(2)}) async-start(), calls=%async_computation.10 | async-start | bytes 2621440 | tf_op jit(solution)/shard_map/all_gather | solution.py:34
  34.1 139.9 %reduce-scatter.3.cloned.1.call-start = ((), (), s32[]{:S(2)}) async-start(), calls=%async_computation.7 | async-start | bytes 2621440 | tf_op jit(solution)/shard_map/reduce_scatter | solution.py:98
  88.2 108.8 %reduce-scatter.5.cloned.1.call-start = ((), (), s32[]{:S(2)}) async-start(), calls=%async_computation.8 | async-start | bytes 2621440 | tf_op jit(solution)/shard_map/reduce_scatter | solution.py:98
  118.4 10.4 %copy-start.1 = (bf16[256,512]{0,1:T(8,128)(2,1)}, bf16[256,512]{0,1:T(8,128)(2,1)S(1)}, u32[]{:S(2)}) copy-start(bf16[256,512]{0,1:T(8,128)(2,1)S(1)} %subtract_convert_fusion) | copy-start | bytes 786436
  128.7 41.6 %all-to-all-start.4 = ((bf16[8,48,4096]{2,1,0:T(8,128)(2,1)}), bf16[8,48,4096]{2,1,0:T(8,128)(2,1)S(1)}, u32[]{:S(2)}, u32[]{:S(2)}) async-start(bf16[8,48,4096]{2,1,0:T(8,128)(2,1)} %bitcast.85), calls=%async_computation.6 | async-start | bytes 6291456 | tf_op jit(solution)/shard_map/all_to_all | solution.py:67
Sparse Core Ops, SparseCore 0:
  10.3 48.6 all-gather.4
  61.1 44.7 all-gather.6
  108.2 42.6 reduce-scatter.2
  153.7 43.1 reduce-scatter.4

commit v3 on v2

--- a/solution.py
+++ b/solution.py
@@ -4,7 +4,7 @@
 from jax.sharding import PartitionSpec as P
 
 inverse_temp = 50.0
-pieces = 2
+pieces = 1
 
 
 def matmul(a, b, left, right):

time: 207 us -> 200 us (0.966)
  blocking collectives: 16.4 us -> 7.96 us
  waiting for transfers between devices: 118 us -> 124 us
  matrix products: 33.2 us -> 28.4 us
    all_to_all x2 -> x1, blocking collectives: 16.4 us -> 7.96 us  [per_device(): stats = lax.all_to_all(stats, 'dp', split_axis=0, concat_axis=0, tiled=True)]
    all_gather x2 -> x1, waiting for transfers between devices: 17.7 us -> 22.6 us  [per_device(): gathered.append(lax.all_gather(piece, 'dp', axis=0, tiled=True))]
    dot_general x8 -> x6, matrix products: 33.2 us -> 28.4 us  [matmul(): lax.dot_general(a, b, (((left,), (right,)), ((), ())), preferred_element_...]
    convert_element_type x1 -> x0, other arithmetic: 2.73 us -> none  [per_device(): query_grad = jnp.concatenate(query_grad, axis=0).astype(jnp.float32)]
    broadcast_in_dim x1, other arithmetic: 0.59 us -> 2.76 us  [per_device(): return (query_grad[None], passage_grad[None], jnp.concatenate(losses)[None])]
    reduce_scatter x2 -> x1, waiting for transfers between devices: 23 us -> 24.2 us  [per_device(): lax.psum_scatter(share, 'dp', scatter_dimension=0, tiled=True)]
  transfers between devices with their start and end apart: 7 -> 5, of which waited for: 5 -> 5; matrix products, arithmetic and copies ran while one was open for 18% -> 10% of each run, Pallas kernels for 0% -> 0%
where the time goes in v3:
time: 200 us; the launch traced here: 199 us
  waiting for transfers between devices  124 us (62%)
  matrix products  28.4 us (14%)
  starting transfers between devices  15.6 us (8%)
  between operations  14.2 us (7%)
  blocking collectives  7.96 us (4%)
  other arithmetic  7.55 us (4%)
    all_to_all x2, waiting for transfers between devices, exchange(): lax.all_to_all(rows, 'group', split_axis=0, concat_axis=0, tiled=True)  70.4 us
    dot_general x6, matrix products, matmul(): lax.dot_general(a, b, (((left,), (right,)), ((), ())), preferred_element_...  28.4 us
    reduce_scatter x1, waiting for transfers between devices, per_device(): lax.psum_scatter(share, 'dp', scatter_dimension=0, tiled=True)  24.2 us
    all_gather x1, waiting for transfers between devices, per_device(): gathered.append(lax.all_gather(piece, 'dp', axis=0, tiled=True))  22.6 us
    all_to_all x2, starting transfers between devices, exchange(): lax.all_to_all(rows, 'group', split_axis=0, concat_axis=0, tiled=True)  8.18 us
    all_to_all x1, blocking collectives, per_device(): stats = lax.all_to_all(stats, 'dp', split_axis=0, concat_axis=0, tiled=True)  7.96 us
    all_to_all x1, starting transfers between devices, per_device(): lax.all_to_all(request, ('dp', 'group'), split_axis=0, concat_axis=0, til...  7.3 us
    all_to_all x1, waiting for transfers between devices, per_device(): lax.all_to_all(request, ('dp', 'group'), split_axis=0, concat_axis=0, til...  6.94 us
  transfers between devices with their start and end apart: 5, of which 5 were waited for; matrix products, arithmetic and copies ran while one was open for 10% of the time, Pallas kernels for 0%

profile of v3, /device:TPU:0, one launch (start us, length us, event | category | flops | bytes accessed | tf_op | source)
XLA Modules:
  0.0 199.2 jit_solution(13520282626200143320)
XLA Ops:
  7.2 0.0 copy-start.2
  7.2 0.0 copy-start
  7.2 0.0 all-gather.3.cloned.1.call-start
  7.2 2.8 %convert_element_type.36 = bf16[1,128,4096]{2,1,0:T(8,128)(2,1)} convert(f32[1,128,4096]{2,1,0:T(8,128)} %param.3) | non-fusion elementwise | flops 524288 | bytes 3145728 | tf_op jit(solution)/shard_map/convert_element_type | solution.py:28
  10.1 0.0 all-gather.3.cloned.1.call-update
  10.1 0.0 copy-done.2
  10.1 0.2 convert_reduce_fusion
  10.4 0.2 select_reduce_fusion.2
  10.6 0.1 sub.62
  10.7 0.1 sub.60
  10.8 0.7 pad_add_fusion
  11.5 7.3 %all-to-all-start = ((s32[32,1,108]{2,1,0:T(1,128)}), s32[32,1,108]{2,1,0:T(1,128)S(1)}, u32[]{:S(2)}, u32[]{:S(2)}) async-start(s32[32,1,108]{2,1,0:T(1,128)} %bitcast.4), calls=%async_computation | async-start | bytes 32768 | tf_op jit(solution)/shard_map/all_to_all | solution.py:56
  18.8 0.0 copy-done
  18.8 0.1 convert_bitcast_fusion
  19.0 6.9 %all-to-all-done = s32[32,1,108]{2,1,0:T(1,128)S(1)} async-done(((s32[32,1,108]{2,1,0:T(1,128)}), s32[32,1,108]{2,1,0:T(1,128)S(1)}, u32[]{:S(2)}, u32[]{:S(2)}) %all-to-all-start) | async-done | bytes 13856 | tf_op jit(solution)/shard_map/all_to_all | solution.py:56
  25.9 0.1 eq.68
  26.0 2.7 %convolution_convert_fusion = bf16[384,4096]{1,0:T(8,128)(2,1)} fusion(bf16[128,4096]{1,0:T(8,128)(2,1)S(1)} %convert_bitcast_fusion, s32[384]{0:T(512)S(1)} %eq.68), kind=kOutput, calls=%fused_computation.2 | convolution fusion | flops 404275200 | bytes 4195840 | tf_op jit(solution)/shard_map/dot_general | solution.py:11
  28.7 4.5 %all-to-all-start.1 = ((bf16[8,48,4096]{2,1,0:T(8,128)(2,1)}), bf16[8,48,4096]{2,1,0:T(8,128)(2,1)}, u32[]{:S(2)}, u32[]{:S(2)}) async-start(bf16[8,48,4096]{2,1,0:T(8,128)(2,1)} %bitcast.9), calls=%async_computation.1 | async-start | bytes 6291456 | tf_op jit(solution)/shard_map/all_to_all | solution.py:67
  33.2 0.0 reduce-scatter.2.cloned.1.call-start
  33.3 0.1 slice.25
  33.4 0.1 reshape.267
  33.5 0.1 reshape.268
  33.7 37.5 %all-to-all-done.1 = bf16[8,48,4096]{2,1,0:T(8,128)(2,1)} async-done(((bf16[8,48,4096]{2,1,0:T(8,128)(2,1)}), bf16[8,48,4096]{2,1,0:T(8,128)(2,1)}, u32[]{:S(2)}, u32[]{:S(2)}) %all-to-all-start.1) | async-done | bytes 3145760 | tf_op jit(solution)/shard_map/all_to_all | solution.py:67
  71.1 22.6 %all-gather.3.cloned.1.call-done = bf16[1,512,4096]{2,1,0:T(8,128)(2,1)} async-done(((bf16[1,128,4096]{2,1,0:T(8,128)(2,1)}), bf16[1,512,4096]{2,1,0:T(8,128)(2,1)}) %all-gather.3.cloned.1.call-update) | async-done | bytes 4194320 | tf_op jit(solution)/shard_map/all_gather | solution.py:34
  93.7 5.6 %fusion.46 = (f32[512]{0:T(512)S(1)}, f32[512,512]{0,1:T(8,128)S(1)}) fusion(bf16[1,512,4096]{2,1,0:T(8,128)(2,1)} %all-gather.3.cloned.1.call-done, bf16[384,4096]{1,0:T(8,128)(2,1)} %bitcast.10, bf16[128,4096]{1,0:T(8,128)(2,1)S(1)} %convert_bitcast_fusion, pred[512]{0:T(512)(128)(4,1)S(1)} %iota_compare_fusion.7, s32[512]{0:T(512)S(1)} %concatenate.17), kind=kOutput, calls=%fused_computation.96 | convolution fusion | flops 2157182464 | bytes 9441792 | tf_op jit(solution)/shard_map/dot_general | solution.py:11
  99.3 0.3 select_reduce_fusion
  99.6 8.0 %all_to_all.24 = f32[4,2,512]{2,1,0:T(2,128)S(1)} all-to-all(f32[4,2,512]{2,1,0:T(2,128)S(1)} %broadcast_in_dim.74), channel_id=1, replica_groups=mesh['dp'=4,'group'=8] {'dp'}, dimensions={0} | all-to-all | bytes 32768 | tf_op jit(solution)/shard_map/all_to_all | solution.py:90
  107.6 0.3 subtract_convert_fusion
  107.9 0.0 copy-start.1
  107.9 6.4 %multiply_convert_fusion = bf16[512,4096]{1,0:T(8,128)(2,1)} fusion(bf16[512,512]{0,1:T(8,128)(2,1)S(1)} %subtract_convert_fusion, bf16[384,4096]{1,0:T(8,128)(2,1)} %bitcast.10, bf16[128,4096]{1,0:T(8,128)(2,1)S(1)} %convert_bitcast_fusion), kind=kOutput, calls=%fused_computation | convolution fusion | flops 2160066560 | bytes 8912896 | tf_op jit(solution)/shard_map/dot_general | solution.py:11
  114.4 0.0 reduce-scatter.2.cloned.1.call-update
  114.4 0.0 copy-done.1
  114.4 5.7 %multiply_convert_fusion.1 = bf16[384,4096]{1,0:T(8,128)(2,1)} fusion(bf16[1,512,4096]{2,1,0:T(8,128)(2,1)} %all-gather.3.cloned.1.call-done, bf16[512,512]{0,1:T(8,128)(2,1)S(1)} %subtract_convert_fusion), kind=kOutput, calls=%fused_computation.1 | convolution fusion | flops 1613758464 | bytes 7733248 | tf_op jit(solution)/shard_map/dot_general | solution.py:11
  120.1 3.7 %all-to-all-start.3 = ((bf16[8,48,4096]{2,1,0:T(8,128)(2,1)}), bf16[8,48,4096]{2,1,0:T(8,128)(2,1)S(1)}, u32[]{:S(2)}, u32[]{:S(2)}) async-start(bf16[8,48,4096]{2,1,0:T(8,128)(2,1)} %bitcast.79), calls=%async_computation.4 | async-start | bytes 6291456 | tf_op jit(solution)/shard_map/all_to_all | solution.py:67
  123.8 0.6 dynamic-slice_bitcast_fusion
  124.4 4.3 %convolution_multiply_fusion = f32[128,4096]{1,0:T(8,128)} fusion(bf16[1,512,4096]{2,1,0:T(8,128)(2,1)} %all-gather.3.cloned.1.call-done, bf16[512,512]{0,1:T(8,128)(2,1)} %copy-done.1), kind=kOutput, calls=%fused_computation.5 | convolution fusion | flops 537395200 | bytes 6422528 | tf_op jit(solution)/shard_map/dot_general | solution.py:11
  128.7 33.0 %all-to-all-done.3 = bf16[8,48,4096]{2,1,0:T(8,128)(2,1)S(1)} async-done(((bf16[8,48,4096]{2,1,0:T(8,128)(2,1)}), bf16[8,48,4096]{2,1,0:T(8,128)(2,1)S(1)}, u32[]{:S(2)}, u32[]{:S(2)}) %all-to-all-start.3) | async-done | bytes 3145760 | tf_op jit(solution)/shard_map/all_to_all | solution.py:67
  161.7 3.6 %fusion = f32[1,128,4096]{2,1,0:T(8,128)} fusion(f32[128,4096]{1,0:T(8,128)} %convolution_multiply_fusion, bf16[384,4096]{1,0:T(8,128)(2,1)S(1)} %bitcast.78, s32[384]{0:T(512)S(1)} %eq.68), kind=kOutput, calls=%fused_computation.4 | convolution fusion | flops 403226624 | bytes 7341568 | tf_op jit(solution)/shard_map/dot_general | solution.py:11
  165.3 24.2 %reduce-scatter.2.cloned.1.call-done = bf16[128,4096]{1,0:T(8,128)(2,1)} async-done(((bf16[512,4096]{1,0:T(8,128)(2,1)}), bf16[128,4096]{1,0:T(8,128)(2,1)}) %reduce-scatter.2.cloned.1.call-update) | async-done | bytes 1048592 | tf_op jit(solution)/shard_map/reduce_scatter | solution.py:98
  189.6 2.8 %bitcast_convert_fusion = f32[1,128,4096]{2,1,0:T(8,128)} fusion(bf16[128,4096]{1,0:T(8,128)(2,1)} %reduce-scatter.2.cloned.1.call-done), kind=kLoop, calls=%fused_computation.14 | loop fusion | flops 524288 | bytes 3145728 | tf_op jit(solution)/shard_map/broadcast_in_dim | solution.py:106
  (19 shorter events, 0.2 us)
Async XLA Ops:
  7.2 2.9 %copy-start.2 = (s32[1,128,3]{1,0,2:T(1,128)S(1)}, s32[1,128,3]{1,0,2:T(1,128)}, u32[]{:S(2)}) copy-start(s32[1,128,3]{1,0,2:T(1,128)} %param.5) | copy-start | bytes 4612
  7.2 11.6 %copy-start = (f32[1,128,4096]{2,1,0:T(8,128)S(1)}, f32[1,128,4096]{2,1,0:T(8,128)}, u32[]{:S(2)}) copy-start(f32[1,128,4096]{2,1,0:T(8,128)} %param.4) | copy-start | bytes 6291460
  7.2 86.5 %all-gather.3.cloned.1.call-start = ((), (), s32[]{:S(2)}) async-start(), calls=%async_computation.6 | async-start | bytes 5242880 | tf_op jit(solution)/shard_map/all_gather | solution.py:34
  11.5 14.4 %all-to-all-start = ((s32[32,1,108]{2,1,0:T(1,128)}), s32[32,1,108]{2,1,0:T(1,128)S(1)}, u32[]{:S(2)}, u32[]{:S(2)}) async-start(s32[32,1,108]{2,1,0:T(1,128)} %bitcast.4), calls=%async_computation | async-start | bytes 32768 | tf_op jit(solution)/shard_map/all_to_all | solution.py:56
  28.7 42.4 %all-to-all-start.1 = ((bf16[8,48,4096]{2,1,0:T(8,128)(2,1)}), bf16[8,48,4096]{2,1,0:T(8,128)(2,1)}, u32[]{:S(2)}, u32[]{:S(2)}) async-start(bf16[8,48,4096]{2,1,0:T(8,128)(2,1)} %bitcast.9), calls=%async_computation.1 | async-start | bytes 6291456 | tf_op jit(solution)/shard_map/all_to_all | solution.py:67
  33.2 156.3 %reduce-scatter.2.cloned.1.call-start = ((), (), s32[]{:S(2)}) async-start(), calls=%async_computation.5 | async-start | bytes 5242880 | tf_op jit(solution)/shard_map/reduce_scatter | solution.py:98
  107.9 6.5 %copy-start.1 = (bf16[512,512]{0,1:T(8,128)(2,1)}, bf16[512,512]{0,1:T(8,128)(2,1)S(1)}, u32[]{:S(2)}) copy-start(bf16[512,512]{0,1:T(8,128)(2,1)S(1)} %subtract_convert_fusion) | copy-start | bytes 1572868
  120.1 41.6 %all-to-all-start.3 = ((bf16[8,48,4096]{2,1,0:T(8,128)(2,1)}), bf16[8,48,4096]{2,1,0:T(8,128)(2,1)S(1)}, u32[]{:S(2)}, u32[]{:S(2)}) async-start(bf16[8,48,4096]{2,1,0:T(8,128)(2,1)} %bitcast.79), calls=%async_computation.4 | async-start | bytes 6291456 | tf_op jit(solution)/shard_map/all_to_all | solution.py:67
Sparse Core Ops, SparseCore 0:
  10.2 83.4 all-gather.2
  114.5 75.0 reduce-scatter.1

commit v4 on v3

v4 whole, which is shorter than its diff:
```python
import jax
import jax.numpy as jnp
from jax import lax
from jax.sharding import PartitionSpec as P

inverse_temp = 50.0
direct_part = 4


def ways(step, count):
    return [(i, i + 1) for i in range(step - 1, count - 1)], [(i + 1, i) for i in range(count - step)]


def scatter_begin(share, me, count):
    rows = share.shape[0] // count

    def part(index):
        return lax.dynamic_slice_in_dim(share, index * rows, rows, axis=0)

    terms = [part(me)]
    up, down = None, None
    for step in range(max(count - 2, 1), 0, -1):
        low, high = part((me - step) % count), part((me + step) % count)
        if up is not None:
            low = low.astype(jnp.float32), down
            high = high.astype(jnp.float32), up
        if step > 1:
            above, below = ways(step, count)
            if up is not None:
                low, high = (added(*x) for x in (low, high))
            down = lax.ppermute(low, "dp", [(j, i) for i, j in above])
            up = lax.ppermute(high, "dp", [(j, i) for i, j in below])
    if count > 2:
        terms.append(lax.ppermute(part(count - 1 - me), "dp", [(0, count - 1), (count - 1, 0)]))
    return terms, low, high


def added(kept, came):
    return (kept + came.astype(jnp.float32)).astype(jnp.bfloat16)


def scatter_end(terms, low, high, count):
    low, high = (added(*x) if isinstance(x, tuple) else x for x in (low, high))
    above, below = ways(1, count)
    down = lax.ppermute(low, "dp", [(j, i) for i, j in above])
    up = lax.ppermute(high, "dp", [(j, i) for i, j in below])
    return sum(term.astype(jnp.float32) for term in terms + [up, down])


def matmul(a, b, left, right):
    return lax.dot_general(a, b, (((left,), (right,)), ((), ())), preferred_element_type=jnp.float32)


def per_device(queries, passages, hard_ids):
    row_count, features = queries.shape[1:]
    hard = hard_ids.shape[2]
    dp_count = lax.axis_size("dp")
    group_count = lax.axis_size("group")
    devices = dp_count * group_count
    me = lax.axis_index("dp")
    my_group = lax.axis_index("group")
    batch_rows = row_count * dp_count
    entries = row_count * hard
    capacity = (entries + devices - 1) // devices
    slots = devices * capacity

    query_low = queries[0].astype(jnp.bfloat16)
    passage_low = passages[0].astype(jnp.bfloat16)

    everything = lax.all_gather(query_low, "dp", axis=0, tiled=True)

    ids = hard_ids[0].T.reshape(entries)
    owner_group = ids // batch_rows
    owner_dp = ids % batch_rows // row_count
    owner = owner_dp * group_count + owner_group
    order = jnp.arange(entries)
    earlier = (order[None, :] < order[:, None]) & (owner[None, :] == owner[:, None])
    rank = jnp.sum(earlier.astype(jnp.int32), axis=1)
    slot = owner * capacity + rank
    placed = jnp.arange(slots)[:, None] == slot[None, :]
    query_row = jnp.sum(jnp.where(placed, order[None, :] % row_count + 1, 0), axis=1) - 1
    passage_row = jnp.sum(jnp.where(placed, ids[None, :] % row_count + 1, 0), axis=1) - 1

    plane = group_count * capacity
    request = jnp.concatenate(
        [
            passage_row.reshape(dp_count, group_count, capacity),
            jnp.broadcast_to(query_row.reshape(dp_count, 1, plane), (dp_count, group_count, plane)),
        ],
        axis=2,
    ).reshape(devices, capacity + plane)
    request = lax.all_to_all(request, ("dp", "group"), split_axis=0, concat_axis=0, tiled=True)
    request = request.reshape(dp_count, group_count, capacity + plane)
    sent_row = request[:, :, :capacity].transpose(1, 0, 2).reshape(slots)
    wanting = lax.dynamic_index_in_dim(request[:, :, capacity:], my_group, axis=1, keepdims=False)
    wanting = wanting.reshape(dp_count, group_count, capacity).transpose(1, 0, 2).reshape(slots)
    wanting_dp = jnp.arange(slots) // capacity % dp_count

    select = (jnp.arange(row_count)[:, None] == sent_row[None, :]).astype(jnp.bfloat16)

    def exchange(rows):
        rows = rows.astype(jnp.bfloat16).reshape(group_count, dp_count * capacity, features)
        return lax.all_to_all(rows, "group", split_axis=0, concat_axis=0, tiled=True).reshape(slots, features)

    table = jnp.concatenate([passage_low, exchange(matmul(select, passage_low, 0, 0))], axis=0)

    row = jnp.arange(batch_rows)[:, None]
    target = jnp.where(wanting >= 0, wanting_dp * row_count + wanting, -1)
    positive = me * row_count + jnp.arange(row_count)
    positive = row == jnp.pad(positive, (0, slots), constant_values=-1)[None, :]
    masked = row != jnp.pad(target, (row_count, 0))[None, :]
    masked = masked & (jnp.arange(row_count + slots)[None, :] >= row_count)
    scores = jnp.where(masked, -jnp.inf, matmul(everything, lax.optimization_barrier(table.T), 1, 0) * inverse_temp)
    highest = jnp.max(scores, axis=1)
    total = jnp.sum(jnp.exp(scores - highest[:, None]), axis=1)
    stats = jnp.broadcast_to(jnp.stack([highest, total])[None], (dp_count, 2, batch_rows))
    stats = lax.all_to_all(stats, "dp", split_axis=0, concat_axis=0, tiled=True)
    highest = jnp.max(stats[:, 0], axis=0)
    normal = highest + jnp.log(jnp.sum(stats[:, 1] * jnp.exp(stats[:, 0] - highest[None, :]), axis=0))
    losses = normal - jnp.sum(jnp.where(positive, scores, 0.0), axis=1)
    losses = lax.dynamic_slice_in_dim(losses, me * row_count, row_count, axis=0)
    weights = jnp.exp(scores - normal[:, None]) - positive.astype(jnp.float32)
    weights = weights.astype(jnp.bfloat16)

    direct = features // direct_part
    share = (matmul(weights, table[:, direct:], 1, 0) * inverse_temp).astype(jnp.bfloat16)
    later = lax.psum_scatter(share, "dp", scatter_dimension=0, tiled=True)
    weights, share = lax.optimization_barrier((weights, share))
    ahead = (matmul(weights, table[:, :direct], 1, 0) * inverse_temp).astype(jnp.bfloat16)
    ahead = scatter_end(*scatter_begin(ahead, me, dp_count), dp_count)

    passage_grad = matmul(weights[:, :row_count], everything, 0, 0)
    hard_grad = matmul(weights[:, row_count:], everything, 0, 0) * inverse_temp
    passage_grad = passage_grad * inverse_temp + matmul(select, exchange(hard_grad), 1, 0)
    query_grad = jnp.pad(ahead, ((0, 0), (0, features - direct)))
    query_grad, later, passage_grad = lax.optimization_barrier((query_grad, later, passage_grad))
    query_grad = lax.dynamic_update_slice(query_grad, later.astype(jnp.float32), (0, direct))
    return (query_grad[None], passage_grad[None], losses[None])


def solution(mesh):
    return jax.shard_map(
        per_device,
        mesh=mesh,
        in_specs=(P("group", "dp", None), P("group", "dp", None), P("group", "dp", None)),
        out_specs=(P("group", "dp", None), P("group", "dp", None), P("group", "dp")),
        check_vma=False,
    )
```

time: 200 us -> 198 us (0.990)
  waiting for transfers between devices: 124 us -> 86.9 us
  starting transfers between devices: 15.6 us -> 39.8 us
  other arithmetic: 7.55 us -> 13.9 us
  local copies, waits for them, and re-layouts: 1.23 us -> 6.42 us
    all_to_all x2, waiting for transfers between devices: 70.4 us -> 37.4 us  [exchange(): lax.all_to_all(rows, 'group', split_axis=0, concat_axis=0, tiled=True)]
    ppermute x0 -> x5, starting transfers between devices: none -> 25.1 us  [the longest x1 15.9 us: scatter_end(): up = lax.ppermute(high, 'dp', [(j, i) for i, j in below])]
    reduce_scatter x1, waiting for transfers between devices: 24.2 us -> 3.7 us  [per_device(): later = lax.psum_scatter(share, 'dp', scatter_dimension=0, tiled=True)]
    ppermute x0 -> x5, waiting for transfers between devices: none -> 19.6 us  [the longest x1 7.9 us: scatter_begin(): up = lax.ppermute(high, 'dp', [(j, i) for i, j in below])]
    transpose x0 -> x1, other arithmetic: none -> 4.25 us  [per_device(): scores = jnp.where(masked, -jnp.inf, matmul(everything, lax.optimization_...]
    all_gather x1, waiting for transfers between devices: 22.6 us -> 19.2 us  [per_device(): everything = lax.all_gather(query_low, 'dp', axis=0, tiled=True)]
    unnamed x6 -> x16, local copies, waits for them, and re-layouts: 0.01 us -> 2.8 us
    broadcast_in_dim x1 -> x0, other arithmetic: 2.76 us -> none  [per_device(): return (query_grad[None], passage_grad[None], jnp.concatenate(losses)[None])]
  transfers between devices with their start and end apart: 5 -> 10, of which waited for: 5 -> 7; matrix products, arithmetic and copies ran while one was open for 10% -> 15% of each run, Pallas kernels for 0% -> 0%
where the time goes in v4:
time: 198 us; the launch traced here: 197 us
  waiting for transfers between devices  86.9 us (44%)
  starting transfers between devices  39.8 us (20%)
  matrix products  27.7 us (14%)
  between operations  14.3 us (7%)
  other arithmetic  13.9 us (7%)
  blocking collectives  7.96 us (4%)
  local copies, waits for them, and re-layouts  6.42 us (3%)
    all_to_all x2, waiting for transfers between devices, exchange(): lax.all_to_all(rows, 'group', split_axis=0, concat_axis=0, tiled=True)  37.4 us
    dot_general x7, matrix products, matmul(): lax.dot_general(a, b, (((left,), (right,)), ((), ())), preferred_element_...  27.7 us
    all_gather x1, waiting for transfers between devices, per_device(): everything = lax.all_gather(query_low, 'dp', axis=0, tiled=True)  19.2 us
    ppermute x1, starting transfers between devices, scatter_end(): up = lax.ppermute(high, 'dp', [(j, i) for i, j in below])  15.9 us
    all_to_all x1, blocking collectives, per_device(): stats = lax.all_to_all(stats, 'dp', split_axis=0, concat_axis=0, tiled=True)  7.96 us
    ppermute x1, waiting for transfers between devices, scatter_begin(): up = lax.ppermute(high, 'dp', [(j, i) for i, j in below])  7.9 us
    all_to_all x2, starting transfers between devices, exchange(): lax.all_to_all(rows, 'group', split_axis=0, concat_axis=0, tiled=True)  7.34 us
    all_to_all x1, starting transfers between devices, per_device(): lax.all_to_all(request, ('dp', 'group'), split_axis=0, concat_axis=0, til...  7.3 us
  transfers between devices with their start and end apart: 10, of which 7 were waited for; matrix products, arithmetic and copies ran while one was open for 15% of the time, Pallas kernels for 0%

profile of v4, /device:TPU:0, one launch (start us, length us, event | category | flops | bytes accessed | tf_op | source)
XLA Modules:
  0.0 197.0 jit_solution(4634575079659319445)
XLA Ops:
  7.2 0.0 all-gather.3.cloned.1.call-start
  7.2 2.8 %convert_element_type.71 = bf16[1,128,4096]{2,1,0:T(8,128)(2,1)} convert(f32[1,128,4096]{2,1,0:T(8,128)} %param.3) | non-fusion elementwise | flops 524288 | bytes 3145728 | tf_op jit(solution)/shard_map/convert_element_type | solution.py:67
  10.1 0.2 convert_reduce_fusion
  10.4 0.2 select_reduce_fusion.2
  10.6 0.1 sub.68
  10.7 0.1 sub.66
  10.8 0.7 pad_add_fusion
  11.5 7.3 %all-to-all-start = ((s32[32,1,108]{2,1,0:T(1,128)}), s32[32,1,108]{2,1,0:T(1,128)S(1)}, u32[]{:S(2)}, u32[]{:S(2)}) async-start(s32[32,1,108]{2,1,0:T(1,128)} %bitcast.4), calls=%async_computation | async-start | bytes 32768 | tf_op jit(solution)/shard_map/all_to_all | solution.py:92
  18.8 0.1 convert_bitcast_fusion
  19.0 7.0 %all-to-all-done = s32[32,1,108]{2,1,0:T(1,128)S(1)} async-done(((s32[32,1,108]{2,1,0:T(1,128)}), s32[32,1,108]{2,1,0:T(1,128)S(1)}, u32[]{:S(2)}, u32[]{:S(2)}) %all-to-all-start) | async-done | bytes 13856 | tf_op jit(solution)/shard_map/all_to_all | solution.py:92
  26.0 0.1 eq.73
  26.1 2.7 %convolution_convert_fusion = bf16[384,4096]{1,0:T(8,128)(2,1)} fusion(bf16[128,4096]{1,0:T(8,128)(2,1)S(1)} %convert_bitcast_fusion, s32[384]{0:T(512)S(1)} %eq.73), kind=kOutput, calls=%fused_computation.5 | convolution fusion | flops 404275200 | bytes 4195840 | tf_op jit(solution)/shard_map/dot_general | solution.py:51
  28.8 3.6 %all-to-all-start.1 = ((bf16[8,48,4096]{2,1,0:T(8,128)(2,1)}), bf16[8,48,4096]{2,1,0:T(8,128)(2,1)S(1)}, u32[]{:S(2)}, u32[]{:S(2)}) async-start(bf16[8,48,4096]{2,1,0:T(8,128)(2,1)} %bitcast.9), calls=%async_computation.1 | async-start | bytes 6291456 | tf_op jit(solution)/shard_map/all_to_all | solution.py:103
  32.5 0.0 reduce-scatter.2.cloned.1.call-start
  32.6 0.1 slice.33
  32.7 0.1 reshape.270
  32.7 0.1 reshape.271
  32.9 37.4 %all-to-all-done.1 = bf16[8,48,4096]{2,1,0:T(8,128)(2,1)S(1)} async-done(((bf16[8,48,4096]{2,1,0:T(8,128)(2,1)}), bf16[8,48,4096]{2,1,0:T(8,128)(2,1)S(1)}, u32[]{:S(2)}, u32[]{:S(2)}) %all-to-all-start.1) | async-done | bytes 3145760 | tf_op jit(solution)/shard_map/all_to_all | solution.py:103
  70.3 4.2 %fusion = bf16[4096,512]{0,1:T(8,128)(2,1)} fusion(bf16[384,4096]{1,0:T(8,128)(2,1)S(1)} %bitcast.83, bf16[128,4096]{1,0:T(8,128)(2,1)} %copy-done.1), kind=kLoop, calls=%fused_computation.10 | loop fusion | flops 8388608 | bytes 8388608 | tf_op jit(solution)/shard_map/transpose | solution.py:113
  74.5 19.2 %all-gather.3.cloned.1.call-done = bf16[1,512,4096]{2,1,0:T(8,128)(2,1)} async-done(((bf16[1,128,4096]{2,1,0:T(8,128)(2,1)}), bf16[1,512,4096]{2,1,0:T(8,128)(2,1)}) %all-gather.3.cloned.1.call-update) | async-done | bytes 4194320 | tf_op jit(solution)/shard_map/all_gather | solution.py:70
  93.7 6.0 %fusion.50 = (f32[512]{0:T(512)S(1)}, f32[512,512]{0,1:T(8,128)S(1)}) fusion(bf16[4096,512]{0,1:T(8,128)(2,1)} %fusion, bf16[1,512,4096]{2,1,0:T(8,128)(2,1)} %all-gather.3.cloned.1.call-done, pred[512]{0:T(512)(128)(4,1)S(1)} %iota_compare_fusion.7, s32[512]{0:T(512)S(1)} %pad.12), kind=kOutput, calls=%fused_computation.109 | convolution fusion | flops 2148793856 | bytes 9441792 | tf_op jit(solution)/shard_map/dot_general | solution.py:51
  99.7 0.3 select_reduce_fusion
  100.0 8.0 %all_to_all.24 = f32[4,2,512]{2,1,0:T(2,128)S(1)} all-to-all(f32[4,2,512]{2,1,0:T(2,128)S(1)} %broadcast_in_dim.72), channel_id=1, replica_groups=mesh['dp'=4,'group'=8] {'dp'}, dimensions={0} | all-to-all | bytes 32768 | tf_op jit(solution)/shard_map/all_to_all | solution.py:117
  108.0 0.3 subtract_convert_fusion
  108.3 0.8 copy-done.5
  109.1 3.2 %multiply_convert_fusion.1 = bf16[512,3072]{1,0:T(8,128)(2,1)} fusion(bf16[512,512]{0,1:T(8,128)(2,1)S(1)} %subtract_convert_fusion, bf16[384,4096]{1,0:T(8,128)(2,1)S(1)} %bitcast.84, bf16[128,4096]{1,0:T(8,128)(2,1)S(1)} %copy-done.2), kind=kOutput, calls=%fused_computation.4 | convolution fusion | flops 1620049920 | bytes 7864320 | tf_op jit(solution)/shard_map/dot_general | solution.py:51
  112.4 1.0 copy-done.6
  113.4 5.7 %multiply_convert_fusion = bf16[384,4096]{1,0:T(8,128)(2,1)} fusion(bf16[1,512,4096]{2,1,0:T(8,128)(2,1)} %all-gather.3.cloned.1.call-done, bf16[512,512]{0,1:T(8,128)(2,1)S(1)} %copy-done.6), kind=kOutput, calls=%fused_computation.3 | convolution fusion | flops 1613758464 | bytes 7733248 | tf_op jit(solution)/shard_map/dot_general | solution.py:51
  119.1 3.7 %all-to-all-start.3 = ((bf16[8,48,4096]{2,1,0:T(8,128)(2,1)}), bf16[8,48,4096]{2,1,0:T(8,128)(2,1)S(1)}, u32[]{:S(2)}, u32[]{:S(2)}) async-start(bf16[8,48,4096]{2,1,0:T(8,128)(2,1)} %bitcast.86), calls=%async_computation.4 | async-start | bytes 6291456 | tf_op jit(solution)/shard_map/all_to_all | solution.py:103
  122.8 2.1 %multiply_convert_fusion.2 = bf16[512,1024]{1,0:T(8,128)(2,1)S(1)} fusion(bf16[512,512]{0,1:T(8,128)(2,1)} %copy-done.5, bf16[384,4096]{1,0:T(8,128)(2,1)} %bitcast.85, bf16[128,4096]{1,0:T(8,128)(2,1)} %copy-done.1), kind=kOutput, calls=%fused_computation.16 | convolution fusion | flops 540016640 | bytes 5767168 | tf_op jit(solution)/shard_map/dot_general | solution.py:51
  124.9 1.0 copy-done.3
  125.9 0.8 constant_dynamic-slice_fusion.2
  126.7 1.4 collective-permute-start.3
  128.1 3.2 %collective-permute-start.1 = (bf16[128,1024]{1,0:T(8,128)(2,1)}, bf16[128,1024]{1,0:T(8,128)(2,1)}, u32[]{:S(2)}, u32[]{:S(2)}) collective-permute-start(bf16[128,1024]{1,0:T(8,128)(2,1)} %get-tuple-element.19), channel_id=1, source_target_pairs={{0,8},{8,16},{1,9},{9,17},{2,10},{10,18},{3,11},{11,19},{4,12},{12... | collective-permute-start | bytes 786440 | tf_op jit(solution)/shard_map/ppermute | solution.py:32
  131.2 3.4 %collective-permute-start = (bf16[128,1024]{1,0:T(8,128)(2,1)S(1)}, bf16[128,1024]{1,0:T(8,128)(2,1)S(1)}, u32[]{:S(2)}, u32[]{:S(2)}) collective-permute-start(bf16[128,1024]{1,0:T(8,128)(2,1)S(1)} %get-tuple-element.17), channel_id=1, source_target_pairs={{0,24},{24,0},{1,25},{25,1},{2,26},{26,2},{3,27},{27,3},{4,28},{28... | collective-permute-start | bytes 786440 | tf_op jit(solution)/shard_map/ppermute | solution.py:34
  134.6 0.6 dynamic-slice_bitcast_fusion
  135.2 7.9 %collective-permute-done.1 = bf16[128,1024]{1,0:T(8,128)(2,1)} collective-permute-done((bf16[128,1024]{1,0:T(8,128)(2,1)}, bf16[128,1024]{1,0:T(8,128)(2,1)}, u32[]{:S(2)}, u32[]{:S(2)}) %collective-permute-start.1) | collective-permute-done | bytes 262176 | tf_op jit(solution)/shard_map/ppermute | solution.py:32
  143.1 1.4 add_convert_fusion.1
  144.5 15.9 %collective-permute-start.2 = (bf16[128,1024]{1,0:T(8,128)(2,1)S(1)}, bf16[128,1024]{1,0:T(8,128)(2,1)S(1)}, u32[]{:S(2)}, u32[]{:S(2)}) collective-permute-start(bf16[128,1024]{1,0:T(8,128)(2,1)S(1)} %get-tuple-element.20), channel_id=1, source_target_pairs={{0,8},{8,16},{16,24},{1,9},{9,17},{17,25},{2,10},{10,18},{18,26},{... | collective-permute-start | bytes 786440 | tf_op jit(solution)/shard_map/ppermute | solution.py:46
  160.4 1.3 collective-permute-start.4
  161.7 4.3 %convolution_multiply_fusion = f32[128,4096]{1,0:T(8,128)} fusion(bf16[1,512,4096]{2,1,0:T(8,128)(2,1)} %all-gather.3.cloned.1.call-done, bf16[512,512]{0,1:T(8,128)(2,1)} %copy-done.5), kind=kOutput, calls=%fused_computation.7 | convolution fusion | flops 537395200 | bytes 6422528 | tf_op jit(solution)/shard_map/dot_general | solution.py:51
  166.0 6.3 %collective-permute-done.2 = bf16[128,1024]{1,0:T(8,128)(2,1)S(1)} collective-permute-done((bf16[128,1024]{1,0:T(8,128)(2,1)S(1)}, bf16[128,1024]{1,0:T(8,128)(2,1)S(1)}, u32[]{:S(2)}, u32[]{:S(2)}) %collective-permute-start.2) | collective-permute-done | bytes 262176 | tf_op jit(solution)/shard_map/ppermute | solution.py:46
  172.3 5.5 %collective-permute-done.4 = bf16[128,1024]{1,0:T(8,128)(2,1)S(1)} collective-permute-done((bf16[128,1024]{1,0:T(8,128)(2,1)S(1)}, bf16[128,1024]{1,0:T(8,128)(2,1)S(1)}, u32[]{:S(2)}, u32[]{:S(2)}) %collective-permute-start.4) | collective-permute-done | bytes 262176 | tf_op jit(solution)/shard_map/ppermute | solution.py:45
  177.8 1.1 convert_add_fusion
  178.9 1.6 pad.14
  180.4 3.6 %convolution_add_fusion = f32[128,4096]{1,0:T(8,128)} fusion(f32[128,4096]{1,0:T(8,128)} %convolution_multiply_fusion, bf16[384,4096]{1,0:T(8,128)(2,1)S(1)} %bitcast.82, s32[384]{0:T(512)S(1)} %eq.73), kind=kOutput, calls=%fused_computation.6 | convolution fusion | flops 403226624 | bytes 7341568 | tf_op jit(solution)/shard_map/dot_general | solution.py:51
  184.1 3.7 %reduce-scatter.2.cloned.1.call-done = bf16[128,3072]{1,0:T(8,128)(2,1)} async-done(((bf16[512,3072]{1,0:T(8,128)(2,1)}), bf16[128,3072]{1,0:T(8,128)(2,1)}) %reduce-scatter.2.cloned.1.call-update) | async-done | bytes 786448 | tf_op jit(solution)/shard_map/reduce_scatter | solution.py:127
  187.8 2.4 %convert_dynamic-update-slice_fusion = f32[1,128,4096]{2,1,0:T(8,128)} fusion(f32[1,128,4096]{2,1,0:T(8,128)} %bitcast.87, bf16[128,3072]{1,0:T(8,128)(2,1)} %reduce-scatter.2.cloned.1.call-done), kind=kLoop, calls=%fused_computation.17 | loop fusion | flops 393216 | bytes 2359296 | tf_op jit(solution)/shard_map/dynamic_update_slice | solution.py:137
  (37 shorter events, 0.3 us)
Async XLA Ops:
  7.2 2.9 %copy-start.7 = (s32[1,128,3]{1,0,2:T(1,128)S(1)}, s32[1,128,3]{1,0,2:T(1,128)}, u32[]{:S(2)}) copy-start(s32[1,128,3]{1,0,2:T(1,128)} %param.5) | copy-start | bytes 4612
  7.2 11.6 %copy-start.4 = (f32[1,128,4096]{2,1,0:T(8,128)S(1)}, f32[1,128,4096]{2,1,0:T(8,128)}, u32[]{:S(2)}) copy-start(f32[1,128,4096]{2,1,0:T(8,128)} %param.4) | copy-start | bytes 6291460
  7.2 86.5 %all-gather.3.cloned.1.call-start = ((), (), s32[]{:S(2)}) async-start(), calls=%async_computation.6 | async-start | bytes 5242880 | tf_op jit(solution)/shard_map/all_gather | solution.py:70
  11.5 14.5 %all-to-all-start = ((s32[32,1,108]{2,1,0:T(1,128)}), s32[32,1,108]{2,1,0:T(1,128)S(1)}, u32[]{:S(2)}, u32[]{:S(2)}) async-start(s32[32,1,108]{2,1,0:T(1,128)} %bitcast.4), calls=%async_computation | async-start | bytes 32768 | tf_op jit(solution)/shard_map/all_to_all | solution.py:92
  18.9 9.9 %copy-start.1 = (bf16[128,4096]{1,0:T(8,128)(2,1)}, bf16[128,4096]{1,0:T(8,128)(2,1)S(1)}, u32[]{:S(2)}) copy-start(bf16[128,4096]{1,0:T(8,128)(2,1)S(1)} %convert_bitcast_fusion) | copy-start | bytes 3145732
  28.8 41.5 %all-to-all-start.1 = ((bf16[8,48,4096]{2,1,0:T(8,128)(2,1)}), bf16[8,48,4096]{2,1,0:T(8,128)(2,1)S(1)}, u32[]{:S(2)}, u32[]{:S(2)}) async-start(bf16[8,48,4096]{2,1,0:T(8,128)(2,1)} %bitcast.9), calls=%async_computation.1 | async-start | bytes 6291456 | tf_op jit(solution)/shard_map/all_to_all | solution.py:103
  32.5 155.3 %reduce-scatter.2.cloned.1.call-start = ((), (), s32[]{:S(2)}) async-start(), calls=%async_computation.5 | async-start | bytes 3932160 | tf_op jit(solution)/shard_map/reduce_scatter | solution.py:127
  70.3 38.0 %copy-start = (bf16[8,48,4096]{2,1,0:T(8,128)(2,1)}, bf16[8,48,4096]{2,1,0:T(8,128)(2,1)S(1)}, u32[]{:S(2)}) copy-start(bf16[8,48,4096]{2,1,0:T(8,128)(2,1)S(1)} %all-to-all-done.1) | copy-start | bytes 9437188
  93.7 15.4 %copy-start.2 = (bf16[128,4096]{1,0:T(8,128)(2,1)S(1)}, bf16[128,4096]{1,0:T(8,128)(2,1)}, u32[]{:S(2)}) copy-start(bf16[128,4096]{1,0:T(8,128)(2,1)} %copy-done.1) | copy-start | bytes 3145732
  108.3 0.8 copy-start.5
  112.4 1.0 copy-start.6
  119.1 61.3 %all-to-all-start.3 = ((bf16[8,48,4096]{2,1,0:T(8,128)(2,1)}), bf16[8,48,4096]{2,1,0:T(8,128)(2,1)S(1)}, u32[]{:S(2)}, u32[]{:S(2)}) async-start(bf16[8,48,4096]{2,1,0:T(8,128)(2,1)} %bitcast.86), calls=%async_computation.4 | async-start | bytes 6291456 | tf_op jit(solution)/shard_map/all_to_all | solution.py:103
  124.9 1.0 copy-start.3
  126.7 8.5 %collective-permute-start.3 = (bf16[128,1024]{1,0:T(8,128)(2,1)}, bf16[128,1024]{1,0:T(8,128)(2,1)}, u32[]{:S(2)}, u32[]{:S(2)}) collective-permute-start(bf16[128,1024]{1,0:T(8,128)(2,1)} %get-tuple-element.18), channel_id=1, source_target_pairs={{16,8},{24,16},{17,9},{25,17},{18,10},{26,18},{19,11},{27,19},{20,... | collective-permute-start | bytes 786440 | tf_op jit(solution)/shard_map/ppermute | solution.py:31
  128.1 15.1 %collective-permute-start.1 = (bf16[128,1024]{1,0:T(8,128)(2,1)}, bf16[128,1024]{1,0:T(8,128)(2,1)}, u32[]{:S(2)}, u32[]{:S(2)}) collective-permute-start(bf16[128,1024]{1,0:T(8,128)(2,1)} %get-tuple-element.19), channel_id=1, source_target_pairs={{0,8},{8,16},{1,9},{9,17},{2,10},{10,18},{3,11},{11,19},{4,12},{12... | collective-permute-start | bytes 786440 | tf_op jit(solution)/shard_map/ppermute | solution.py:32
  131.2 34.8 %collective-permute-start = (bf16[128,1024]{1,0:T(8,128)(2,1)S(1)}, bf16[128,1024]{1,0:T(8,128)(2,1)S(1)}, u32[]{:S(2)}, u32[]{:S(2)}) collective-permute-start(bf16[128,1024]{1,0:T(8,128)(2,1)S(1)} %get-tuple-element.17), channel_id=1, source_target_pairs={{0,24},{24,0},{1,25},{25,1},{2,26},{26,2},{3,27},{27,3},{4,28},{28... | collective-permute-start | bytes 786440 | tf_op jit(solution)/shard_map/ppermute | solution.py:34
  144.5 27.8 %collective-permute-start.2 = (bf16[128,1024]{1,0:T(8,128)(2,1)S(1)}, bf16[128,1024]{1,0:T(8,128)(2,1)S(1)}, u32[]{:S(2)}, u32[]{:S(2)}) collective-permute-start(bf16[128,1024]{1,0:T(8,128)(2,1)S(1)} %get-tuple-element.20), channel_id=1, source_target_pairs={{0,8},{8,16},{16,24},{1,9},{9,17},{17,25},{2,10},{10,18},{18,26},{... | collective-permute-start | bytes 786440 | tf_op jit(solution)/shard_map/ppermute | solution.py:46
  160.4 17.4 %collective-permute-start.4 = (bf16[128,1024]{1,0:T(8,128)(2,1)S(1)}, bf16[128,1024]{1,0:T(8,128)(2,1)S(1)}, u32[]{:S(2)}, u32[]{:S(2)}) collective-permute-start(bf16[128,1024]{1,0:T(8,128)(2,1)S(1)} %get-tuple-element.21), channel_id=1, source_target_pairs={{8,0},{16,8},{24,16},{9,1},{17,9},{25,17},{10,2},{18,10},{26,18},{... | collective-permute-start | bytes 786440 | tf_op jit(solution)/shard_map/ppermute | solution.py:45
Sparse Core Ops, SparseCore 0:
  10.2 83.4 all-gather.2
  112.5 75.1 reduce-scatter.1

commit v5 on v4

--- a/solution.py
+++ b/solution.py
@@ -4,11 +4,23 @@
 from jax.sharding import PartitionSpec as P
 
 inverse_temp = 50.0
-direct_part = 4
+later_part = 8
 
 
 def ways(step, count):
     return [(i, i + 1) for i in range(step - 1, count - 1)], [(i + 1, i) for i in range(count - step)]
+
+
+def send_direct(block, count):
+    return [lax.ppermute(block, "dp", [(i, (i + step) % count) for i in range(count)]) for step in range(1, count)]
+
+
+def in_order(block, moved, me, count):
+    rows = block.shape[0]
+    whole = jnp.zeros((rows * count, block.shape[1]), block.dtype)
+    for step, x in enumerate([block] + moved):
+        whole = lax.dynamic_update_slice_in_dim(whole, x, (me - step) % count * rows, axis=0)
+    return whole
 
 
 def scatter_begin(share, me, count):
@@ -64,10 +76,15 @@
     capacity = (entries + devices - 1) // devices
     slots = devices * capacity
 
-    query_low = queries[0].astype(jnp.bfloat16)
+    ahead = row_count - row_count // later_part
+    query_ahead = queries[0, :ahead].astype(jnp.bfloat16)
+    query_later = queries[0, ahead:].astype(jnp.bfloat16)
     passage_low = passages[0].astype(jnp.bfloat16)
 
-    everything = lax.all_gather(query_low, "dp", axis=0, tiled=True)
+    piece_ahead = lax.all_gather(query_ahead, "dp", axis=0, tiled=True)
+    piece_later = in_order(query_later, send_direct(query_later, dp_count), me, dp_count)
+    gathered = [piece_ahead, piece_later]
+    starts = [(0, ahead), (ahead, row_count)]
 
     ids = hard_ids[0].T.reshape(entries)
     owner_group = ids // batch_rows
@@ -104,38 +121,49 @@
 
     table = jnp.concatenate([passage_low, exchange(matmul(select, passage_low, 0, 0))], axis=0)
 
-    row = jnp.arange(batch_rows)[:, None]
-    target = jnp.where(wanting >= 0, wanting_dp * row_count + wanting, -1)
-    positive = me * row_count + jnp.arange(row_count)
-    positive = row == jnp.pad(positive, (0, slots), constant_values=-1)[None, :]
-    masked = row != jnp.pad(target, (row_count, 0))[None, :]
-    masked = masked & (jnp.arange(row_count + slots)[None, :] >= row_count)
-    scores = jnp.where(masked, -jnp.inf, matmul(everything, lax.optimization_barrier(table.T), 1, 0) * inverse_temp)
-    highest = jnp.max(scores, axis=1)
-    total = jnp.sum(jnp.exp(scores - highest[:, None]), axis=1)
-    stats = jnp.broadcast_to(jnp.stack([highest, total])[None], (dp_count, 2, batch_rows))
+    scored = []
+    for (first, last), piece in zip(starts, gathered):
+        piece_rows = last - first
+        count = dp_count * piece_rows
+        row = jnp.arange(count)[:, None]
+        local = wanting - first
+        target = jnp.where((local >= 0) & (local < piece_rows), wanting_dp * piece_rows + local, -1)
+        mine = jnp.arange(row_count) - first
+        positive = jnp.where((mine >= 0) & (mine < piece_rows), me * piece_rows + mine, -1)
+        positive = row == jnp.pad(positive, (0, slots), constant_values=-1)[None, :]
+        masked = (row != jnp.pad(target, (row_count, 0))[None, :]) & (jnp.arange(row_count + slots)[None, :] >= row_count)
+        scores = jnp.where(masked, -jnp.inf, matmul(piece, table, 1, 1) * inverse_temp)
+        highest = jnp.max(scores, axis=1)
+        scored.append((scores, positive, highest, jnp.sum(jnp.exp(scores - highest[:, None]), axis=1)))
+    stats = jnp.stack([jnp.concatenate([x[i] for x in scored]) for i in (2, 3)])
+    stats = jnp.broadcast_to(stats[None], (dp_count,) + stats.shape)
     stats = lax.all_to_all(stats, "dp", split_axis=0, concat_axis=0, tiled=True)
     highest = jnp.max(stats[:, 0], axis=0)
-    normal = highest + jnp.log(jnp.sum(stats[:, 1] * jnp.exp(stats[:, 0] - highest[None, :]), axis=0))
-    losses = normal - jnp.sum(jnp.where(positive, scores, 0.0), axis=1)
-    losses = lax.dynamic_slice_in_dim(losses, me * row_count, row_count, axis=0)
-    weights = jnp.exp(scores - normal[:, None]) - positive.astype(jnp.float32)
-    weights = weights.astype(jnp.bfloat16)
+    normals = highest + jnp.log(jnp.sum(stats[:, 1] * jnp.exp(stats[:, 0] - highest[None, :]), axis=0))
+    weights, losses, shares, start = [], [], [], 0
+    for (first, last), (scores, positive, _, _) in zip(starts, scored):
+        normal = normals[start : start + scores.shape[0]]
+        start += scores.shape[0]
+        loss = normal - jnp.sum(jnp.where(positive, scores, 0.0), axis=1)
+        losses.append(lax.dynamic_slice_in_dim(loss, me * (last - first), last - first, axis=0))
+        weight = (jnp.exp(scores - normal[:, None]) - positive.astype(jnp.float32)).astype(jnp.bfloat16)
+        weights.append(weight)
+        shares.append((matmul(weight, table, 1, 0) * inverse_temp).astype(jnp.bfloat16))
+    query_grad = [
+        lax.psum_scatter(shares[0], "dp", scatter_dimension=0, tiled=True),
+        scatter_end(*scatter_begin(shares[1], me, dp_count), dp_count),
+    ]
 
-    direct = features // direct_part
-    share = (matmul(weights, table[:, direct:], 1, 0) * inverse_temp).astype(jnp.bfloat16)
-    later = lax.psum_scatter(share, "dp", scatter_dimension=0, tiled=True)
-    weights, share = lax.optimization_barrier((weights, share))
-    ahead = (matmul(weights, table[:, :direct], 1, 0) * inverse_temp).astype(jnp.bfloat16)
-    ahead = scatter_end(*scatter_begin(ahead, me, dp_count), dp_count)
-
+    weights = jnp.concatenate(weights, axis=0)
+    everything = jnp.concatenate(gathered, axis=0)
     passage_grad = matmul(weights[:, :row_count], everything, 0, 0)
     hard_grad = matmul(weights[:, row_count:], everything, 0, 0) * inverse_temp
     passage_grad = passage_grad * inverse_temp + matmul(select, exchange(hard_grad), 1, 0)
-    query_grad = jnp.pad(ahead, ((0, 0), (0, features - direct)))
-    query_grad, later, passage_grad = lax.optimization_barrier((query_grad, later, passage_grad))
-    query_grad = lax.dynamic_update_slice(query_grad, later.astype(jnp.float32), (0, direct))
-    return (query_grad[None], passage_grad[None], losses[None])
+    early, late = query_grad
+    query_grad = jnp.pad(late, ((ahead, 0), (0, 0)))
+    query_grad, early, passage_grad = lax.optimization_barrier((query_grad, early, passage_grad))
+    query_grad = lax.dynamic_update_slice(query_grad, early.astype(jnp.float32), (0, 0))
+    return (query_grad[None], passage_grad[None], jnp.concatenate(losses)[None])
 
 
 def solution(mesh):

time: 198 us -> 194 us (0.980)
  other arithmetic: 13.9 us -> 10.9 us
    reduce_scatter x1, waiting for transfers between devices: 3.7 us -> 17.9 us  [per_device(): lax.psum_scatter(shares[0], 'dp', scatter_dimension=0, tiled=True)]
    all_gather x1, waiting for transfers between devices: 19.2 us -> 10.3 us  [per_device(): piece_ahead = lax.all_gather(query_ahead, 'dp', axis=0, tiled=True)]
    ppermute x0 -> x3, starting transfers between devices: none -> 7.93 us  [send_direct(): lax.ppermute(block, 'dp', [(i, (i + step) % count) for i in range(count)])]
    ppermute x1, starting transfers between devices: 15.9 us -> 10 us  [scatter_end(): up = lax.ppermute(high, 'dp', [(j, i) for i, j in below])]
    ppermute x1, waiting for transfers between devices: 7.9 us -> 2.97 us  [scatter_begin(): up = lax.ppermute(high, 'dp', [(j, i) for i, j in below])]
    all_to_all x1, starting transfers between devices: 7.3 us -> 2.81 us  [per_device(): lax.all_to_all(request, ('dp', 'group'), split_axis=0, concat_axis=0, til...]
    transpose x1 -> x0, other arithmetic: 4.25 us -> none  [per_device(): scores = jnp.where(masked, -jnp.inf, matmul(everything, lax.optimization_...]
    convert_element_type x2, other arithmetic: 3.1 us -> 0.34 us  [per_device(): (jnp.exp(scores - normal[:, None]) - positive.astype(jnp.float32)).astype...]
  transfers between devices with their start and end apart: 10 -> 13, of which waited for: 7 -> 7; matrix products, arithmetic and copies ran while one was open for 15% -> 15% of each run, Pallas kernels for 0% -> 0%
where the time goes in v5:
time: 194 us; the launch traced here: 193 us
  waiting for transfers between devices  85 us (44%)
  starting transfers between devices  38.1 us (20%)
  matrix products  28.7 us (15%)
  between operations  14.5 us (7%)
  other arithmetic  10.9 us (6%)
  blocking collectives  7.96 us (4%)
  local copies, waits for them, and re-layouts  7.85 us (4%)
    all_to_all x2, waiting for transfers between devices, exchange(): lax.all_to_all(rows, 'group', split_axis=0, concat_axis=0, tiled=True)  37.1 us
    dot_general x8, matrix products, matmul(): lax.dot_general(a, b, (((left,), (right,)), ((), ())), preferred_element_...  28.7 us
    reduce_scatter x1, waiting for transfers between devices, per_device(): lax.psum_scatter(shares[0], 'dp', scatter_dimension=0, tiled=True)  17.9 us
    all_gather x1, waiting for transfers between devices, per_device(): piece_ahead = lax.all_gather(query_ahead, 'dp', axis=0, tiled=True)  10.3 us
    ppermute x1, starting transfers between devices, scatter_end(): up = lax.ppermute(high, 'dp', [(j, i) for i, j in below])  10 us
    all_to_all x2, starting transfers between devices, exchange(): lax.all_to_all(rows, 'group', split_axis=0, concat_axis=0, tiled=True)  8.16 us
    all_to_all x1, blocking collectives, per_device(): stats = lax.all_to_all(stats, 'dp', split_axis=0, concat_axis=0, tiled=True)  7.96 us
    ppermute x3, starting transfers between devices, send_direct(): lax.ppermute(block, 'dp', [(i, (i + step) % count) for i in range(count)])  7.93 us
  transfers between devices with their start and end apart: 13, of which 7 were waited for; matrix products, arithmetic and copies ran while one was open for 15% of the time, Pallas kernels for 0%

profile of v5, /device:TPU:0, one launch (start us, length us, event | category | flops | bytes accessed | tf_op | source)
XLA Modules:
  0.0 193.1 jit_solution(2473919967547366280)
XLA Ops:
  7.2 1.7 convert.5
  9.0 4.1 %collective-permute-start.1 = (bf16[16,4096]{1,0:T(8,128)(2,1)S(1)}, bf16[16,4096]{1,0:T(8,128)(2,1)S(1)}, u32[]{:S(2)}, u32[]{:S(2)}) collective-permute-start(bf16[16,4096]{1,0:T(8,128)(2,1)S(1)} %slice_bitcast_fusion), channel_id=1, source_target_pairs={{0,16},{8,24},{16,0},{24,8},{1,17},{9,25},{17,1},{25,9},{2,18},{10... | collective-permute-start | bytes 393224 | tf_op jit(solution)/shard_map/ppermute | solution.py:15
  13.1 1.6 collective-permute-start
  14.6 2.2 %collective-permute-start.2 = (bf16[16,4096]{1,0:T(8,128)(2,1)S(1)}, bf16[16,4096]{1,0:T(8,128)(2,1)S(1)}, u32[]{:S(2)}, u32[]{:S(2)}) collective-permute-start(bf16[16,4096]{1,0:T(8,128)(2,1)S(1)} %slice_bitcast_fusion), channel_id=1, source_target_pairs={{0,24},{8,0},{16,8},{24,16},{1,25},{9,1},{17,9},{25,17},{2,26},{10... | collective-permute-start | bytes 393224 | tf_op jit(solution)/shard_map/ppermute | solution.py:15
  16.9 1.0 slice.46
  17.9 0.2 convert_reduce_fusion
  18.2 0.2 select_reduce_fusion.2
  18.6 0.7 pad_add_fusion
  19.3 2.8 %all-to-all-start = ((s32[32,1,108]{2,1,0:T(1,128)}), s32[32,1,108]{2,1,0:T(1,128)S(1)}, u32[]{:S(2)}, u32[]{:S(2)}) async-start(s32[32,1,108]{2,1,0:T(1,128)} %bitcast.4), calls=%async_computation | async-start | bytes 32768 | tf_op jit(solution)/shard_map/all_to_all | solution.py:109
  22.1 1.9 convert_bitcast_fusion
  24.1 5.2 %all-to-all-done = s32[32,1,108]{2,1,0:T(1,128)S(1)} async-done(((s32[32,1,108]{2,1,0:T(1,128)}), s32[32,1,108]{2,1,0:T(1,128)S(1)}, u32[]{:S(2)}, u32[]{:S(2)}) %all-to-all-start) | async-done | bytes 13856 | tf_op jit(solution)/shard_map/all_to_all | solution.py:109
  29.3 0.1 eq.88
  29.4 2.7 %convolution_convert_fusion = bf16[384,4096]{1,0:T(8,128)(2,1)} fusion(bf16[128,4096]{1,0:T(8,128)(2,1)S(1)} %convert_bitcast_fusion, s32[384]{0:T(512)S(1)} %eq.88), kind=kOutput, calls=%fused_computation.2 | convolution fusion | flops 404275200 | bytes 4195840 | tf_op jit(solution)/shard_map/dot_general | solution.py:63
  32.1 4.5 %all-to-all-start.1 = ((bf16[8,48,4096]{2,1,0:T(8,128)(2,1)}), bf16[8,48,4096]{2,1,0:T(8,128)(2,1)}, u32[]{:S(2)}, u32[]{:S(2)}) async-start(bf16[8,48,4096]{2,1,0:T(8,128)(2,1)} %bitcast.10), calls=%async_computation.1 | async-start | bytes 6291456 | tf_op jit(solution)/shard_map/all_to_all | solution.py:120
  37.1 0.1 reshape.271
  37.3 37.1 %all-to-all-done.1 = bf16[8,48,4096]{2,1,0:T(8,128)(2,1)} async-done(((bf16[8,48,4096]{2,1,0:T(8,128)(2,1)}), bf16[8,48,4096]{2,1,0:T(8,128)(2,1)}, u32[]{:S(2)}, u32[]{:S(2)}) %all-to-all-start.1) | async-done | bytes 3145760 | tf_op jit(solution)/shard_map/all_to_all | solution.py:120
  74.5 3.4 %fusion.39 = (f32[64]{0:T(128)S(1)}, f32[64,512]{1,0:T(8,128)S(1)}) fusion(bf16[64,4096]{1,0:T(8,128)(2,1)S(1)} %constant_dynamic-update-slice_fusion, bf16[384,4096]{1,0:T(8,128)(2,1)} %bitcast.11, bf16[128,4096]{1,0:T(8,128)(2,1)S(1)} %convert_bitcast_fusion, pred[512]{0:T(512)(128)(4,1)S(1)} %iota_compare_fusion.9, s32[512]{0:T(512)S(1)} %pad.18), kind=kOutput, calls=%fused_computation.122 | convolution fusion | flops 276987840 | bytes 4852480 | tf_op jit(solution)/shard_map/dot_general | solution.py:63
  77.9 0.2 select_reduce_fusion.3
  78.1 10.3 %all-gather.3.cloned.1.call-done = bf16[1,448,4096]{2,1,0:T(8,128)(2,1)} async-done(((bf16[1,112,4096]{2,1,0:T(8,128)(2,1)}), bf16[1,448,4096]{2,1,0:T(8,128)(2,1)}) %all-gather.3.cloned.1.call-update) | async-done | bytes 3670032 | tf_op jit(solution)/shard_map/all_gather | solution.py:84
  88.4 5.2 %fusion.40 = (f32[448]{0:T(512)S(1)}, f32[448,512]{1,0:T(8,128)S(1)}) fusion(bf16[1,448,4096]{2,1,0:T(8,128)(2,1)} %all-gather.3.cloned.1.call-done, bf16[384,4096]{1,0:T(8,128)(2,1)} %bitcast.11, bf16[128,4096]{1,0:T(8,128)(2,1)S(1)} %convert_bitcast_fusion, pred[512]{0:T(512)(128)(4,1)S(1)} %iota_compare_fusion.9, s32[512]{0:T(512)S(1)} %pad.19), kind=kOutput, calls=%fused_computation.123 | convolution fusion | flops 1888583168 | bytes 8786176 | tf_op jit(solution)/shard_map/dot_general | solution.py:63
  93.7 0.4 select_reduce_fusion
  94.2 8.0 %all_to_all.24 = f32[4,2,512]{2,1,0:T(2,128)S(1)} all-to-all(f32[4,2,512]{2,1,0:T(2,128)S(1)} %broadcast_in_dim.97), channel_id=1, replica_groups=mesh['dp'=4,'group'=8] {'dp'}, dimensions={0} | all-to-all | bytes 32768 | tf_op jit(solution)/shard_map/all_to_all | solution.py:140
  102.2 0.2 subtract_convert_fusion
  102.5 6.0 %multiply_convert_fusion = bf16[448,4096]{1,0:T(8,128)(2,1)} fusion(bf16[448,512]{1,0:T(8,128)(2,1)S(1)} %subtract_convert_fusion, bf16[384,4096]{1,0:T(8,128)(2,1)} %bitcast.11, bf16[128,4096]{1,0:T(8,128)(2,1)S(1)} %convert_bitcast_fusion), kind=kOutput, calls=%fused_computation | convolution fusion | flops 1891106816 | bytes 8323072 | tf_op jit(solution)/shard_map/dot_general | solution.py:63
  108.7 5.6 %multiply_convert_fusion.1 = bf16[384,4096]{1,0:T(8,128)(2,1)} fusion(bf16[64,4096]{1,0:T(8,128)(2,1)S(1)} %constant_dynamic-update-slice_fusion, bf16[448,4096]{1,0:T(8,128)(2,1)} %bitcast.75, bf16[64,512]{1,0:T(8,128)(2,1)S(1)} %subtract_convert_fusion.1, bf16[448,512]{1,0:T(8,128)(2,1)S(1)} %subtract_convert_fusion), kind=kOutput, calls=%fused_computation.1 | convolution fusion | flops 1622933504 | bytes 7864320 | tf_op jit(solution)/shard_map/dot_general | solution.py:63
  114.3 3.7 %all-to-all-start.3 = ((bf16[8,48,4096]{2,1,0:T(8,128)(2,1)}), bf16[8,48,4096]{2,1,0:T(8,128)(2,1)S(1)}, u32[]{:S(2)}, u32[]{:S(2)}) async-start(bf16[8,48,4096]{2,1,0:T(8,128)(2,1)} %bitcast.77), calls=%async_computation.4 | async-start | bytes 6291456 | tf_op jit(solution)/shard_map/all_to_all | solution.py:120
  118.0 3.0 %fusion.1 = bf16[64,4096]{1,0:T(8,128)(2,1)S(1)} fusion(bf16[64,512]{1,0:T(8,128)(2,1)S(1)} %subtract_convert_fusion.1, bf16[384,4096]{1,0:T(8,128)(2,1)} %bitcast.11, bf16[128,4096]{1,0:T(8,128)(2,1)} %copy-done), kind=kOutput, calls=%fused_computation.6 | convolution fusion | flops 277348352 | bytes 4784128 | tf_op jit(solution)/shard_map/dot_general | solution.py:63
  121.0 0.8 copy-done.8
  121.8 0.7 constant_dynamic-slice_fusion.2
  122.5 1.3 collective-permute-start.6
  123.9 3.2 %collective-permute-start.4 = (bf16[16,4096]{1,0:T(8,128)(2,1)}, bf16[16,4096]{1,0:T(8,128)(2,1)}, u32[]{:S(2)}, u32[]{:S(2)}) collective-permute-start(bf16[16,4096]{1,0:T(8,128)(2,1)} %get-tuple-element.17), channel_id=1, source_target_pairs={{0,8},{8,16},{1,9},{9,17},{2,10},{10,18},{3,11},{11,19},{4,12},{12... | collective-permute-start | bytes 393224 | tf_op jit(solution)/shard_map/ppermute | solution.py:44
  127.1 3.3 %collective-permute-start.3 = (bf16[16,4096]{1,0:T(8,128)(2,1)S(1)}, bf16[16,4096]{1,0:T(8,128)(2,1)S(1)}, u32[]{:S(2)}, u32[]{:S(2)}) collective-permute-start(bf16[16,4096]{1,0:T(8,128)(2,1)S(1)} %get-tuple-element.15), channel_id=1, source_target_pairs={{0,24},{24,0},{1,25},{25,1},{2,26},{26,2},{3,27},{27,3},{4,28},{28... | collective-permute-start | bytes 393224 | tf_op jit(solution)/shard_map/ppermute | solution.py:46
  130.4 3.0 %collective-permute-done.4 = bf16[16,4096]{1,0:T(8,128)(2,1)} collective-permute-done((bf16[16,4096]{1,0:T(8,128)(2,1)}, bf16[16,4096]{1,0:T(8,128)(2,1)}, u32[]{:S(2)}, u32[]{:S(2)}) %collective-permute-start.4) | collective-permute-done | bytes 131104 | tf_op jit(solution)/shard_map/ppermute | solution.py:44
  133.4 1.8 add_convert_fusion.1
  135.2 10.0 %collective-permute-start.5 = (bf16[16,4096]{1,0:T(8,128)(2,1)}, bf16[16,4096]{1,0:T(8,128)(2,1)}, u32[]{:S(2)}, u32[]{:S(2)}) collective-permute-start(bf16[16,4096]{1,0:T(8,128)(2,1)} %get-tuple-element.18), channel_id=1, source_target_pairs={{0,8},{8,16},{16,24},{1,9},{9,17},{17,25},{2,10},{10,18},{18,26},{... | collective-permute-start | bytes 393224 | tf_op jit(solution)/shard_map/ppermute | solution.py:58
  145.2 1.3 collective-permute-start.7
  146.7 0.6 maximum_bitcast_fusion
  147.3 4.1 %collective-permute-done.5 = bf16[16,4096]{1,0:T(8,128)(2,1)} collective-permute-done((bf16[16,4096]{1,0:T(8,128)(2,1)}, bf16[16,4096]{1,0:T(8,128)(2,1)}, u32[]{:S(2)}, u32[]{:S(2)}) %collective-permute-start.5) | collective-permute-done | bytes 131104 | tf_op jit(solution)/shard_map/ppermute | solution.py:58
  151.3 7.4 %collective-permute-done.7 = bf16[16,4096]{1,0:T(8,128)(2,1)} collective-permute-done((bf16[16,4096]{1,0:T(8,128)(2,1)}, bf16[16,4096]{1,0:T(8,128)(2,1)}, u32[]{:S(2)}, u32[]{:S(2)}) %collective-permute-start.7) | collective-permute-done | bytes 131104 | tf_op jit(solution)/shard_map/ppermute | solution.py:57
  158.8 1.1 convert_add_fusion
  159.9 1.5 pad.21
  161.4 0.7 fusion.8
  162.1 1.3 copy-done.1
  163.6 0.1 copy-done.7
  163.7 2.1 %fusion = f32[128,4096]{1,0:T(8,128)} fusion(f32[128,4096]{1,0:T(8,128)S(1)} %fusion.8, bf16[64,4096]{1,0:T(8,128)(2,1)S(1)} %copy-done.5, bf16[448,4096]{1,0:T(8,128)(2,1)S(1)} %bitcast.76, bf16[64,512]{1,0:T(8,128)(2,1)S(1)} %subtract_convert_fusion.1, bf16[448,512]{1,0:T(8,128)(2,1)S(1)} %copy-done.7), kind=kOutput, calls=%fused_computation.4 | convolution fusion | flops 546570240 | bytes 8912896 | tf_op jit(solution)/shard_map/dot_general | solution.py:63
  165.8 17.9 %reduce-scatter.2.cloned.1.call-done = bf16[112,4096]{1,0:T(8,128)(2,1)} async-done(((bf16[448,4096]{1,0:T(8,128)(2,1)}), bf16[112,4096]{1,0:T(8,128)(2,1)}) %reduce-scatter.2.cloned.1.call-update) | async-done | bytes 917520 | tf_op jit(solution)/shard_map/reduce_scatter | solution.py:153
  183.6 1.3 convert_dynamic-update-slice_fusion
  185.0 1.3 copy-done.3
  (65 shorter events, 1.4 us)
Async XLA Ops:
  7.2 10.7 %copy-start.9 = (s32[1,128,3]{1,0,2:T(1,128)S(1)}, s32[1,128,3]{1,0,2:T(1,128)}, u32[]{:S(2)}) copy-start(s32[1,128,3]{1,0,2:T(1,128)} %param.5) | copy-start | bytes 4612
  7.2 81.2 %all-gather.3.cloned.1.call-start = ((), (), s32[]{:S(2)}) async-start(), calls=%async_computation.6 | async-start | bytes 4587520 | tf_op jit(solution)/shard_map/all_gather | solution.py:84
  9.0 28.3 %collective-permute-start.1 = (bf16[16,4096]{1,0:T(8,128)(2,1)S(1)}, bf16[16,4096]{1,0:T(8,128)(2,1)S(1)}, u32[]{:S(2)}, u32[]{:S(2)}) collective-permute-start(bf16[16,4096]{1,0:T(8,128)(2,1)S(1)} %slice_bitcast_fusion), channel_id=1, source_target_pairs={{0,16},{8,24},{16,0},{24,8},{1,17},{9,25},{17,1},{25,9},{2,18},{10... | collective-permute-start | bytes 393224 | tf_op jit(solution)/shard_map/ppermute | solution.py:15
  13.1 24.2 %collective-permute-start = (bf16[16,4096]{1,0:T(8,128)(2,1)S(1)}, bf16[16,4096]{1,0:T(8,128)(2,1)S(1)}, u32[]{:S(2)}, u32[]{:S(2)}) collective-permute-start(bf16[16,4096]{1,0:T(8,128)(2,1)S(1)} %slice_bitcast_fusion), channel_id=1, source_target_pairs={{0,8},{8,16},{16,24},{24,0},{1,9},{9,17},{17,25},{25,1},{2,10},{10... | collective-permute-start | bytes 393224 | tf_op jit(solution)/shard_map/ppermute | solution.py:15
  14.6 22.7 %collective-permute-start.2 = (bf16[16,4096]{1,0:T(8,128)(2,1)S(1)}, bf16[16,4096]{1,0:T(8,128)(2,1)S(1)}, u32[]{:S(2)}, u32[]{:S(2)}) collective-permute-start(bf16[16,4096]{1,0:T(8,128)(2,1)S(1)} %slice_bitcast_fusion), channel_id=1, source_target_pairs={{0,24},{8,0},{16,8},{24,16},{1,25},{9,1},{17,9},{25,17},{2,26},{10... | collective-permute-start | bytes 393224 | tf_op jit(solution)/shard_map/ppermute | solution.py:15
  19.3 10.0 %all-to-all-start = ((s32[32,1,108]{2,1,0:T(1,128)}), s32[32,1,108]{2,1,0:T(1,128)S(1)}, u32[]{:S(2)}, u32[]{:S(2)}) async-start(s32[32,1,108]{2,1,0:T(1,128)} %bitcast.4), calls=%async_computation | async-start | bytes 32768 | tf_op jit(solution)/shard_map/all_to_all | solution.py:109
  24.0 78.5 %copy-start = (bf16[128,4096]{1,0:T(8,128)(2,1)}, bf16[128,4096]{1,0:T(8,128)(2,1)S(1)}, u32[]{:S(2)}) copy-start(bf16[128,4096]{1,0:T(8,128)(2,1)S(1)} %convert_bitcast_fusion) | copy-start | bytes 3145732
  32.1 42.4 %all-to-all-start.1 = ((bf16[8,48,4096]{2,1,0:T(8,128)(2,1)}), bf16[8,48,4096]{2,1,0:T(8,128)(2,1)}, u32[]{:S(2)}, u32[]{:S(2)}) async-start(bf16[8,48,4096]{2,1,0:T(8,128)(2,1)} %bitcast.10), calls=%async_computation.1 | async-start | bytes 6291456 | tf_op jit(solution)/shard_map/all_to_all | solution.py:120
  36.6 147.0 %reduce-scatter.2.cloned.1.call-start = ((), (), s32[]{:S(2)}) async-start(), calls=%async_computation.5 | async-start | bytes 4587520 | tf_op jit(solution)/shard_map/reduce_scatter | solution.py:153
  37.3 71.4 %copy-start.4 = (bf16[64,4096]{1,0:T(8,128)(2,1)}, bf16[64,4096]{1,0:T(8,128)(2,1)S(1)}, u32[]{:S(2)}) copy-start(bf16[64,4096]{1,0:T(8,128)(2,1)S(1)} %constant_dynamic-update-slice_fusion) | copy-start | bytes 1572868
  102.5 6.2 %copy-start.6 = (bf16[448,512]{1,0:T(8,128)(2,1)}, bf16[448,512]{1,0:T(8,128)(2,1)S(1)}, u32[]{:S(2)}) copy-start(bf16[448,512]{1,0:T(8,128)(2,1)S(1)} %subtract_convert_fusion) | copy-start | bytes 1376260
  114.3 47.1 %all-to-all-start.3 = ((bf16[8,48,4096]{2,1,0:T(8,128)(2,1)}), bf16[8,48,4096]{2,1,0:T(8,128)(2,1)S(1)}, u32[]{:S(2)}, u32[]{:S(2)}) async-start(bf16[8,48,4096]{2,1,0:T(8,128)(2,1)} %bitcast.77), calls=%async_computation.4 | async-start | bytes 6291456 | tf_op jit(solution)/shard_map/all_to_all | solution.py:120
  121.0 0.8 copy-start.8
  122.5 7.8 %collective-permute-start.6 = (bf16[16,4096]{1,0:T(8,128)(2,1)}, bf16[16,4096]{1,0:T(8,128)(2,1)}, u32[]{:S(2)}, u32[]{:S(2)}) collective-permute-start(bf16[16,4096]{1,0:T(8,128)(2,1)} %get-tuple-element.16), channel_id=1, source_target_pairs={{16,8},{24,16},{17,9},{25,17},{18,10},{26,18},{19,11},{27,19},{20,... | collective-permute-start | bytes 393224 | tf_op jit(solution)/shard_map/ppermute | solution.py:43
  123.9 9.5 %collective-permute-start.4 = (bf16[16,4096]{1,0:T(8,128)(2,1)}, bf16[16,4096]{1,0:T(8,128)(2,1)}, u32[]{:S(2)}, u32[]{:S(2)}) collective-permute-start(bf16[16,4096]{1,0:T(8,128)(2,1)} %get-tuple-element.17), channel_id=1, source_target_pairs={{0,8},{8,16},{1,9},{9,17},{2,10},{10,18},{3,11},{11,19},{4,12},{12... | collective-permute-start | bytes 393224 | tf_op jit(solution)/shard_map/ppermute | solution.py:44
  127.1 20.2 %collective-permute-start.3 = (bf16[16,4096]{1,0:T(8,128)(2,1)S(1)}, bf16[16,4096]{1,0:T(8,128)(2,1)S(1)}, u32[]{:S(2)}, u32[]{:S(2)}) collective-permute-start(bf16[16,4096]{1,0:T(8,128)(2,1)S(1)} %get-tuple-element.15), channel_id=1, source_target_pairs={{0,24},{24,0},{1,25},{25,1},{2,26},{26,2},{3,27},{27,3},{4,28},{28... | collective-permute-start | bytes 393224 | tf_op jit(solution)/shard_map/ppermute | solution.py:46
  135.2 16.1 %collective-permute-start.5 = (bf16[16,4096]{1,0:T(8,128)(2,1)}, bf16[16,4096]{1,0:T(8,128)(2,1)}, u32[]{:S(2)}, u32[]{:S(2)}) collective-permute-start(bf16[16,4096]{1,0:T(8,128)(2,1)} %get-tuple-element.18), channel_id=1, source_target_pairs={{0,8},{8,16},{16,24},{1,9},{9,17},{17,25},{2,10},{10,18},{18,26},{... | collective-permute-start | bytes 393224 | tf_op jit(solution)/shard_map/ppermute | solution.py:58
  145.2 13.5 %collective-permute-start.7 = (bf16[16,4096]{1,0:T(8,128)(2,1)}, bf16[16,4096]{1,0:T(8,128)(2,1)}, u32[]{:S(2)}, u32[]{:S(2)}) collective-permute-start(bf16[16,4096]{1,0:T(8,128)(2,1)} %get-tuple-element.19), channel_id=1, source_target_pairs={{8,0},{16,8},{24,16},{9,1},{17,9},{25,17},{10,2},{18,10},{26,18},{... | collective-permute-start | bytes 393224 | tf_op jit(solution)/shard_map/ppermute | solution.py:57
  161.4 2.1 %copy-start.1 = (bf16[1,448,4096]{2,1,0:T(8,128)(2,1)S(1)}, bf16[1,448,4096]{2,1,0:T(8,128)(2,1)}, u32[]{:S(2)}) copy-start(bf16[1,448,4096]{2,1,0:T(8,128)(2,1)} %all-gather.3.cloned.1.call-done) | copy-start | bytes 11010052
  161.4 2.2 %copy-start.5 = (bf16[64,4096]{1,0:T(8,128)(2,1)S(1)}, bf16[64,4096]{1,0:T(8,128)(2,1)}, u32[]{:S(2)}) copy-start(bf16[64,4096]{1,0:T(8,128)(2,1)} %copy-done.4) | copy-start | bytes 1572868
  161.4 2.3 %copy-start.7 = (bf16[448,512]{1,0:T(8,128)(2,1)S(1)}, bf16[448,512]{1,0:T(8,128)(2,1)}, u32[]{:S(2)}) copy-start(bf16[448,512]{1,0:T(8,128)(2,1)} %copy-done.6) | copy-start | bytes 1376260
  163.7 20.0 %copy-start.2 = (f32[128,4096]{1,0:T(8,128)S(1)}, f32[128,4096]{1,0:T(8,128)}, u32[]{:S(2)}) copy-start(f32[128,4096]{1,0:T(8,128)} %pad.21) | copy-start | bytes 6291460
  185.0 1.3 copy-start.3
Sparse Core Ops, SparseCore 0:
  18.0 70.3 all-gather.2
  108.6 74.9 reduce-scatter.1

commit v6 on v5

--- a/solution.py
+++ b/solution.py
@@ -78,7 +78,7 @@
 
     ahead = row_count - row_count // later_part
     query_ahead = queries[0, :ahead].astype(jnp.bfloat16)
-    query_later = queries[0, ahead:].astype(jnp.bfloat16)
+    query_later = lax.optimization_barrier(queries[0, ahead:]).astype(jnp.bfloat16)
     passage_low = passages[0].astype(jnp.bfloat16)
 
     piece_ahead = lax.all_gather(query_ahead, "dp", axis=0, tiled=True)

time: 194 us -> 202 us (1.041)
  waiting for transfers between devices: 85 us -> 91.1 us
  local copies, waits for them, and re-layouts: 7.85 us -> 10.7 us
  other arithmetic: 10.9 us -> 8.15 us
    all_to_all x2, waiting for transfers between devices: 37.1 us -> 17.9 us  [exchange(): lax.all_to_all(rows, 'group', split_axis=0, concat_axis=0, tiled=True)]
    ppermute x3, waiting for transfers between devices: 0.01 us -> 13.9 us  [send_direct(): lax.ppermute(block, 'dp', [(i, (i + step) % count) for i in range(count)])]
    all_gather x1, waiting for transfers between devices: 10.3 us -> 20.8 us  [per_device(): piece_ahead = lax.all_gather(query_ahead, 'dp', axis=0, tiled=True)]
    all_to_all x1, starting transfers between devices: 2.81 us -> 7.3 us  [per_device(): lax.all_to_all(request, ('dp', 'group'), split_axis=0, concat_axis=0, til...]
    ppermute x3, starting transfers between devices: 7.93 us -> 4.47 us  [send_direct(): lax.ppermute(block, 'dp', [(i, (i + step) % count) for i in range(count)])]
  transfers between devices with their start and end apart: 13 -> 13, of which waited for: 7 -> 9; matrix products, arithmetic and copies ran while one was open for 15% -> 15% of each run, Pallas kernels for 0% -> 0%
where the time goes in v6:
time: 202 us; the launch traced here: 201 us
  waiting for transfers between devices  91.1 us (45%)
  starting transfers between devices  39 us (19%)
  matrix products  29.5 us (15%)
  between operations  14.4 us (7%)
  local copies, waits for them, and re-layouts  10.7 us (5%)
  other arithmetic  8.15 us (4%)
  blocking collectives  7.96 us (4%)
    dot_general x8, matrix products, matmul(): lax.dot_general(a, b, (((left,), (right,)), ((), ())), preferred_element_...  29.5 us
    all_gather x1, waiting for transfers between devices, per_device(): piece_ahead = lax.all_gather(query_ahead, 'dp', axis=0, tiled=True)  20.8 us
    all_to_all x2, waiting for transfers between devices, exchange(): lax.all_to_all(rows, 'group', split_axis=0, concat_axis=0, tiled=True)  17.9 us
    reduce_scatter x1, waiting for transfers between devices, per_device(): lax.psum_scatter(shares[0], 'dp', scatter_dimension=0, tiled=True)  16.8 us
    ppermute x3, waiting for transfers between devices, send_direct(): lax.ppermute(block, 'dp', [(i, (i + step) % count) for i in range(count)])  13.9 us
    ppermute x1, starting transfers between devices, scatter_end(): up = lax.ppermute(high, 'dp', [(j, i) for i, j in below])  9.89 us
    all_to_all x2, starting transfers between devices, exchange(): lax.all_to_all(rows, 'group', split_axis=0, concat_axis=0, tiled=True)  8.14 us
    ppermute x1, waiting for transfers between devices, scatter_end(): down = lax.ppermute(low, 'dp', [(j, i) for i, j in above])  7.99 us
  transfers between devices with their start and end apart: 13, of which 9 were waited for; matrix products, arithmetic and copies ran while one was open for 15% of the time, Pallas kernels for 0%

profile of v6, /device:TPU:0, one launch (start us, length us, event | category | flops | bytes accessed | tf_op | source)
XLA Modules:
  0.0 200.8 jit_solution(16614243298494994351)
XLA Ops:
  7.2 2.7 %slice.53 = bf16[1,112,4096]{2,1,0:T(8,128)(2,1)} slice(f32[1,128,4096]{2,1,0:T(8,128)} %param.3), slice={[0:1], [0:112], [0:4096]} | slice | bytes 1835008 | tf_op jit(solution)/shard_map/slice | solution.py:80
  9.9 0.7 fusion.22
  10.6 0.2 convert_reduce_fusion
  10.9 0.2 select_reduce_fusion.2
  11.3 0.7 pad_add_fusion
  12.0 7.3 %all-to-all-start = ((s32[32,1,108]{2,1,0:T(1,128)}), s32[32,1,108]{2,1,0:T(1,128)S(1)}, u32[]{:S(2)}, u32[]{:S(2)}) async-start(s32[32,1,108]{2,1,0:T(1,128)} %bitcast.4), calls=%async_computation | async-start | bytes 32768 | tf_op jit(solution)/shard_map/all_to_all | solution.py:109
  19.3 0.1 convert_bitcast_fusion
  19.5 7.0 %all-to-all-done = s32[32,1,108]{2,1,0:T(1,128)S(1)} async-done(((s32[32,1,108]{2,1,0:T(1,128)}), s32[32,1,108]{2,1,0:T(1,128)S(1)}, u32[]{:S(2)}, u32[]{:S(2)}) %all-to-all-start) | async-done | bytes 13856 | tf_op jit(solution)/shard_map/all_to_all | solution.py:109
  26.6 2.7 %convolution_convert_fusion = bf16[384,4096]{1,0:T(8,128)(2,1)} fusion(bf16[128,4096]{1,0:T(8,128)(2,1)S(1)} %convert_bitcast_fusion, s32[384]{0:T(512)S(1)} %eq.88), kind=kOutput, calls=%fused_computation.2 | convolution fusion | flops 404275200 | bytes 4195840 | tf_op jit(solution)/shard_map/dot_general | solution.py:63
  29.3 4.5 %all-to-all-start.1 = ((bf16[8,48,4096]{2,1,0:T(8,128)(2,1)}), bf16[8,48,4096]{2,1,0:T(8,128)(2,1)}, u32[]{:S(2)}, u32[]{:S(2)}) async-start(bf16[8,48,4096]{2,1,0:T(8,128)(2,1)} %bitcast.10), calls=%async_computation.1 | async-start | bytes 6291456 | tf_op jit(solution)/shard_map/all_to_all | solution.py:120
  33.8 1.0 slice_bitcast_fusion
  34.8 0.7 collective-permute-start.1
  35.5 0.5 collective-permute-start
  36.0 3.3 %collective-permute-start.2 = (bf16[16,4096]{1,0:T(8,128)(2,1)S(1)}, bf16[16,4096]{1,0:T(8,128)(2,1)S(1)}, u32[]{:S(2)}, u32[]{:S(2)}) collective-permute-start(bf16[16,4096]{1,0:T(8,128)(2,1)S(1)} %slice_bitcast_fusion), channel_id=1, source_target_pairs={{0,24},{8,0},{16,8},{24,16},{1,25},{9,1},{17,9},{25,17},{2,26},{10... | collective-permute-start | bytes 393224 | tf_op jit(solution)/shard_map/ppermute | solution.py:15
  39.8 10.8 %collective-permute-done = bf16[16,4096]{1,0:T(8,128)(2,1)S(1)} collective-permute-done((bf16[16,4096]{1,0:T(8,128)(2,1)S(1)}, bf16[16,4096]{1,0:T(8,128)(2,1)S(1)}, u32[]{:S(2)}, u32[]{:S(2)}) %collective-permute-start) | collective-permute-done | bytes 131104 | tf_op jit(solution)/shard_map/ppermute | solution.py:15
  50.6 3.1 %collective-permute-done.1 = bf16[16,4096]{1,0:T(8,128)(2,1)S(1)} collective-permute-done((bf16[16,4096]{1,0:T(8,128)(2,1)S(1)}, bf16[16,4096]{1,0:T(8,128)(2,1)S(1)}, u32[]{:S(2)}, u32[]{:S(2)}) %collective-permute-start.1) | collective-permute-done | bytes 131104 | tf_op jit(solution)/shard_map/ppermute | solution.py:15
  53.8 17.9 %all-to-all-done.1 = bf16[8,48,4096]{2,1,0:T(8,128)(2,1)} async-done(((bf16[8,48,4096]{2,1,0:T(8,128)(2,1)}), bf16[8,48,4096]{2,1,0:T(8,128)(2,1)}, u32[]{:S(2)}, u32[]{:S(2)}) %all-to-all-start.1) | async-done | bytes 3145760 | tf_op jit(solution)/shard_map/all_to_all | solution.py:120
  71.7 3.4 %fusion.39 = (f32[64]{0:T(128)S(1)}, f32[64,512]{1,0:T(8,128)S(1)}) fusion(bf16[64,4096]{1,0:T(8,128)(2,1)S(1)} %constant_dynamic-update-slice_fusion, bf16[384,4096]{1,0:T(8,128)(2,1)} %bitcast.11, bf16[128,4096]{1,0:T(8,128)(2,1)S(1)} %convert_bitcast_fusion, pred[512]{0:T(512)(128)(4,1)S(1)} %iota_compare_fusion.9, s32[512]{0:T(512)S(1)} %pad.18), kind=kOutput, calls=%fused_computation.123 | convolution fusion | flops 276987840 | bytes 4852480 | tf_op jit(solution)/shard_map/dot_general | solution.py:63
  75.1 0.2 select_reduce_fusion.3
  75.3 20.8 %all-gather.3.cloned.1.call-done = bf16[1,448,4096]{2,1,0:T(8,128)(2,1)} async-done(((bf16[1,112,4096]{2,1,0:T(8,128)(2,1)}), bf16[1,448,4096]{2,1,0:T(8,128)(2,1)}) %all-gather.3.cloned.1.call-update) | async-done | bytes 3670032 | tf_op jit(solution)/shard_map/all_gather | solution.py:84
  96.1 5.3 %fusion.40 = (f32[448]{0:T(512)S(1)}, f32[448,512]{1,0:T(8,128)S(1)}) fusion(bf16[1,448,4096]{2,1,0:T(8,128)(2,1)} %all-gather.3.cloned.1.call-done, bf16[384,4096]{1,0:T(8,128)(2,1)} %bitcast.11, bf16[128,4096]{1,0:T(8,128)(2,1)S(1)} %convert_bitcast_fusion, pred[512]{0:T(512)(128)(4,1)S(1)} %iota_compare_fusion.9, s32[512]{0:T(512)S(1)} %pad.19), kind=kOutput, calls=%fused_computation.124 | convolution fusion | flops 1888583168 | bytes 8786176 | tf_op jit(solution)/shard_map/dot_general | solution.py:63
  101.4 0.4 select_reduce_fusion
  101.9 8.0 %all_to_all.24 = f32[4,2,512]{2,1,0:T(2,128)S(1)} all-to-all(f32[4,2,512]{2,1,0:T(2,128)S(1)} %broadcast_in_dim.97), channel_id=1, replica_groups=mesh['dp'=4,'group'=8] {'dp'}, dimensions={0} | all-to-all | bytes 32768 | tf_op jit(solution)/shard_map/all_to_all | solution.py:140
  109.9 0.2 subtract_convert_fusion
  110.2 6.0 %multiply_convert_fusion = bf16[448,4096]{1,0:T(8,128)(2,1)} fusion(bf16[448,512]{1,0:T(8,128)(2,1)S(1)} %subtract_convert_fusion, bf16[384,4096]{1,0:T(8,128)(2,1)} %bitcast.11, bf16[128,4096]{1,0:T(8,128)(2,1)S(1)} %convert_bitcast_fusion), kind=kOutput, calls=%fused_computation | convolution fusion | flops 1891106816 | bytes 8323072 | tf_op jit(solution)/shard_map/dot_general | solution.py:63
  116.4 5.6 %multiply_convert_fusion.1 = bf16[384,4096]{1,0:T(8,128)(2,1)} fusion(bf16[64,4096]{1,0:T(8,128)(2,1)S(1)} %constant_dynamic-update-slice_fusion, bf16[448,4096]{1,0:T(8,128)(2,1)} %bitcast.73, bf16[64,512]{1,0:T(8,128)(2,1)S(1)} %subtract_convert_fusion.1, bf16[448,512]{1,0:T(8,128)(2,1)S(1)} %subtract_convert_fusion), kind=kOutput, calls=%fused_computation.1 | convolution fusion | flops 1622933504 | bytes 7864320 | tf_op jit(solution)/shard_map/dot_general | solution.py:63
  122.0 3.7 %all-to-all-start.3 = ((bf16[8,48,4096]{2,1,0:T(8,128)(2,1)}), bf16[8,48,4096]{2,1,0:T(8,128)(2,1)S(1)}, u32[]{:S(2)}, u32[]{:S(2)}) async-start(bf16[8,48,4096]{2,1,0:T(8,128)(2,1)} %bitcast.75), calls=%async_computation.4 | async-start | bytes 6291456 | tf_op jit(solution)/shard_map/all_to_all | solution.py:120
  125.7 3.8 %fusion.1 = bf16[64,4096]{1,0:T(8,128)(2,1)} fusion(bf16[64,512]{1,0:T(8,128)(2,1)S(1)} %subtract_convert_fusion.1, bf16[384,4096]{1,0:T(8,128)(2,1)} %bitcast.11, bf16[128,4096]{1,0:T(8,128)(2,1)} %copy-done), kind=kOutput, calls=%fused_computation.6 | convolution fusion | flops 277348352 | bytes 4784128 | tf_op jit(solution)/shard_map/dot_general | solution.py:63
  129.5 1.8 constant_dynamic-slice_fusion.2
  131.2 1.3 collective-permute-start.6
  132.5 3.2 %collective-permute-start.4 = (bf16[16,4096]{1,0:T(8,128)(2,1)}, bf16[16,4096]{1,0:T(8,128)(2,1)}, u32[]{:S(2)}, u32[]{:S(2)}) collective-permute-start(bf16[16,4096]{1,0:T(8,128)(2,1)} %get-tuple-element.17), channel_id=1, source_target_pairs={{0,8},{8,16},{1,9},{9,17},{2,10},{10,18},{3,11},{11,19},{4,12},{12... | collective-permute-start | bytes 393224 | tf_op jit(solution)/shard_map/ppermute | solution.py:44
  135.8 3.3 %collective-permute-start.3 = (bf16[16,4096]{1,0:T(8,128)(2,1)S(1)}, bf16[16,4096]{1,0:T(8,128)(2,1)S(1)}, u32[]{:S(2)}, u32[]{:S(2)}) collective-permute-start(bf16[16,4096]{1,0:T(8,128)(2,1)S(1)} %get-tuple-element.15), channel_id=1, source_target_pairs={{0,24},{24,0},{1,25},{25,1},{2,26},{26,2},{3,27},{27,3},{4,28},{28... | collective-permute-start | bytes 393224 | tf_op jit(solution)/shard_map/ppermute | solution.py:46
  139.1 3.0 %collective-permute-done.4 = bf16[16,4096]{1,0:T(8,128)(2,1)} collective-permute-done((bf16[16,4096]{1,0:T(8,128)(2,1)}, bf16[16,4096]{1,0:T(8,128)(2,1)}, u32[]{:S(2)}, u32[]{:S(2)}) %collective-permute-start.4) | collective-permute-done | bytes 131104 | tf_op jit(solution)/shard_map/ppermute | solution.py:44
  142.1 1.9 add_convert_fusion.1
  143.9 9.9 %collective-permute-start.5 = (bf16[16,4096]{1,0:T(8,128)(2,1)}, bf16[16,4096]{1,0:T(8,128)(2,1)}, u32[]{:S(2)}, u32[]{:S(2)}) collective-permute-start(bf16[16,4096]{1,0:T(8,128)(2,1)} %get-tuple-element.18), channel_id=1, source_target_pairs={{0,8},{8,16},{16,24},{1,9},{9,17},{17,25},{2,10},{10,18},{18,26},{... | collective-permute-start | bytes 393224 | tf_op jit(solution)/shard_map/ppermute | solution.py:58
  153.8 1.3 collective-permute-start.7
  155.3 0.6 maximum_bitcast_fusion
  155.9 3.7 %collective-permute-done.5 = bf16[16,4096]{1,0:T(8,128)(2,1)} collective-permute-done((bf16[16,4096]{1,0:T(8,128)(2,1)}, bf16[16,4096]{1,0:T(8,128)(2,1)}, u32[]{:S(2)}, u32[]{:S(2)}) %collective-permute-start.5) | collective-permute-done | bytes 131104 | tf_op jit(solution)/shard_map/ppermute | solution.py:58
  159.6 8.0 %collective-permute-done.7 = bf16[16,4096]{1,0:T(8,128)(2,1)} collective-permute-done((bf16[16,4096]{1,0:T(8,128)(2,1)}, bf16[16,4096]{1,0:T(8,128)(2,1)}, u32[]{:S(2)}, u32[]{:S(2)}) %collective-permute-start.7) | collective-permute-done | bytes 131104 | tf_op jit(solution)/shard_map/ppermute | solution.py:57
  167.6 1.1 convert_add_fusion
  168.6 1.5 pad.21
  170.2 0.7 fusion.8
  170.9 1.3 copy-done.1
  172.3 0.1 copy-done.8
  172.5 2.1 %fusion = f32[128,4096]{1,0:T(8,128)} fusion(f32[128,4096]{1,0:T(8,128)S(1)} %fusion.8, bf16[64,4096]{1,0:T(8,128)(2,1)S(1)} %copy-done.5, bf16[448,4096]{1,0:T(8,128)(2,1)S(1)} %bitcast.74, bf16[64,512]{1,0:T(8,128)(2,1)S(1)} %subtract_convert_fusion.1, bf16[448,512]{1,0:T(8,128)(2,1)S(1)} %copy-done.8), kind=kOutput, calls=%fused_computation.4 | convolution fusion | flops 546570240 | bytes 8912896 | tf_op jit(solution)/shard_map/dot_general | solution.py:63
  174.5 16.8 %reduce-scatter.2.cloned.1.call-done = bf16[112,4096]{1,0:T(8,128)(2,1)} async-done(((bf16[448,4096]{1,0:T(8,128)(2,1)}), bf16[112,4096]{1,0:T(8,128)(2,1)}) %reduce-scatter.2.cloned.1.call-update) | async-done | bytes 917520 | tf_op jit(solution)/shard_map/reduce_scatter | solution.py:153
  191.3 1.3 convert_dynamic-update-slice_fusion
  192.7 1.3 copy-done.3
  (62 shorter events, 1.6 us)
Async XLA Ops:
  7.2 12.1 %copy-start.6 = (f32[1,128,4096]{2,1,0:T(8,128)S(1)}, f32[1,128,4096]{2,1,0:T(8,128)}, u32[]{:S(2)}) copy-start(f32[1,128,4096]{2,1,0:T(8,128)} %param.4) | copy-start | bytes 6291460
  7.2 88.9 %all-gather.3.cloned.1.call-start = ((), (), s32[]{:S(2)}) async-start(), calls=%async_computation.6 | async-start | bytes 4587520 | tf_op jit(solution)/shard_map/all_gather | solution.py:84
  12.0 14.5 %all-to-all-start = ((s32[32,1,108]{2,1,0:T(1,128)}), s32[32,1,108]{2,1,0:T(1,128)S(1)}, u32[]{:S(2)}, u32[]{:S(2)}) async-start(s32[32,1,108]{2,1,0:T(1,128)} %bitcast.4), calls=%async_computation | async-start | bytes 32768 | tf_op jit(solution)/shard_map/all_to_all | solution.py:109
  19.4 90.7 %copy-start = (bf16[128,4096]{1,0:T(8,128)(2,1)}, bf16[128,4096]{1,0:T(8,128)(2,1)S(1)}, u32[]{:S(2)}) copy-start(bf16[128,4096]{1,0:T(8,128)(2,1)S(1)} %convert_bitcast_fusion) | copy-start | bytes 3145732
  29.3 42.4 %all-to-all-start.1 = ((bf16[8,48,4096]{2,1,0:T(8,128)(2,1)}), bf16[8,48,4096]{2,1,0:T(8,128)(2,1)}, u32[]{:S(2)}, u32[]{:S(2)}) async-start(bf16[8,48,4096]{2,1,0:T(8,128)(2,1)} %bitcast.10), calls=%async_computation.1 | async-start | bytes 6291456 | tf_op jit(solution)/shard_map/all_to_all | solution.py:120
  33.8 157.5 %reduce-scatter.2.cloned.1.call-start = ((), (), s32[]{:S(2)}) async-start(), calls=%async_computation.5 | async-start | bytes 4587520 | tf_op jit(solution)/shard_map/reduce_scatter | solution.py:153
  34.8 18.9 %collective-permute-start.1 = (bf16[16,4096]{1,0:T(8,128)(2,1)S(1)}, bf16[16,4096]{1,0:T(8,128)(2,1)S(1)}, u32[]{:S(2)}, u32[]{:S(2)}) collective-permute-start(bf16[16,4096]{1,0:T(8,128)(2,1)S(1)} %slice_bitcast_fusion), channel_id=1, source_target_pairs={{0,16},{8,24},{16,0},{24,8},{1,17},{9,25},{17,1},{25,9},{2,18},{10... | collective-permute-start | bytes 393224 | tf_op jit(solution)/shard_map/ppermute | solution.py:15
  35.5 15.1 %collective-permute-start = (bf16[16,4096]{1,0:T(8,128)(2,1)S(1)}, bf16[16,4096]{1,0:T(8,128)(2,1)S(1)}, u32[]{:S(2)}, u32[]{:S(2)}) collective-permute-start(bf16[16,4096]{1,0:T(8,128)(2,1)S(1)} %slice_bitcast_fusion), channel_id=1, source_target_pairs={{0,8},{8,16},{16,24},{24,0},{1,9},{9,17},{17,25},{25,1},{2,10},{10... | collective-permute-start | bytes 393224 | tf_op jit(solution)/shard_map/ppermute | solution.py:15
  36.0 17.7 %collective-permute-start.2 = (bf16[16,4096]{1,0:T(8,128)(2,1)S(1)}, bf16[16,4096]{1,0:T(8,128)(2,1)S(1)}, u32[]{:S(2)}, u32[]{:S(2)}) collective-permute-start(bf16[16,4096]{1,0:T(8,128)(2,1)S(1)} %slice_bitcast_fusion), channel_id=1, source_target_pairs={{0,24},{8,0},{16,8},{24,16},{1,25},{9,1},{17,9},{25,17},{2,26},{10... | collective-permute-start | bytes 393224 | tf_op jit(solution)/shard_map/ppermute | solution.py:15
  53.8 62.6 %copy-start.4 = (bf16[64,4096]{1,0:T(8,128)(2,1)}, bf16[64,4096]{1,0:T(8,128)(2,1)S(1)}, u32[]{:S(2)}) copy-start(bf16[64,4096]{1,0:T(8,128)(2,1)S(1)} %constant_dynamic-update-slice_fusion) | copy-start | bytes 1572868
  110.2 6.2 %copy-start.7 = (bf16[448,512]{1,0:T(8,128)(2,1)}, bf16[448,512]{1,0:T(8,128)(2,1)S(1)}, u32[]{:S(2)}) copy-start(bf16[448,512]{1,0:T(8,128)(2,1)S(1)} %subtract_convert_fusion) | copy-start | bytes 1376260
  122.0 48.2 %all-to-all-start.3 = ((bf16[8,48,4096]{2,1,0:T(8,128)(2,1)}), bf16[8,48,4096]{2,1,0:T(8,128)(2,1)S(1)}, u32[]{:S(2)}, u32[]{:S(2)}) async-start(bf16[8,48,4096]{2,1,0:T(8,128)(2,1)} %bitcast.75), calls=%async_computation.4 | async-start | bytes 6291456 | tf_op jit(solution)/shard_map/all_to_all | solution.py:120
  131.2 7.9 %collective-permute-start.6 = (bf16[16,4096]{1,0:T(8,128)(2,1)}, bf16[16,4096]{1,0:T(8,128)(2,1)}, u32[]{:S(2)}, u32[]{:S(2)}) collective-permute-start(bf16[16,4096]{1,0:T(8,128)(2,1)} %get-tuple-element.16), channel_id=1, source_target_pairs={{16,8},{24,16},{17,9},{25,17},{18,10},{26,18},{19,11},{27,19},{20,... | collective-permute-start | bytes 393224 | tf_op jit(solution)/shard_map/ppermute | solution.py:43
  132.5 9.5 %collective-permute-start.4 = (bf16[16,4096]{1,0:T(8,128)(2,1)}, bf16[16,4096]{1,0:T(8,128)(2,1)}, u32[]{:S(2)}, u32[]{:S(2)}) collective-permute-start(bf16[16,4096]{1,0:T(8,128)(2,1)} %get-tuple-element.17), channel_id=1, source_target_pairs={{0,8},{8,16},{1,9},{9,17},{2,10},{10,18},{3,11},{11,19},{4,12},{12... | collective-permute-start | bytes 393224 | tf_op jit(solution)/shard_map/ppermute | solution.py:44
  135.8 20.1 %collective-permute-start.3 = (bf16[16,4096]{1,0:T(8,128)(2,1)S(1)}, bf16[16,4096]{1,0:T(8,128)(2,1)S(1)}, u32[]{:S(2)}, u32[]{:S(2)}) collective-permute-start(bf16[16,4096]{1,0:T(8,128)(2,1)S(1)} %get-tuple-element.15), channel_id=1, source_target_pairs={{0,24},{24,0},{1,25},{25,1},{2,26},{26,2},{3,27},{27,3},{4,28},{28... | collective-permute-start | bytes 393224 | tf_op jit(solution)/shard_map/ppermute | solution.py:46
  143.9 15.6 %collective-permute-start.5 = (bf16[16,4096]{1,0:T(8,128)(2,1)}, bf16[16,4096]{1,0:T(8,128)(2,1)}, u32[]{:S(2)}, u32[]{:S(2)}) collective-permute-start(bf16[16,4096]{1,0:T(8,128)(2,1)} %get-tuple-element.18), channel_id=1, source_target_pairs={{0,8},{8,16},{16,24},{1,9},{9,17},{17,25},{2,10},{10,18},{18,26},{... | collective-permute-start | bytes 393224 | tf_op jit(solution)/shard_map/ppermute | solution.py:58
  153.8 13.7 %collective-permute-start.7 = (bf16[16,4096]{1,0:T(8,128)(2,1)}, bf16[16,4096]{1,0:T(8,128)(2,1)}, u32[]{:S(2)}, u32[]{:S(2)}) collective-permute-start(bf16[16,4096]{1,0:T(8,128)(2,1)} %get-tuple-element.19), channel_id=1, source_target_pairs={{8,0},{16,8},{24,16},{9,1},{17,9},{25,17},{10,2},{18,10},{26,18},{... | collective-permute-start | bytes 393224 | tf_op jit(solution)/shard_map/ppermute | solution.py:57
  170.2 2.0 %copy-start.1 = (bf16[1,448,4096]{2,1,0:T(8,128)(2,1)S(1)}, bf16[1,448,4096]{2,1,0:T(8,128)(2,1)}, u32[]{:S(2)}) copy-start(bf16[1,448,4096]{2,1,0:T(8,128)(2,1)} %all-gather.3.cloned.1.call-done) | copy-start | bytes 11010052
  170.2 2.1 %copy-start.5 = (bf16[64,4096]{1,0:T(8,128)(2,1)S(1)}, bf16[64,4096]{1,0:T(8,128)(2,1)}, u32[]{:S(2)}) copy-start(bf16[64,4096]{1,0:T(8,128)(2,1)} %copy-done.4) | copy-start | bytes 1572868
  170.2 2.3 %copy-start.8 = (bf16[448,512]{1,0:T(8,128)(2,1)S(1)}, bf16[448,512]{1,0:T(8,128)(2,1)}, u32[]{:S(2)}) copy-start(bf16[448,512]{1,0:T(8,128)(2,1)} %copy-done.7) | copy-start | bytes 1376260
  172.5 18.9 %copy-start.2 = (f32[128,4096]{1,0:T(8,128)S(1)}, f32[128,4096]{1,0:T(8,128)}, u32[]{:S(2)}) copy-start(f32[128,4096]{1,0:T(8,128)} %pad.21) | copy-start | bytes 6291460
  192.7 1.3 copy-start.3
Sparse Core Ops, SparseCore 0:
  10.2 85.8 all-gather.2
  116.3 74.9 reduce-scatter.1
